TPU v7x, 32 devices: a whole 2x2x4 slice. The times are simulated.
32 devices in a mesh: dp: 8 (over y, x, core), ctx: 4 (over z).
Axes of the slice: x: 2, y: 2, z: 4, core: 2. Of those that a mesh axis runs over, the one named last changes fastest.
Arguments:
- tokens: bfloat16 [64, 512, 1024], P('dp', 'ctx'), may hold values from -6 to 6
- lengths: int32 [64], P('dp'), may hold values from 128 to 512, as said below
- w_qkv: bfloat16 [1024, 3072], P('dp'), may hold values from -0.1875 to 0.1875
- bias_qv: bfloat16 [2048], P('dp'), may hold values from -3 to 3
- w_out: bfloat16 [1024, 1024], P('dp'), may hold values from -1.5 to 1.5
- bias_out: bfloat16 [1024], P('dp'), may hold values from -3 to 3
- gain_one: bfloat16 [1024], P('dp'), may hold values from 0.5 to 1.5
- shift_one: bfloat16 [1024], P('dp'), may hold values from -3 to 3
- w_up: bfloat16 [1024, 4096], P('dp'), may hold values from -0.1875 to 0.1875
- bias_up: bfloat16 [4096], P('dp'), may hold values from -3 to 3
- w_down: bfloat16 [4096, 1024], P('dp'), may hold values from -0.09375 to 0.09375
- bias_down: bfloat16 [1024], P('dp'), may hold values from -3 to 3
- gain_two: bfloat16 [1024], P('dp'), may hold values from 0.5 to 1.5
- shift_two: bfloat16 [1024], P('dp'), may hold values from -3 to 3
- cotangent: bfloat16 [64, 512, 1024], P('dp', 'ctx'), may hold values from -6 to 6
Outputs:
- output: bfloat16 [64, 512, 1024], P('dp', 'ctx')
- grad_input: float32 [64, 512, 1024], P('dp', 'ctx')
- grad_w_qkv: float32 [1024, 3072], P('dp')
- grad_bias_qv: float32 [2048], P('dp')
- grad_w_out: float32 [1024, 1024], P('dp')
- grad_bias_out: float32 [1024], P('dp')
- grad_gain_one: float32 [1024], P('dp')
- grad_shift_one: float32 [1024], P('dp')
- grad_w_up: float32 [1024, 4096], P('dp')
- grad_bias_up: float32 [4096], P('dp')
- grad_w_down: float32 [4096, 1024], P('dp')
- grad_bias_down: float32 [1024], P('dp')
- grad_gain_two: float32 [1024], P('dp')
- grad_shift_two: float32 [1024], P('dp')
Inputs may be any that keep to these rules, and one draw needn't show every extreme that they name: `lengths`: in each group of 8 slots that one index of dp holds, one slot has length 512 and another length 128.
All inputs are finite; a program needn't handle non-finite values.
Results may differ from a plain program's by a relative error of at most 0.017.
Values may be sent and summed in bfloat16 or wider, within the bound.
No kernel may reach another device: no remote copies, remote signals or barrier semaphores. Data moves between devices by JAX's collectives and lax.ppermute only.
A program may use at most 256 MiB of HBM per device.

v0:
```python
import functools

import jax
import jax.numpy as jnp
from jax import lax
from jax.experimental import pallas as pl
from jax.experimental.pallas import tpu as pltpu
from jax.sharding import PartitionSpec as P

HD = 64
GROUP = 4
NEG = -1e30
EPS = 1e-06
BF = jnp.bfloat16
F32 = jnp.float32
MIB = 1024 * 1024
COSTS = {'qkv': 13, 'out': 10, 'up': 23, 'down': 21, 'hidden': 18, 'first': 23, 'input': 14, 'attend': 24, 'attend_back': 21, 'gd_away': 11, 'gd_keep': 11, 'gu_away': 11, 'gu_keep': 11, 'gb_away': 14, 'gb_keep': 3, 'gc_away': 8, 'gc_keep': 8}


def cost(name):
    return pl.CostEstimate(flops=COSTS[name] * 1000000000, bytes_accessed=1000000, transcendentals=0)


ANY = pl.BlockSpec(memory_space=pl.ANY)


def swap(x, axis, bit):
    n = lax.axis_size(axis)
    return lax.ppermute(x, axis, [(i, i ^ bit) for i in range(n)])


def after(x, *others):
    return lax.optimization_barrier((x,) + others)[0]


def sync(*values):
    return lax.optimization_barrier(values)


def gather_near(own):
    if lax.axis_size("dp") != 8:
        return ()
    return swap(own, "dp", 2), swap(own, "dp", 4)


def gather_far(near):
    if not near:
        return ()
    half = near[0].shape[1] // 2
    return swap(near[0][:, :half], "dp", 4), swap(near[1][:, half:], "dp", 2)


def gather_stack(own, near, far):
    if near:
        return jnp.stack([own, near[0], near[1], jnp.concatenate(far, axis=1)])
    mine = own[None]
    bit = 2
    while bit < lax.axis_size("dp"):
        mine = jnp.concatenate([mine, swap(mine, "dp", bit)])
        bit *= 2
    return mine


def add_low(*parts):
    total = parts[0].astype(F32)
    for part in parts[1:]:
        total = total + part.astype(F32)
    return total.astype(BF)


def reduce_any(grad):
    n = lax.axis_size("dp")
    me = lax.axis_index("dp")
    rows = grad.shape[0] // n
    width = grad.shape[1]

    def stack(odd):
        return jnp.stack(
            [lax.dynamic_slice(grad, ((me ^ (2 * k + odd)) * rows, 0), (rows, width)) for k in range(n // 2)]
        )

    mine = add_low(stack(0), swap(stack(1), "dp", 1))
    bit = n // 2
    while bit > 1:
        keep = mine.shape[0] // 2
        mine = add_low(mine[:keep], swap(mine[keep:], "dp", bit))
        bit //= 2
    return mine[0]


def send_far(sums):
    return swap(sums[3], "dp", 4), swap(sums[4], "dp", 2)


def send_near(sums, far):
    own, to_x, to_y = sums[:3]
    cut, width = far[0].shape[1], to_x.shape[1]
    to_x = add_low(to_x, jnp.pad(far[0], ((0, 0), (0, width - cut))))
    to_y = add_low(to_y, jnp.pad(far[1], ((0, 0), (cut, 0))))
    return swap(to_x, "dp", 2), swap(to_y, "dp", 4)


def halves_ctx(share, bit):
    half = share.shape[1] // 2
    mine = (lax.axis_index("ctx") // bit) % 2
    keep = lax.dynamic_slice_in_dim(share, mine * half, half, axis=1)
    return keep, lax.dynamic_slice_in_dim(share, (1 - mine) * half, half, axis=1)


def halve_ctx(share, bit):
    keep, away = halves_ctx(share, bit)
    return add_low(keep, swap(away, "ctx", bit))


def join_ctx(half, other, bit):
    low = (lax.axis_index("ctx") // bit) % 2 == 0
    return jnp.concatenate([jnp.where(low, half, other), jnp.where(low, other, half)], axis=1)


def whole_ctx(half, bit):
    return join_ctx(half, swap(half, "ctx", bit), bit)


def to_sequences(block):
    return lax.all_to_all(block, "ctx", 0, 0, tiled=True)


def part_of(block, j, axis=0):
    n = lax.axis_size("ctx")
    per = block.shape[axis] // n
    return lax.dynamic_slice_in_dim(block, (lax.axis_index("ctx") ^ j) * per, per, axis=axis)


def put_slots(pieces, per, dtype):
    n = lax.axis_size("ctx")
    out = jnp.zeros((n * per,) + pieces[0][2].shape[1:], dtype)
    for j, first, piece in pieces:
        start = (lax.axis_index("ctx") ^ j) * per + first
        out = lax.dynamic_update_slice_in_dim(out, piece.astype(dtype), start, axis=0)
    return out


def put_positions(pieces):
    n = len(pieces)
    per, blk, width = pieces[0].shape
    out = jnp.zeros((per, n * blk, width), pieces[0].dtype)
    for j in range(n):
        out = lax.dynamic_update_slice_in_dim(out, pieces[j], (lax.axis_index("ctx") ^ j) * blk, axis=1)
    return out


def trade(block, j):
    return swap(block, "ctx", j)


def nn(left, right):
    return jnp.dot(left, right, preferred_element_type=F32)


def nt(left, right):
    return lax.dot_general(left, right, (((1,), (1,)), ((), ())), preferred_element_type=F32)


def tn(left, right):
    return lax.dot_general(left, right, (((0,), (0,)), ((), ())), preferred_element_type=F32)


def fold(rows):
    return jnp.sum(rows.reshape(rows.shape[0] // 8, 8, rows.shape[1]), axis=0)


class Weight:
    def __init__(self, stacks, whole, sems, me, rows, first, pieces):
        self.whole, self.pieces = whole, pieces
        self.step = whole.shape[1] // max(pieces, 1)
        self.copies, self.starts = [], []
        for odd, stack in enumerate(stacks):
            count = stack.shape[0]
            for k in range(count):
                start = pl.multiple_of((me ^ (2 * k + odd)) * rows if len(stacks) == 2 else k * rows, rows)
                self.starts.append(pl.ds(start, rows))
                for p in range(max(pieces, 1)):
                    here, there = pl.ds(first + p * self.step, self.step), pl.ds(p * self.step, self.step)
                    copy = pltpu.make_async_copy(
                        stack.at[k, pl.ds(0, rows), here], whole.at[self.starts[-1], there], sems.at[odd * count + k, p]
                    )
                    self.copies.append((k * 2 + odd, p, copy))
        self.wait_for = False

    def start(self):
        for _, _, copy in sorted(self.copies, key=lambda c: c[1] if self.pieces else c[0]):
            copy.start()

    def cols(self, p):
        if self.wait_for:
            for _, q, copy in self.copies:
                if q == p:
                    copy.wait()
        return slice(p * self.step, (p + 1) * self.step)

    def rows(self, c):
        _, _, copy = self.copies[c]
        if self.wait_for:
            copy.wait()
        return self.starts[c]


def row_spec(tile, width):
    return pl.BlockSpec((tile, width), lambda i, *_: (i, 0))


def one_spec(height, width):
    return pl.BlockSpec((height, width), lambda i, *_: (0, 0))


def dense(body, name, meta, rows, tile, row_ins, vec_ins, weights, row_outs, sums):
    stacks, spans, scratch = [], [], []
    for mine, other, r, _, width, pieces in weights:
        held = [mine] if other is None else [mine, other]
        spans.append(slice(len(stacks), len(stacks) + len(held)))
        stacks += held
        count = mine.shape[0] * len(held)
        scratch.append(pltpu.VMEM((count * r, width), BF))
        scratch.append(pltpu.SemaphoreType.DMA((count, max(pieces, 1))))
    n_row, n_vec, n_stack = len(row_ins), len(vec_ins), len(stacks)
    n_out, n_sum = len(row_outs), len(sums)

    def kernel(meta_ref, *refs):
        pos = 0
        groups = []
        for count in (n_row, n_vec, n_stack, n_out, n_sum, 2 * len(weights)):
            groups.append(refs[pos : pos + count])
            pos += count
        row_refs, vec_refs, stack_refs, out_refs, sum_refs, scratch_refs = groups

        whole = [
            Weight(stack_refs[spans[w]], scratch_refs[2 * w], scratch_refs[2 * w + 1], meta_ref[0], weights[w][2], weights[w][3], weights[w][5])
            for w in range(len(weights))
        ]

        def work(wait_for):
            for weight in whole:
                weight.wait_for = wait_for
            body(meta_ref, row_refs, vec_refs, whole, out_refs, sum_refs)

        @pl.when(pl.program_id(0) == 0)
        def _():
            for weight in whole:
                weight.start()
            for ref in sum_refs:
                ref[...] = jnp.zeros_like(ref)
            work(True)

        @pl.when(pl.program_id(0) > 0)
        def _():
            work(False)

    in_specs = (
        [row_spec(tile, a.shape[-1]) if a.ndim == 2 else pl.BlockSpec((a.shape[0], tile, a.shape[2]), lambda i, *_: (0, i, 0)) for a in row_ins]
        + [one_spec(1, v.shape[1]) for v in vec_ins]
        + [ANY] * n_stack
    )
    out_specs = [row_spec(tile, w) for w, _ in row_outs] + [one_spec(8, w) for w in sums]
    out_shape = [jax.ShapeDtypeStruct((rows, w), d) for w, d in row_outs] + [
        jax.ShapeDtypeStruct((8, w), F32) for w in sums
    ]
    return pl.pallas_call(
        kernel,
        grid_spec=pltpu.PrefetchScalarGridSpec(
            num_scalar_prefetch=1,
            grid=(rows // tile,),
            in_specs=in_specs,
            out_specs=out_specs,
            scratch_shapes=scratch,
        ),
        out_shape=out_shape,
        compiler_params=pltpu.CompilerParams(vmem_limit_bytes=60 * MIB, dimension_semantics=("arbitrary",)),
        cost_estimate=cost(name),
        name=name,
    )(meta, *row_ins, *vec_ins, *stacks)


def by_columns(left, weight):
    parts = []
    for p in range(weight.pieces):
        cols = weight.cols(p)
        parts.append(nn(left[...], weight.whole[:, cols]))
    return jnp.concatenate(parts, axis=1)


def by_columns_turned(left, weight):
    total = None
    for p in range(weight.pieces):
        cols = weight.cols(p)
        part = nt(left[:, cols], weight.whole[:, cols])
        total = part if total is None else total + part
    return total


def by_shards(left, weight):
    if weight.pieces:
        return by_columns(left, weight)
    if not weight.wait_for:
        return nn(left[...], weight.whole[...])
    total = None
    for c in range(len(weight.copies)):
        here = weight.rows(c)
        part = nn(left[:, here], weight.whole[here, :])
        total = part if total is None else total + part
    return total


def qkv_body(meta, rows, vecs, whole, outs, sums):
    (x,) = rows
    (bias,) = vecs
    for p in range(whole[0].pieces):
        cols = whole[0].cols(p)
        outs[0][:, cols] = (nn(x[...], whole[0].whole[:, cols]) + bias[:, cols]).astype(BF)


def out_body(meta, rows, vecs, whole, outs, sums):
    mixed, x = rows
    bias, gain, shift = vecs
    total = x[...].astype(F32) + (by_columns(mixed, whole[0]) + bias[...])
    centre = total - jnp.mean(total, axis=-1, keepdims=True)
    inverse = lax.rsqrt(jnp.mean(centre * centre, axis=-1, keepdims=True) + EPS)
    normed = centre * inverse
    outs[0][...] = normed
    outs[1][...] = jnp.broadcast_to(inverse, outs[1].shape)
    outs[2][...] = (normed * gain[...] + shift[...]).astype(BF)


def up_body(meta, rows, vecs, whole, outs, sums):
    (low,) = rows
    (bias,) = vecs
    for p in range(whole[0].pieces):
        cols = whole[0].cols(p)
        hidden = nn(low[...], whole[0].whole[:, cols]) + bias[:, cols]
        cdf = 0.5 + 0.5 * lax.erf(hidden * 0.7071067811865476)
        pdf = jnp.exp(-0.5 * hidden * hidden) * 0.3989422804014327
        outs[0][:, cols] = (hidden * cdf).astype(BF)
        outs[1][:, cols] = (cdf + hidden * pdf).astype(BF)


def down_body(seq, per, meta, rows, vecs, whole, outs, sums):
    active, normed_one, cot = rows
    bias, gain_one, shift_one, gain, shift = vecs
    total = (normed_one[...] * gain_one[...] + shift_one[...]) + (by_shards(active, whole[0]) + bias[...])
    centre = total - jnp.mean(total, axis=-1, keepdims=True)
    inverse = lax.rsqrt(jnp.mean(centre * centre, axis=-1, keepdims=True) + EPS)
    normed = centre * inverse
    tile = total.shape[0]
    at = lax.broadcasted_iota(jnp.int32, (tile, 1), 0) + pl.program_id(0) * tile
    valid = jnp.zeros(at.shape, jnp.bool_)
    for s in range(per):
        valid = valid | ((at >= s * seq) & (at < s * seq + meta[2 + s]))
    keep = jnp.where(valid, 1.0, 0.0)
    outs[0][...] = ((normed * gain[...] + shift[...]) * keep).astype(BF)
    grad = cot[...].astype(F32) * keep
    sums[0][...] += fold(grad * normed)
    sums[1][...] += fold(grad)
    scaled = grad * gain[...]
    back = inverse * (
        scaled
        - jnp.mean(scaled, axis=-1, keepdims=True)
        - normed * jnp.mean(scaled * normed, axis=-1, keepdims=True)
    )
    low = back.astype(BF)
    outs[1][...] = back
    outs[2][...] = low
    sums[2][...] += fold(low.astype(F32))


def hidden_body(meta, rows, vecs, whole, outs, sums):
    second, deriv = rows
    if whole[0].pieces:
        whole[0].cols(0)
        places = [slice(c, c + 512) for c in range(0, deriv.shape[1], 512)]
    else:
        places = range(len(whole[0].copies))
    for cols in places:
        if not whole[0].pieces:
            cols = whole[0].rows(cols)
        low = (nt(second[...], whole[0].whole[cols, :]) * deriv[:, cols].astype(F32)).astype(BF)
        outs[0][:, cols] = low
        sums[0][:, cols] += fold(low.astype(F32))


def first_body(meta, rows, vecs, whole, outs, sums):
    hidden, sum_two, normed, inverse = rows
    (gain,) = vecs
    grad = sum_two[...] + by_columns_turned(hidden, whole[0])
    n1 = normed[...]
    sums[0][...] += fold(grad * n1)
    sums[1][...] += fold(grad)
    scaled = grad * gain[...]
    back = inverse[:, 0:1] * (
        scaled - jnp.mean(scaled, axis=-1, keepdims=True) - n1 * jnp.mean(scaled * n1, axis=-1, keepdims=True)
    )
    low = back.astype(BF)
    outs[0][...] = back
    outs[1][...] = low
    sums[2][...] += fold(low.astype(F32))
    whole[1].cols(0)
    outs[2][...] = nt(low, whole[1].whole[...]).astype(BF)


def input_body(meta, rows, vecs, whole, outs, sums):
    sum_one = rows[-1]
    total = sum_one[...]
    parts = len(rows) - 1
    for p in range(whole[0].pieces):
        cols = whole[0].cols(p)
        total = total + nt(rows[p % parts][p // parts], whole[0].whole[:, cols])
    outs[0][...] = total.astype(BF)


def key_mask(meta, seq):
    at = lax.broadcasted_iota(jnp.int32, (seq, 1), 0)
    return at < meta[2 + pl.program_id(0)]


def attend_kernel(meta, q_ref, k_ref, v_ref, mixed_ref, lse_ref):
    seq, lanes = q_ref.shape
    ok = key_mask(meta, seq)
    q_all = q_ref[...] * BF(HD ** (-0.5))
    k_all, v_turned = k_ref[...], v_ref[...].T
    ones = jnp.ones((16, seq), BF)
    outs = []
    for h in range(lanes // HD):
        cols = slice(h * HD, (h + 1) * HD)
        scores = jnp.where(ok, nt(k_all[:, cols], q_all[:, cols]), NEG)
        peak = jnp.max(scores, axis=0, keepdims=True)
        weights = jnp.exp(scores - peak).astype(BF)
        both = nn(jnp.concatenate([v_turned[cols], ones], axis=0), weights)
        total = both[HD : HD + 1]
        lse_ref[h : h + 1, :] = peak + jnp.log(total)
        outs.append(both[:HD] * (1.0 / total))
    mixed_ref[...] = jnp.concatenate(outs, axis=0).T.astype(BF)


def attend_back_kernel(meta, q_ref, k_ref, v_ref, g_ref, mixed_ref, lse_ref, proj_ref, sum_ref):
    seq, lanes = q_ref.shape
    ok = key_mask(meta, seq)
    scale = HD ** (-0.5)
    q_all = q_ref[...] * BF(scale)
    k_all, v_all, g_all = k_ref[...], v_ref[...], g_ref[...]
    k_turned = k_all.T
    inners = (g_all.astype(F32) * mixed_ref[...].astype(F32)).T
    gq, gk, gv = [], [], []
    for h in range(lanes // HD):
        cols = slice(h * HD, (h + 1) * HD)
        q, k, v, g = q_all[:, cols], k_all[:, cols], v_all[:, cols], g_all[:, cols]
        exact = jnp.exp(jnp.where(ok, nt(k, q), NEG) - lse_ref[h : h + 1, :])
        inner = jnp.sum(inners[cols], axis=0, keepdims=True)
        low = (exact * (nt(v, g) - inner)).astype(BF)
        gq.append(nn(k_turned[cols], low) * scale)
        gk.append(nn(low, q))
        gv.append(nn(exact.astype(BF), g))
    wholes = (jnp.concatenate(gq, axis=0).T, jnp.concatenate(gk, axis=1), jnp.concatenate(gv, axis=1))
    for c, whole in enumerate(wholes):
        low = whole.astype(BF)
        proj_ref[c] = low
        sum_ref[c] = fold(low.astype(F32))


def attend(meta, proj, per, seq):
    lanes = GROUP * HD
    groups = proj.shape[-1] // 3 // lanes
    shaped = proj.reshape(per, seq, proj.shape[-1])

    def spec(c):
        return pl.BlockSpec((None, seq, lanes), lambda s, h, *_: (s, 0, c * groups + h))

    mixed, lse = pl.pallas_call(
        attend_kernel,
        grid_spec=pltpu.PrefetchScalarGridSpec(
            num_scalar_prefetch=1,
            grid=(per, groups),
            in_specs=[spec(0), spec(1), spec(2)],
            out_specs=[spec(0), pl.BlockSpec((None, None, GROUP, seq), lambda s, h, *_: (s, h, 0, 0))],
        ),
        out_shape=[
            jax.ShapeDtypeStruct((per, seq, groups * lanes), BF),
            jax.ShapeDtypeStruct((per, groups, GROUP, seq), F32),
        ],
        compiler_params=pltpu.CompilerParams(vmem_limit_bytes=60 * MIB),
        cost_estimate=cost("attend"),
        name="attend",
    )(meta, shaped, shaped, shaped)
    return mixed.reshape(per * seq, -1), lse


def attend_back(meta, proj, grad, mixed, lse, per, seq, first, count):
    width = proj.shape[-1] // 3
    lanes = GROUP * HD
    groups = width // lanes
    shaped = proj.reshape(per, seq, proj.shape[-1])

    def spec(c):
        return pl.BlockSpec((None, seq, lanes), lambda s, h, *_: (s, 0, c * groups + first + h))

    out, sums = pl.pallas_call(
        attend_back_kernel,
        grid_spec=pltpu.PrefetchScalarGridSpec(
            num_scalar_prefetch=1,
            grid=(per, count),
            in_specs=[spec(0), spec(1), spec(2), spec(0), spec(0)]
            + [pl.BlockSpec((None, None, GROUP, seq), lambda s, h, *_: (s, first + h, 0, 0))],
            out_specs=[
                pl.BlockSpec((3, None, seq, lanes), lambda s, h, *_: (0, s, 0, h)),
                pl.BlockSpec((3, None, 8, lanes), lambda s, h, *_: (0, s, 0, h)),
            ],
        ),
        out_shape=[
            jax.ShapeDtypeStruct((3, per, seq, count * lanes), BF),
            jax.ShapeDtypeStruct((3, per, 8, count * lanes), F32),
        ],
        compiler_params=pltpu.CompilerParams(vmem_limit_bytes=60 * MIB),
        cost_estimate=cost("attend_back"),
        name="attend_back",
    )(meta, shaped, shaped, shaped, grad.reshape(per, seq, width), mixed.reshape(per, seq, width), lse)
    return out.reshape(3, per * seq, count * lanes), sums


def weight_grad(name, meta, odd, lefts, rights, chunk, come=None, extra=None):
    rows = lefts[0].shape[0]
    tall = lefts[0].shape[1] // 8
    plan = []
    for li, group in enumerate(rights):
        for right in group:
            for c in range((right.shape[0] if right.ndim == 3 else 1) * (right.shape[-1] // chunk)):
                plan.append((li, right, c))
    steps = len(plan)
    flat = [r for group in rights for r in group]
    firsts, pos = [], 0
    for right in flat:
        firsts.append(pos)
        pos += (right.shape[0] if right.ndim == 3 else 1) * (right.shape[-1] // chunk)
    owners = [li for li, group in enumerate(rights) for _ in group]
    below = 0 if extra is None else extra.shape[1]
    cut = (steps + 1) // 2
    n_left = len(lefts)

    def kernel(meta_ref, *refs):
        left_refs = refs[: 4 * n_left]
        pos = 4 * n_left
        right_refs = refs[pos : pos + len(flat)]
        pos += len(flat)
        extra_refs = refs[pos : pos + 4] if below else ()
        pos += len(extra_refs)
        come_ref = refs[pos] if come is not None else None
        pos += come is not None
        outs = refs[pos:]
        c = pl.program_id(0)

        def store(lefts_here, right):
            for k in range(4):
                part = tn(lefts_here[k][...], right)
                if come is None:
                    outs[0][k, 0:tall, :] = part.astype(BF)
                    if below:
                        outs[0][k, tall:, :] = extra_refs[k][...]
                    continue
                part = (part + come_ref[k, 0:tall, :].astype(F32)).astype(BF)
                if below:
                    low = (extra_refs[k][...].astype(F32) + come_ref[k, tall:, :].astype(F32)).astype(BF)
                if k < 3:
                    outs[k][0:tall, :] = part
                    if below:
                        outs[k][tall:, :] = low
                    continue

                @pl.when(c < cut)
                def _():
                    outs[3][0:tall, :] = part
                    if below:
                        outs[3][tall:, :] = low

                @pl.when(c >= cut)
                def _():
                    outs[4][0:tall, :] = part
                    if below:
                        outs[4][tall:, :] = low

        for i, right_ref in enumerate(right_refs):
            last = firsts[i + 1] if i + 1 < len(flat) else steps
            li = owners[i]

            @pl.when((c >= firsts[i]) & (c < last))
            def _(right_ref=right_ref, li=li):
                store(left_refs[4 * li : 4 * li + 4], right_ref[...])

    def left_spec(k):
        return pl.BlockSpec((rows, tall), lambda c, m: (0, m[0] ^ (2 * k + odd)))

    def right_spec(i, right):
        last = (firsts[i + 1] if i + 1 < len(flat) else steps) - 1
        inner = right.shape[-1] // chunk

        def place(c):
            return jnp.clip(c, firsts[i], last) - firsts[i]

        if right.ndim == 3:
            return pl.BlockSpec((None, rows, chunk), lambda c, m: (place(c) // inner, 0, place(c) % inner))
        return pl.BlockSpec((rows, chunk), lambda c, m: (0, place(c)))

    def extra_spec(k):
        return pl.BlockSpec((None, below, chunk), lambda c, m: (m[0] ^ (2 * k + odd), 0, c))

    high = tall + below
    four = pl.BlockSpec((4, high, chunk), lambda c, m: (0, 0, c))
    in_specs = [left_spec(k) for _ in lefts for k in range(4)] + [right_spec(i, r) for i, r in enumerate(flat)]
    args = [left for left in lefts for _ in range(4)] + flat
    if below:
        in_specs += [extra_spec(k) for k in range(4)]
        args += [extra] * 4
    if come is None:
        out_specs = [four]
        out_shape = [jax.ShapeDtypeStruct((4, high, steps * chunk), BF)]
    else:
        in_specs.append(four)
        args.append(come)
        out_specs = [pl.BlockSpec((high, chunk), lambda c, m: (0, c))] * 3 + [
            pl.BlockSpec((high, chunk), lambda c, m: (0, jnp.minimum(c, cut - 1))),
            pl.BlockSpec((high, chunk), lambda c, m: (0, jnp.maximum(c - cut, 0))),
        ]
        out_shape = [jax.ShapeDtypeStruct((high, steps * chunk), BF)] * 3 + [
            jax.ShapeDtypeStruct((high, cut * chunk), BF),
            jax.ShapeDtypeStruct((high, (steps - cut) * chunk), BF),
        ]
    return pl.pallas_call(
        kernel,
        grid_spec=pltpu.PrefetchScalarGridSpec(
            num_scalar_prefetch=1,
            grid=(steps,),
            in_specs=in_specs,
            out_specs=out_specs,
        ),
        out_shape=out_shape,
        compiler_params=pltpu.CompilerParams(vmem_limit_bytes=60 * MIB),
        cost_estimate=cost(name),
        name=name,
    )(meta, *args)


def shards(
    tokens, lengths, w_qkv, bias_qv, w_out, bias_out, gain_one, shift_one,
    w_up, bias_up, w_down, bias_down, gain_two, shift_two, cotangent,
):
    seqs, blk, width = tokens.shape
    n = lax.axis_size("ctx")
    ndp = lax.axis_size("dp")
    me = lax.axis_index("dp")
    place = lax.axis_index("ctx")
    per = seqs // n
    rows = seqs * blk
    tile = per * blk
    ff = w_up.shape[1]
    thin = w_qkv.shape[0]
    tuned = ndp == 8
    half = width // (GROUP * HD) // 2

    own = lax.dynamic_slice_in_dim(lengths, place * per, per)
    meta = jnp.concatenate([jnp.stack([me, place]).astype(jnp.int32), own])

    vectors = (bias_qv, bias_out, gain_one, shift_one, bias_up, bias_down, gain_two, shift_two)
    sizes = [v.shape[0] for v in vectors]
    count = sum(sizes)
    line = jnp.pad(jnp.concatenate(vectors).reshape(1, count), ((0, 15), (0, 3 * width - count)))
    qkv_own = jnp.concatenate([w_qkv, line])
    mid_own = jnp.concatenate([w_out, w_up], axis=1)
    shared = tokens.reshape(n, per, blk, width)
    x = jnp.swapaxes(to_sequences(shared), 0, 1).reshape(rows, width)
    qkv_near = gather_near(qkv_own)
    mid_near = gather_near(mid_own)
    x, qkv_near, mid_near, cotangent = sync(x, qkv_near, mid_near, cotangent)
    qkv_far = gather_far(qkv_near)
    qkv_mine = gather_stack(qkv_own, qkv_near, qkv_far)
    qkv_other = swap(qkv_mine, "dp", 1)
    mid_far = gather_far(mid_near)
    cot_1 = trade(part_of(cotangent, 1), 1)

    both = jnp.concatenate([qkv_mine[:, thin, :count], qkv_other[:, thin, :count]])
    index = jnp.arange(ndp, dtype=jnp.int32) ^ me
    packed = jnp.take(both, (index >> 1) + (index & 1) * (ndp // 2), axis=0).astype(F32)
    fulls, pos = [], 0
    for size in sizes:
        fulls.append(packed[:, pos : pos + size].reshape(1, ndp * size))
        pos += size
    bqv, bout, gone, sone, bup, bdown, gtwo, stwo = fulls
    bqkv = jnp.concatenate([bqv[:, :width], jnp.zeros((1, width), F32), bqv[:, width:]], axis=1)

    qkv_w = (qkv_mine, qkv_other, thin, 0, 3 * width, 3)
    (proj,) = dense(qkv_body, "qkv", meta, rows, tile, [x], [bqkv], [qkv_w], [(3 * width, BF)], [])
    proj, mid_far, cot_1, w_down, cotangent = sync(proj, mid_far, cot_1, w_down, cotangent)
    mid_mine = gather_stack(mid_own, mid_near, mid_far)
    mid_other = swap(mid_mine, "dp", 1)
    down_all = lax.all_gather(w_down, "dp", axis=0, tiled=True)
    cot_2 = trade(part_of(cotangent, 2), 2)
    mixed, lse = attend(meta, proj, per, n * blk)
    mixed, mid_other, cot_2 = sync(mixed, mid_other, cot_2)
    out_w = (mid_mine, mid_other, thin, 0, width, 2)
    up_w = (mid_mine, mid_other, thin, width, ff, 8)
    normed_one, inverse_one, first_low = dense(
        out_body, "out", meta, rows, tile, [mixed, x], [bout, gone, sone], [out_w], [(width, F32), (128, F32), (width, BF)], []
    )
    first_low, cotangent = sync(first_low, cotangent)
    cot_3 = trade(part_of(cotangent, 3), 3)
    active, deriv = dense(up_body, "up", meta, rows, tile, [first_low], [bup], [up_w], [(ff, BF), (ff, BF)], [])
    active, down_all, cot_3 = sync(active, down_all, cot_3)
    down_w = (down_all.reshape(8, ff // 8, width), None, ff // 8, 0, width, 0)
    cot = put_positions([part_of(cotangent, 0), cot_1, cot_2, cot_3]).reshape(rows, width)
    out_parts, sum_two, second, s_gtwo, s_stwo, s_bdown = dense(
        functools.partial(down_body, n * blk, per), "down", meta, rows, tile, [active, normed_one, cot],
        [bdown, gone, sone, gtwo, stwo], [down_w], [(width, BF), (width, F32), (width, BF)], [width] * 3,
    )
    out_parts = out_parts.reshape(per, n * blk, width)
    out_own = part_of(out_parts, 0, 1)
    out_1 = trade(part_of(out_parts, 1, 1), 1)
    cut = (per + 1) // 2

    come = ()
    if tuned:
        (away,) = weight_grad("gd_away", meta, 1, [active], [[second]], 512)
        come = swap(away, "dp", 1)
        second = after(second, away)
    hidden, s_bup = dense(hidden_body, "hidden", meta, rows, tile, [second, deriv], [], [down_w], [(ff, BF)], [ff])
    hidden, come, out_1, out_parts = sync(hidden, come, out_1, out_parts)
    part = part_of(out_parts, 2, 1)
    out_2 = trade(part[:cut], 2)
    d_far, d_near = (), ()
    if tuned:
        d_sums = weight_grad("gd_keep", meta, 0, [active], [[second]], 512, come=come)
        d_far = send_far(d_sums)
        hidden, out_2, part = sync(after(hidden, d_sums[0]), out_2, part)
    out_2b = trade(part[cut:], 2)
    if tuned:
        (away,) = weight_grad("gu_away", meta, 1, [first_low], [[hidden]], 1024)
        hidden = after(hidden, away)
        away, d_far, out_2b = sync(away, d_far, out_2b)
        come = swap(away, "dp", 1)
    hidden, d_far, out_2b, out_parts = sync(hidden, d_far, out_2b, out_parts)
    if tuned:
        d_near = send_near(d_sums, d_far)
    out_3 = trade(part_of(out_parts, 3, 1), 3)
    sum_one, branch, g_mixed, s_gone, s_sone, s_bout = dense(
        first_body, "first", meta, rows, tile, [hidden, sum_two, normed_one, inverse_one], [gone], [up_w[:5] + (4,), out_w[:5] + (1,)],
        [(width, F32), (width, BF), (width, BF)], [width] * 3,
    )
    branch, g_mixed, come, d_near, out_3 = sync(branch, g_mixed, come, d_near, out_3)
    output = put_slots([(0, 0, out_own), (1, 0, out_1), (2, 0, out_2), (2, cut, out_2b), (3, 0, out_3)], per, BF)
    u_far = ()
    if tuned:
        d_share = add_low(d_sums[0], *d_near)
        g_down = lax.psum(d_share, "ctx")
        u_sums = weight_grad("gu_keep", meta, 0, [first_low], [[hidden]], 1024, come=come)
        u_far = send_far(u_sums)
        g_mixed = after(g_mixed, u_sums[0])
    p_one, s_one = attend_back(meta, proj, g_mixed, mixed, lse, per, n * blk, 0, half)
    p_one, g_mixed, u_far = sync(p_one, g_mixed, u_far)
    u_near = ()
    if tuned:
        u_near = send_near(u_sums, u_far)
    p_two, s_two = attend_back(meta, proj, g_mixed, mixed, lse, per, n * blk, half, half)
    if tuned:
        p_two, u_near, g_down = sync(p_two, u_near, g_down)

    s_proj = jnp.concatenate([jnp.sum(s_one, axis=(1, 2)), jnp.sum(s_two, axis=(1, 2))], axis=1)
    vec = [jnp.concatenate([s_proj[0], s_proj[2]])] + [
        jnp.sum(s, axis=0) for s in (s_bout, s_gone, s_sone, s_bup, s_bdown, s_gtwo, s_stwo)
    ]
    vec = jnp.concatenate([v.reshape(ndp, -1) for v in vec], axis=1)

    come = ()
    if tuned:
        u_keep, u_away = halves_ctx(add_low(u_sums[0], *u_near), 1)
        u_come = swap(u_away, "ctx", 1)
        extra = jnp.pad(vec[:, None, :].astype(BF), ((0, 0), (0, 15), (0, 4 * width - count)))
        products = ([x, mixed], [[p_one, p_two], [branch]])
        (away,) = weight_grad("gb_away", meta, 1, *products, 512, extra=extra)
        sum_one = after(sum_one, away)
        away, u_come = sync(away, u_come)
        come = swap(away, "dp", 1)
        u_keep, u_away = halves_ctx(add_low(u_keep, u_come), 2)
        u_come = swap(u_away, "ctx", 2)
    else:
        u_come = ()
    (grad_in,) = dense(input_body, "input", meta, rows, tile, [p_one, p_two, sum_one], [], [qkv_w[:5] + (6,)], [(width, BF)], [])
    grad_in, come, u_come = sync(grad_in, come, u_come)
    grad_in = grad_in.reshape(per, n * blk, width)
    in_1 = trade(part_of(grad_in, 1, 1), 1)
    if tuned:
        u_half = add_low(u_keep, u_come)
        u_other = swap(u_half, "ctx", 2)
        b_sums = weight_grad("gb_keep", meta, 0, *products, 512, come=come, extra=extra)
        b_sums, u_other, in_1, grad_in = sync(b_sums, u_other, in_1, grad_in)
    part_2, part_3 = part_of(grad_in, 2, 1), part_of(grad_in, 3, 1)
    in_2 = trade(part_2[:cut], 2)
    if tuned:
        b_far = send_far(b_sums)
        u_whole = join_ctx(u_half, u_other, 2)
        u_other = swap(u_whole, "ctx", 1)
        b_far, in_2, u_other, part_2, part_3 = sync(b_far, in_2, u_other, part_2, part_3)
        b_near = send_near(b_sums, b_far)
    in_2b, in_3 = trade(part_2[cut:], 2), trade(part_3[:cut], 3)
    if tuned:
        b_near, in_2b, in_3, part_3 = sync(b_near, in_2b, in_3, part_3)
        b_keep, b_away = halves_ctx(add_low(b_sums[0], *b_near), 1)
        b_come = swap(b_away, "ctx", 1)
    in_3b = trade(part_3[cut:], 3)
    in_rest = [(2, 0, in_2), (2, cut, in_2b), (3, 0, in_3), (3, cut, in_3b)]
    if tuned:
        b_come, in_3b = sync(b_come, in_3b)
        b_half = add_low(b_keep, b_come)
        g_up = join_ctx(u_whole, u_other, 1)
        total = whole_ctx(whole_ctx(halve_ctx(b_half, 2), 2), 1).astype(F32)
        part = width // 2
        g_qkv = jnp.concatenate(
            [total[:thin, (p * 3 + c) * part : (p * 3 + c + 1) * part] for c in range(3) for p in range(2)], axis=1
        )
        g_out = total[:thin, 3 * width :]
        g_up = g_up.astype(F32)
        g_down = g_down.astype(F32)
        vec = total[thin, :count]
    else:
        def whole(*products):
            return jnp.concatenate([tn(a, b).astype(BF) for a, b in products], axis=1)

        def total(grad):
            return lax.psum(reduce_any(grad).astype(F32), "ctx")

        g_down = total(whole((active, second)))
        g_up = total(whole((first_low, hidden)))
        g_out = total(whole((mixed, branch)))
        g_qkv = total(whole(*[(x, p[c]) for c in range(3) for p in (p_one, p_two)]))
        vec = lax.psum(lax.psum_scatter(vec, "dp", scatter_dimension=0, tiled=True), "ctx").reshape(-1)
    grads, pos = [], 0
    for size in sizes:
        grads.append(vec[pos : pos + size])
        pos += size
    g_bqv, g_bout, g_gone, g_sone, g_bup, g_bdown, g_gtwo, g_stwo = grads
    grad_input = put_slots([(0, 0, part_of(grad_in, 0, 1)), (1, 0, in_1)] + in_rest, per, F32)
    return (
        output, grad_input, g_qkv, g_bqv, g_out, g_bout, g_gone, g_sone, g_up, g_bup, g_down, g_bdown, g_gtwo, g_stwo,
    )


def solution(mesh):
    row = P("dp", "ctx", None)
    mat = P("dp", None)
    vec = P("dp")
    weights = (mat, vec, mat, vec, vec, vec, mat, vec, mat, vec, vec, vec)
    return jax.shard_map(
        shards, mesh=mesh, in_specs=(row, vec) + weights + (row,), out_specs=(row, row) + weights, check_vma=False
    )
```

profile of v0, /device:TPU:0, one launch (start us, length us, event | category | flops | bytes accessed | tf_op | source)
XLA Modules:
  0.0 540.2 jit_solution(3066761368113238734)
XLA Ops:
  23.9 38.0 %all-to-all-done = bf16[4,2,128,1024]{3,2,1,0:T(8,128)(2,1)S(1)} async-done(((bf16[4,2,128,1024]{3,2,1,0:T(8,128)(2,1)}), bf16[4,2,128,1024]{3,2,1,0:T(8,128)(2,1)S(1)}, u32[]{:S(2)}, u32[]{:S(2)}) %all-to-all-start) | async-done | bytes 2097184 | tf_op jit(solution)/shard_map/all_to_all | solution.py:125
  70.9 7.3 %collective-permute-done.4 = bf16[144,1536]{1,0:T(8,128)(2,1)S(1)} collective-permute-done((bf16[144,1536]{1,0:T(8,128)(2,1)S(1)}, bf16[144,1536]{1,0:T(8,128)(2,1)S(1)}, u32[]{:S(2)}, u32[]{:S(2)}) %collective-permute-start.4) | collective-permute-done | bytes 442400 | tf_op jit(solution)/shard_map/ppermute | solution.py:29
  98.5 12.3 %qkv.1 = bf16[1024,3072]{1,0:T(8,128)(2,1)} custom-call(s32[4]{0:T(128)} %pad_add_fusion.meta_ref.meta, bf16[1024,1024]{1,0:T(8,128)(2,1)} %bitcast.84, f32[1,3072]{1,0:T(1,128)} %pad_maximum_fusion.5.refs_1_, bf16[4,144,3072]{2,1,0:T(8,128)(2,1)} %copy-done.1, bf16[4,144,3072]{2,1,0:T(8,128)(2,1)} %collective-permute-done.6.refs_3_.refs_4_), custom_call_target="tpu_custom_call" | custom-call | flops 12999999488 | bytes 1000000 | tf_op jit(solution)/shard_map/qkv/pallas_call | solution.py:267
  120.9 20.5 %attend.1 = (bf16[2,512,1024]{2,1,0:T(8,128)(2,1)}, f32[2,4,4,512]{3,2,1,0:T(4,128)}) custom-call(s32[4]{0:T(128)} %pad_add_fusion.meta_ref.meta, bf16[2,512,3072]{2,1,0:T(8,128)(2,1)} %bitcast.145, bf16[2,512,3072]{2,1,0:T(8,128)(2,1)} %bitcast.146, bf16[2,512,3072]{2,1,0:T(8,128)(2,1)} %bitcast.147), custom_call_target="tpu_custom_call" | custom-call | flops 24000000000 | bytes 1000000 | tf_op jit(solution)/shard_map/attend/pallas_call | solution.py:475
  145.0 9.8 %out.1 = (f32[1024,1024]{1,0:T(8,128)}, f32[1024,128]{1,0:T(8,128)}, bf16[1024,1024]{1,0:T(8,128)(2,1)}) custom-call(s32[4]{0:T(128)} %pad_add_fusion.meta_ref.meta, bf16[1024,1024]{1,0:T(8,128)(2,1)} %bitcast.94, bf16[1024,1024]{1,0:T(8,128)(2,1)} %bitcast.85, f32[1,1024]{1,0:T(1,128)} %bitcast.140, f32[1,1024]{1,0:T(1,128)} %bitcast.132, ...), custom_call_target="tpu_custom_call" | custom-call | flops 10000000000 | bytes 1000000 | tf_op jit(solution)/shard_map/out/pallas_call | solution.py:267
  158.7 23.0 %up.1 = (bf16[1024,4096]{1,0:T(8,128)(2,1)}, bf16[1024,4096]{1,0:T(8,128)(2,1)}) custom-call(s32[4]{0:T(128)} %pad_add_fusion.meta_ref.meta, bf16[1024,1024]{1,0:T(8,128)(2,1)} %get-tuple-element.148.refs_0_.refs_1_.refs_2_.refs_3_, f32[1,4096]{1,0:T(1,128)} %bitcast.125, bf16[4,128,5120]{2,1,0:T(8,128)(2,1)} %pad_maximum_fusion.refs_5_.refs_2_.refs_7_, ...), custom_call_target="tpu_custom_call" | custom-call | flops 23000000512 | bytes 1000000 | tf_op jit(solution)/shard_map/up/pallas_call | solution.py:267
  184.3 19.8 %down.1 = (bf16[1024,1024]{1,0:T(8,128)(2,1)}, f32[1024,1024]{1,0:T(8,128)}, bf16[1024,1024]{1,0:T(8,128)(2,1)}, f32[8,1024]{1,0:T(8,128)}, f32[8,1024]{1,0:T(8,128)}, /*index=5*/f32[8,1024]{1,0:T(8,128)}) custom-call(s32[4]{0:T(128)} %pad_add_fusion.meta_ref.meta, bf16[1024,4096]{1,0:T(8,128)(2,1)} %get-tuple-element.152.refs_0_.refs_1_.refs_2_.refs_3_, ...), custom_call_target="tpu_custom_call" | custom-call | flops 20999999488 | bytes 1000000 | tf_op jit(solution)/shard_map/down/pallas_call | solution.py:267
  204.1 9.4 %gd_away.1 = bf16[4,512,1024]{2,1,0:T(8,128)(2,1)} custom-call(s32[4]{0:T(128)} %pad_add_fusion.meta_ref.meta, bf16[1024,4096]{1,0:T(8,128)(2,1)} %get-tuple-element.152.refs_0_.refs_1_.refs_2_.refs_3_, bf16[1024,4096]{1,0:T(8,128)(2,1)} %get-tuple-element.152.refs_0_.refs_1_.refs_2_.refs_3_, ...), custom_call_target="tpu_custom_call" | custom-call | flops 11000000512 | bytes 1000000 | tf_op jit(solution)/shard_map/gd_away/pallas_call | solution.py:632
  216.7 17.3 %hidden.1 = (bf16[1024,4096]{1,0:T(8,128)(2,1)}, f32[8,4096]{1,0:T(8,128)}) custom-call(s32[4]{0:T(128)} %pad_add_fusion.meta_ref.meta, bf16[1024,1024]{1,0:T(8,128)(2,1)} %get-tuple-element.160.refs_4_.refs_0_, bf16[1024,4096]{1,0:T(8,128)(2,1)} %get-tuple-element.161.refs_1_, bf16[8,512,1024]{2,1,0:T(8,128)(2,1)} %bitcast.144), custom_call_target="tpu_custom_call" | custom-call | flops 17999998976 | bytes 1000000 | tf_op jit(solution)/shard_map/hidden/pallas_call | solution.py:267
  236.2 10.3 %gd_keep.1 = (bf16[512,1024]{1,0:T(8,128)(2,1)}, bf16[512,1024]{1,0:T(8,128)(2,1)}, bf16[512,1024]{1,0:T(8,128)(2,1)}, bf16[512,512]{1,0:T(8,128)(2,1)}, bf16[512,512]{1,0:T(8,128)(2,1)}) custom-call(s32[4]{0:T(128)} %pad_add_fusion.meta_ref.meta, bf16[1024,4096]{1,0:T(8,128)(2,1)} %get-tuple-element.152.refs_0_.refs_1_.refs_2_.refs_3_, ...), custom_call_target="tpu_custom_call" | custom-call | flops 11000000512 | bytes 1000000 | tf_op jit(solution)/shard_map/gd_keep/pallas_call | solution.py:632
  251.2 9.7 %gu_away.1 = bf16[4,128,4096]{2,1,0:T(8,128)(2,1)} custom-call(s32[4]{0:T(128)} %pad_add_fusion.meta_ref.meta, bf16[1024,1024]{1,0:T(8,128)(2,1)} %get-tuple-element.148.refs_0_.refs_1_.refs_2_.refs_3_, bf16[1024,1024]{1,0:T(8,128)(2,1)} %get-tuple-element.148.refs_0_.refs_1_.refs_2_.refs_3_, ...), custom_call_target="tpu_custom_call" | custom-call | flops 11000000512 | bytes 1000000 | tf_op jit(solution)/shard_map/gu_away/pallas_call | solution.py:632
  275.0 21.7 %first.1 = (f32[1024,1024]{1,0:T(8,128)}, bf16[1024,1024]{1,0:T(8,128)(2,1)}, bf16[1024,1024]{1,0:T(8,128)(2,1)}, f32[8,1024]{1,0:T(8,128)}, f32[8,1024]{1,0:T(8,128)}, /*index=5*/f32[8,1024]{1,0:T(8,128)}) custom-call(s32[4]{0:T(128)} %pad_add_fusion.meta_ref.meta, bf16[1024,4096]{1,0:T(8,128)(2,1)} %get-tuple-element.179.refs_4_.refs_0_, ...), custom_call_target="tpu_custom_call" | custom-call | flops 23000000512 | bytes 1000000 | tf_op jit(solution)/shard_map/first/pallas_call | solution.py:267
  302.1 10.4 %gu_keep.1 = (bf16[128,4096]{1,0:T(8,128)(2,1)}, bf16[128,4096]{1,0:T(8,128)(2,1)}, bf16[128,4096]{1,0:T(8,128)(2,1)}, bf16[128,2048]{1,0:T(8,128)(2,1)}, bf16[128,2048]{1,0:T(8,128)(2,1)}) custom-call(s32[4]{0:T(128)} %pad_add_fusion.meta_ref.meta, bf16[1024,1024]{1,0:T(8,128)(2,1)} %get-tuple-element.148.refs_0_.refs_1_.refs_2_.refs_3_, ...), custom_call_target="tpu_custom_call" | custom-call | flops 11000000512 | bytes 1000000 | tf_op jit(solution)/shard_map/gu_keep/pallas_call | solution.py:632
  315.5 17.0 %attend_back.2 = (bf16[3,2,512,512]{3,2,1,0:T(8,128)(2,1)}, f32[3,2,8,512]{3,2,1,0:T(8,128)}) custom-call(s32[4]{0:T(128)} %pad_add_fusion.meta_ref.meta, bf16[2,512,3072]{2,1,0:T(8,128)(2,1)} %bitcast.148, bf16[2,512,3072]{2,1,0:T(8,128)(2,1)} %bitcast.149, bf16[2,512,3072]{2,1,0:T(8,128)(2,1)} %bitcast.150, bf16[2,512,1024]{2,1,0:T(8,128)(2,1)} %bitcast.154, ...), custom_call_target="tpu_custom_call" | custom-call | flops 20999999488 | bytes 1000000 | tf_op jit(solution)/shard_map/attend_back/pallas_call | solution.py:503
  337.2 16.7 %attend_back.3 = (bf16[3,2,512,512]{3,2,1,0:T(8,128)(2,1)}, f32[3,2,8,512]{3,2,1,0:T(8,128)}) custom-call(s32[4]{0:T(128)} %pad_add_fusion.meta_ref.meta, bf16[2,512,3072]{2,1,0:T(8,128)(2,1)} %bitcast.151, bf16[2,512,3072]{2,1,0:T(8,128)(2,1)} %bitcast.152, bf16[2,512,3072]{2,1,0:T(8,128)(2,1)} %bitcast.153, bf16[2,512,1024]{2,1,0:T(8,128)(2,1)} %bitcast.155, ...), custom_call_target="tpu_custom_call" | custom-call | flops 20999999488 | bytes 1000000 | tf_op jit(solution)/shard_map/attend_back/pallas_call | solution.py:503
  363.0 12.8 %gb_away.1 = bf16[4,144,4096]{2,1,0:T(8,128)(2,1)} custom-call(s32[4]{0:T(128)} %pad_add_fusion.meta_ref.meta, bf16[1024,1024]{1,0:T(8,128)(2,1)} %bitcast.86, bf16[1024,1024]{1,0:T(8,128)(2,1)} %bitcast.87, bf16[1024,1024]{1,0:T(8,128)(2,1)} %bitcast.88, bf16[1024,1024]{1,0:T(8,128)(2,1)} %bitcast.89, bf16[1024,1024]{1,0:T(8,128)(2,1)} %bitcast.95, ...), custom_call_target="tpu_custom_call" | custom-call | flops 14000000000 | bytes 1000000 | tf_op jit(solution)/shard_map/gb_away/pallas_call | solution.py:632
  378.1 12.9 %input.1 = bf16[1024,1024]{1,0:T(8,128)(2,1)} custom-call(s32[4]{0:T(128)} %pad_add_fusion.meta_ref.meta, bf16[3,1024,512]{2,1,0:T(8,128)(2,1)} %bitcast.105, bf16[3,1024,512]{2,1,0:T(8,128)(2,1)} %bitcast.108, f32[1024,1024]{1,0:T(8,128)} %get-tuple-element.220.refs_2_, bf16[4,144,3072]{2,1,0:T(8,128)(2,1)} %copy-done.1, ...), custom_call_target="tpu_custom_call" | custom-call | flops 14000000000 | bytes 1000000 | tf_op jit(solution)/shard_map/input/pallas_call | solution.py:267
  395.3 13.8 %gb_keep.1 = (bf16[144,4096]{1,0:T(8,128)(2,1)}, bf16[144,4096]{1,0:T(8,128)(2,1)}, bf16[144,4096]{1,0:T(8,128)(2,1)}, bf16[144,2048]{1,0:T(8,128)(2,1)}, bf16[144,2048]{1,0:T(8,128)(2,1)}) custom-call(s32[4]{0:T(128)} %pad_add_fusion.meta_ref.meta, bf16[1024,1024]{1,0:T(8,128)(2,1)} %bitcast.90, bf16[1024,1024]{1,0:T(8,128)(2,1)} %bitcast.91, ...), custom_call_target="tpu_custom_call" | custom-call | flops 3000000000 | bytes 1000000 | tf_op jit(solution)/shard_map/gb_keep/pallas_call | solution.py:632
  417.2 14.1 %collective-permute-done.34 = bf16[1,128,1024]{2,1,0:T(8,128)(2,1)S(1)} collective-permute-done((bf16[1,128,1024]{2,1,0:T(8,128)(2,1)S(1)}, bf16[1,128,1024]{2,1,0:T(8,128)(2,1)S(1)}, u32[]{:S(2)}, u32[]{:S(2)}) %collective-permute-start.34) | collective-permute-done | bytes 262176 | tf_op jit(solution)/shard_map/ppermute | solution.py:29
  444.0 14.2 %collective-permute-done.38 = bf16[1,128,1024]{2,1,0:T(8,128)(2,1)} collective-permute-done((bf16[1,128,1024]{2,1,0:T(8,128)(2,1)}, bf16[1,128,1024]{2,1,0:T(8,128)(2,1)}, u32[]{:S(2)}, u32[]{:S(2)}) %collective-permute-start.38) | collective-permute-done | bytes 262176 | tf_op jit(solution)/shard_map/ppermute | solution.py:29
  474.5 13.7 %collective-permute-done.40 = bf16[1,128,1024]{2,1,0:T(8,128)(2,1)S(1)} collective-permute-done((bf16[1,128,1024]{2,1,0:T(8,128)(2,1)S(1)}, bf16[1,128,1024]{2,1,0:T(8,128)(2,1)S(1)}, u32[]{:S(2)}, u32[]{:S(2)}) %collective-permute-start.40) | collective-permute-done | bytes 262176 | tf_op jit(solution)/shard_map/ppermute | solution.py:29
  488.8 10.9 %collective-permute-done.42 = bf16[144,1024]{1,0:T(8,128)(2,1)S(1)} collective-permute-done((bf16[144,1024]{1,0:T(8,128)(2,1)S(1)}, bf16[144,1024]{1,0:T(8,128)(2,1)S(1)}, u32[]{:S(2)}, u32[]{:S(2)}) %collective-permute-start.42) | collective-permute-done | bytes 294944 | tf_op jit(solution)/shard_map/ppermute | solution.py:29
  501.5 11.9 %collective-permute-done.43 = bf16[144,1024]{1,0:T(8,128)(2,1)S(1)} collective-permute-done((bf16[144,1024]{1,0:T(8,128)(2,1)S(1)}, bf16[144,1024]{1,0:T(8,128)(2,1)S(1)}, u32[]{:S(2)}, u32[]{:S(2)}) %collective-permute-start.43) | collective-permute-done | bytes 294944 | tf_op jit(solution)/shard_map/ppermute | solution.py:29
  515.6 13.2 %collective-permute-done.44 = bf16[144,2048]{1,0:T(8,128)(2,1)S(1)} collective-permute-done((bf16[144,2048]{1,0:T(8,128)(2,1)S(1)}, bf16[144,2048]{1,0:T(8,128)(2,1)S(1)}, u32[]{:S(2)}, u32[]{:S(2)}) %collective-permute-start.44) | collective-permute-done | bytes 589856 | tf_op jit(solution)/shard_map/ppermute | solution.py:29
  (306 shorter events, 164.3 us)
Async XLA Ops:
  7.2 54.7 %all-to-all-start = ((bf16[4,2,128,1024]{3,2,1,0:T(8,128)(2,1)}), bf16[4,2,128,1024]{3,2,1,0:T(8,128)(2,1)S(1)}, u32[]{:S(2)}, u32[]{:S(2)}) async-start(bf16[4,2,128,1024]{3,2,1,0:T(8,128)(2,1)} %bitcast.120), calls=%async_computation | async-start | bytes 4194304 | tf_op jit(solution)/shard_map/all_to_all | solution.py:125
  13.7 169.1 %all-gather.2.cloned.1.call-start = ((), (), s32[]{:S(2)}) async-start(), calls=%async_computation.1 | async-start | bytes 9437184 | tf_op jit(solution)/shard_map/all_gather | solution.py:699
  15.6 50.7 %collective-permute-start.2 = (bf16[128,5120]{1,0:T(8,128)(2,1)}, bf16[128,5120]{1,0:T(8,128)(2,1)S(1)}, u32[]{:S(2)}, u32[]{:S(2)}) collective-permute-start(bf16[128,5120]{1,0:T(8,128)(2,1)} %constant_dynamic-update-slice_fusion), channel_id=1, source_target_pairs={{0,8},{4,12},{8,0},{12,4},{16,24},{20,28},{24,16},{28,20},{1,9},{5... | collective-permute-start | bytes 3932168 | tf_op jit(solution)/shard_map/ppermute | solution.py:29
  17.0 49.2 %collective-permute-start.3 = (bf16[128,5120]{1,0:T(8,128)(2,1)}, bf16[128,5120]{1,0:T(8,128)(2,1)}, u32[]{:S(2)}, u32[]{:S(2)}) collective-permute-start(bf16[128,5120]{1,0:T(8,128)(2,1)} %constant_dynamic-update-slice_fusion), channel_id=1, source_target_pairs={{0,16},{4,20},{8,24},{12,28},{16,0},{20,4},{24,8},{28,12},{1,17},{... | collective-permute-start | bytes 3932168 | tf_op jit(solution)/shard_map/ppermute | solution.py:29
  22.8 42.3 %collective-permute-start = (bf16[144,3072]{1,0:T(8,128)(2,1)}, bf16[144,3072]{1,0:T(8,128)(2,1)}, u32[]{:S(2)}, u32[]{:S(2)}) collective-permute-start(bf16[144,3072]{1,0:T(8,128)(2,1)} %get-tuple-element.273), channel_id=1, source_target_pairs={{0,8},{4,12},{8,0},{12,4},{16,24},{20,28},{24,16},{28,20},{1,9},{5... | collective-permute-start | bytes 2654216 | tf_op jit(solution)/shard_map/ppermute | solution.py:29
  23.3 42.9 %collective-permute-start.1 = (bf16[144,3072]{1,0:T(8,128)(2,1)}, bf16[144,3072]{1,0:T(8,128)(2,1)}, u32[]{:S(2)}, u32[]{:S(2)}) collective-permute-start(bf16[144,3072]{1,0:T(8,128)(2,1)} %get-tuple-element.273), channel_id=1, source_target_pairs={{0,16},{4,20},{8,24},{12,28},{16,0},{20,4},{24,8},{28,12},{1,17},{... | collective-permute-start | bytes 2654216 | tf_op jit(solution)/shard_map/ppermute | solution.py:29
  86.4 24.4 %collective-permute-start.9 = (bf16[2,128,1024]{2,1,0:T(8,128)(2,1)}, bf16[2,128,1024]{2,1,0:T(8,128)(2,1)}, u32[]{:S(2)}, u32[]{:S(2)}) collective-permute-start(bf16[2,128,1024]{2,1,0:T(8,128)(2,1)} %constant_dynamic-slice_fusion.14), channel_id=1, source_target_pairs={{0,1},{1,0},{2,3},{3,2},{4,5},{5,4},{6,7},{7,6},{8,9},{9,8},{10,11... | collective-permute-start | bytes 1572872 | tf_op jit(solution)/shard_map/ppermute | solution.py:29
  89.8 21.0 %collective-permute-start.7 = (bf16[128,2560]{1,0:T(8,128)(2,1)}, bf16[128,2560]{1,0:T(8,128)(2,1)}, u32[]{:S(2)}, u32[]{:S(2)}) collective-permute-start(bf16[128,2560]{1,0:T(8,128)(2,1)} %slice.159), channel_id=1, source_target_pairs={{0,16},{4,20},{8,24},{12,28},{16,0},{20,4},{24,8},{28,12},{1,17},{... | collective-permute-start | bytes 1966088 | tf_op jit(solution)/shard_map/ppermute | solution.py:29
  110.9 245.3 %all-reduce.10.cloned.1.call-start = ((), (), s32[]{:S(2)}) async-start(), calls=%async_computation.2 | async-start | bytes 2097152 | tf_op jit(solution)/shard_map/psum | solution.py:756
  117.3 27.7 %collective-permute-start.10 = (bf16[4,128,5120]{2,1,0:T(8,128)(2,1)}, bf16[4,128,5120]{2,1,0:T(8,128)(2,1)}, u32[]{:S(2)}, u32[]{:S(2)}) collective-permute-start(bf16[4,128,5120]{2,1,0:T(8,128)(2,1)} %pad_maximum_fusion.refs_5_.refs_2_.refs_7_), channel_id=1, source_target_pairs={{0,4},{4,0},{8,12},{12,8},{16,20},{20,16},{24,28},{28,24},{1,5},{5... | collective-permute-start | bytes 15728648 | tf_op jit(solution)/shard_map/ppermute | solution.py:29
  118.4 26.5 %collective-permute-start.11 = (bf16[2,128,1024]{2,1,0:T(8,128)(2,1)S(1)}, bf16[2,128,1024]{2,1,0:T(8,128)(2,1)S(1)}, u32[]{:S(2)}, u32[]{:S(2)}) collective-permute-start(bf16[2,128,1024]{2,1,0:T(8,128)(2,1)S(1)} %constant_dynamic-slice_fusion.13), channel_id=1, source_target_pairs={{0,2},{1,3},{2,0},{3,1},{4,6},{5,7},{6,4},{7,5},{8,10},{9,11},{10,... | collective-permute-start | bytes 1572872 | tf_op jit(solution)/shard_map/ppermute | solution.py:29
  156.4 26.4 %collective-permute-start.12 = (bf16[2,128,1024]{2,1,0:T(8,128)(2,1)S(1)}, bf16[2,128,1024]{2,1,0:T(8,128)(2,1)S(1)}, u32[]{:S(2)}, u32[]{:S(2)}) collective-permute-start(bf16[2,128,1024]{2,1,0:T(8,128)(2,1)S(1)} %get-tuple-element.261), channel_id=1, source_target_pairs={{0,3},{1,2},{2,1},{3,0},{4,7},{5,6},{6,5},{7,4},{8,11},{9,10},{10,... | collective-permute-start | bytes 1572872 | tf_op jit(solution)/shard_map/ppermute | solution.py:29
  213.5 20.5 %collective-permute-start.13 = (bf16[4,512,1024]{2,1,0:T(8,128)(2,1)}, bf16[4,512,1024]{2,1,0:T(8,128)(2,1)}, u32[]{:S(2)}, u32[]{:S(2)}) collective-permute-start(bf16[4,512,1024]{2,1,0:T(8,128)(2,1)} %gd_away.1), channel_id=1, source_target_pairs={{0,4},{4,0},{8,12},{12,8},{16,20},{20,16},{24,28},{28,24},{1,5},{5... | collective-permute-start | bytes 12582920 | tf_op jit(solution)/shard_map/ppermute | solution.py:29
  263.6 35.5 %collective-permute-start.19 = (bf16[4,128,4096]{2,1,0:T(8,128)(2,1)}, bf16[4,128,4096]{2,1,0:T(8,128)(2,1)}, u32[]{:S(2)}, u32[]{:S(2)}) collective-permute-start(bf16[4,128,4096]{2,1,0:T(8,128)(2,1)} %gu_away.1), channel_id=1, source_target_pairs={{0,4},{4,0},{8,12},{12,8},{16,20},{20,16},{24,28},{28,24},{1,5},{5... | collective-permute-start | bytes 12582920 | tf_op jit(solution)/shard_map/ppermute | solution.py:29
  268.6 30.5 %collective-permute-start.21 = (bf16[512,1024]{1,0:T(8,128)(2,1)}, bf16[512,1024]{1,0:T(8,128)(2,1)}, u32[]{:S(2)}, u32[]{:S(2)}) collective-permute-start(bf16[512,1024]{1,0:T(8,128)(2,1)} %add_convert_fusion.7), channel_id=1, source_target_pairs={{0,16},{4,20},{8,24},{12,28},{16,0},{20,4},{24,8},{28,12},{1,17},{... | collective-permute-start | bytes 3145736 | tf_op jit(solution)/shard_map/ppermute | solution.py:29
  271.2 27.8 %collective-permute-start.20 = (bf16[512,1024]{1,0:T(8,128)(2,1)}, bf16[512,1024]{1,0:T(8,128)(2,1)S(1)}, u32[]{:S(2)}, u32[]{:S(2)}) collective-permute-start(bf16[512,1024]{1,0:T(8,128)(2,1)} %add_convert_fusion.8), channel_id=1, source_target_pairs={{0,8},{4,12},{8,0},{12,4},{16,24},{20,28},{24,16},{28,20},{1,9},{5... | collective-permute-start | bytes 3145736 | tf_op jit(solution)/shard_map/ppermute | solution.py:29
  272.8 26.3 %collective-permute-start.22 = (bf16[2,128,1024]{2,1,0:T(8,128)(2,1)}, bf16[2,128,1024]{2,1,0:T(8,128)(2,1)S(1)}, u32[]{:S(2)}, u32[]{:S(2)}) collective-permute-start(bf16[2,128,1024]{2,1,0:T(8,128)(2,1)} %constant_dynamic-slice_fusion.8), channel_id=1, source_target_pairs={{0,3},{1,2},{2,1},{3,0},{4,7},{5,6},{6,5},{7,4},{8,11},{9,10},{10,... | collective-permute-start | bytes 1572872 | tf_op jit(solution)/shard_map/ppermute | solution.py:29
  312.5 21.0 %collective-permute-start.23 = (bf16[128,2048]{1,0:T(8,128)(2,1)}, bf16[128,2048]{1,0:T(8,128)(2,1)S(1)}, u32[]{:S(2)}, u32[]{:S(2)}) collective-permute-start(bf16[128,2048]{1,0:T(8,128)(2,1)} %get-tuple-element.197), channel_id=1, source_target_pairs={{0,16},{4,20},{8,24},{12,28},{16,0},{20,4},{24,8},{28,12},{1,17},{... | collective-permute-start | bytes 1572872 | tf_op jit(solution)/shard_map/ppermute | solution.py:29
  335.8 24.5 %collective-permute-start.26 = (bf16[128,4096]{1,0:T(8,128)(2,1)S(1)}, bf16[128,4096]{1,0:T(8,128)(2,1)}, u32[]{:S(2)}, u32[]{:S(2)}) collective-permute-start(bf16[128,4096]{1,0:T(8,128)(2,1)S(1)} %add_convert_fusion.5), channel_id=1, source_target_pairs={{0,16},{4,20},{8,24},{12,28},{16,0},{20,4},{24,8},{28,12},{1,17},{... | collective-permute-start | bytes 3145736 | tf_op jit(solution)/shard_map/ppermute | solution.py:29
  336.5 24.3 %collective-permute-start.25 = (bf16[128,4096]{1,0:T(8,128)(2,1)S(1)}, bf16[128,4096]{1,0:T(8,128)(2,1)}, u32[]{:S(2)}, u32[]{:S(2)}) collective-permute-start(bf16[128,4096]{1,0:T(8,128)(2,1)S(1)} %add_convert_fusion.6), channel_id=1, source_target_pairs={{0,8},{4,12},{8,0},{12,4},{16,24},{20,28},{24,16},{28,20},{1,9},{5... | collective-permute-start | bytes 3145736 | tf_op jit(solution)/shard_map/ppermute | solution.py:29
  411.8 20.6 %collective-permute-start.32 = (bf16[144,2048]{1,0:T(8,128)(2,1)}, bf16[144,2048]{1,0:T(8,128)(2,1)S(1)}, u32[]{:S(2)}, u32[]{:S(2)}) collective-permute-start(bf16[144,2048]{1,0:T(8,128)(2,1)} %get-tuple-element.235), channel_id=1, source_target_pairs={{0,16},{4,20},{8,24},{12,28},{16,0},{20,4},{24,8},{28,12},{1,17},{... | collective-permute-start | bytes 1769480 | tf_op jit(solution)/shard_map/ppermute | solution.py:29
  434.4 26.0 %collective-permute-start.37 = (bf16[144,4096]{1,0:T(8,128)(2,1)}, bf16[144,4096]{1,0:T(8,128)(2,1)}, u32[]{:S(2)}, u32[]{:S(2)}) collective-permute-start(bf16[144,4096]{1,0:T(8,128)(2,1)} %add_convert_fusion.1), channel_id=1, source_target_pairs={{0,16},{4,20},{8,24},{12,28},{16,0},{20,4},{24,8},{28,12},{1,17},{... | collective-permute-start | bytes 3538952 | tf_op jit(solution)/shard_map/ppermute | solution.py:29
  436.7 26.0 %collective-permute-start.36 = (bf16[144,4096]{1,0:T(8,128)(2,1)}, bf16[144,4096]{1,0:T(8,128)(2,1)}, u32[]{:S(2)}, u32[]{:S(2)}) collective-permute-start(bf16[144,4096]{1,0:T(8,128)(2,1)} %add_convert_fusion.2), channel_id=1, source_target_pairs={{0,8},{4,12},{8,0},{12,4},{16,24},{20,28},{24,16},{28,20},{1,9},{5... | collective-permute-start | bytes 3538952 | tf_op jit(solution)/shard_map/ppermute | solution.py:29
  465.3 23.0 %collective-permute-start.41 = (bf16[144,2048]{1,0:T(8,128)(2,1)S(1)}, bf16[144,2048]{1,0:T(8,128)(2,1)S(1)}, u32[]{:S(2)}, u32[]{:S(2)}) collective-permute-start(bf16[144,2048]{1,0:T(8,128)(2,1)S(1)} %constant_dynamic-slice_fusion.1), channel_id=1, source_target_pairs={{0,1},{1,0},{2,3},{3,2},{4,5},{5,4},{6,7},{7,6},{8,9},{9,8},{10,11... | collective-permute-start | bytes 1769480 | tf_op jit(solution)/shard_map/ppermute | solution.py:29
  (66 other events, 733.0 us)
Sparse Core Ops, SparseCore 0:
  111.0 54.3 all-gather.1
  302.2 50.9 all-reduce.9
where the time goes:
time: 548 us; the launch traced here: 540 us
  Pallas kernels  237 us (43%)
  waiting for transfers between devices  147 us (27%)
  starting transfers between devices  54.9 us (10%)
  other arithmetic  45 us (8%)
  local copies, waits for them, and re-layouts  40.7 us (7%)
  between operations  15.4 us (3%)
    pallas_call x7, Pallas kernels, dense(): pl.pallas_call(kernel, grid_spec=pltpu.PrefetchScalarGridSpec(num_scalar_...  117 us
    ppermute x45, waiting for transfers between devices, swap(): return lax.ppermute(x, axis, [(i, i ^ bit) for i in range(n)])  109 us
    pallas_call x6, Pallas kernels, weight_grad(): pl.pallas_call(kernel, grid_spec=pltpu.PrefetchScalarGridSpec(num_scalar_...  66.3 us
    ppermute x45, starting transfers between devices, swap(): return lax.ppermute(x, axis, [(i, i ^ bit) for i in range(n)])  48.1 us
    all_to_all x1, waiting for transfers between devices, to_sequences(): return lax.all_to_all(block, 'ctx', 0, 0, tiled=True)  38 us
    pallas_call x2, Pallas kernels, attend_back(): pl.pallas_call(attend_back_kernel, grid_spec=pltpu.PrefetchScalarGridSpec...  33.7 us
    pallas_call x1, Pallas kernels, attend(): pl.pallas_call(attend_kernel, grid_spec=pltpu.PrefetchScalarGridSpec(num_...  20.5 us
    convert_element_type x13, other arithmetic, add_low(): return total.astype(BF)  16.6 us
  transfers between devices with their start and end apart: 48, of which 21 were waited for; matrix products, arithmetic and copies ran while one was open for 12% of the time, Pallas kernels for 39%

commit v1 on v0

--- a/solution.py
+++ b/solution.py
@@ -140,12 +140,12 @@
     return out
 
 
-def put_positions(pieces):
-    n = len(pieces)
-    per, blk, width = pieces[0].shape
-    out = jnp.zeros((per, n * blk, width), pieces[0].dtype)
-    for j in range(n):
-        out = lax.dynamic_update_slice_in_dim(out, pieces[j], (lax.axis_index("ctx") ^ j) * blk, axis=1)
+def put_positions(pieces, per):
+    n = lax.axis_size("ctx")
+    blk, width = pieces[0][2].shape[1:]
+    out = jnp.zeros((per, n * blk, width), pieces[0][2].dtype)
+    for j, first, piece in pieces:
+        out = lax.dynamic_update_slice(out, piece, (first, (lax.axis_index("ctx") ^ j) * blk, 0))
     return out
 
 
@@ -371,19 +371,26 @@
     sums[2][...] += fold(low.astype(F32))
 
 
-def hidden_body(meta, rows, vecs, whole, outs, sums):
-    second, deriv = rows
-    if whole[0].pieces:
-        whole[0].cols(0)
-        places = [slice(c, c + 512) for c in range(0, deriv.shape[1], 512)]
-    else:
-        places = range(len(whole[0].copies))
-    for cols in places:
-        if not whole[0].pieces:
-            cols = whole[0].rows(cols)
-        low = (nt(second[...], whole[0].whole[cols, :]) * deriv[:, cols].astype(F32)).astype(BF)
-        outs[0][:, cols] = low
-        sums[0][:, cols] += fold(low.astype(F32))
+def hidden_kernel(second, whole, deriv, out, total):
+    low = (nt(second[...], whole[...]) * deriv[...].astype(F32)).astype(BF)
+    out[...] = low
+    total[...] = fold(low.astype(F32))
+
+
+def hidden_grad(second, whole, deriv, step):
+    rows, width = second.shape
+    ff = whole.shape[0]
+    cols = pl.BlockSpec((rows, step), lambda i: (0, i))
+    return pl.pallas_call(
+        hidden_kernel,
+        grid=(ff // step,),
+        in_specs=[pl.BlockSpec((rows, width), lambda i: (0, 0)), pl.BlockSpec((step, width), lambda i: (i, 0)), cols],
+        out_specs=[cols, pl.BlockSpec((8, step), lambda i: (0, i))],
+        out_shape=[jax.ShapeDtypeStruct((rows, ff), BF), jax.ShapeDtypeStruct((8, ff), F32)],
+        compiler_params=pltpu.CompilerParams(vmem_limit_bytes=60 * MIB),
+        cost_estimate=cost("hidden"),
+        name="hidden",
+    )(second, whole, deriv)
 
 
 def first_body(meta, rows, vecs, whole, outs, sums):
@@ -526,18 +533,17 @@
 def weight_grad(name, meta, odd, lefts, rights, chunk, come=None, extra=None):
     rows = lefts[0].shape[0]
     tall = lefts[0].shape[1] // 8
-    plan = []
-    for li, group in enumerate(rights):
-        for right in group:
-            for c in range((right.shape[0] if right.ndim == 3 else 1) * (right.shape[-1] // chunk)):
-                plan.append((li, right, c))
-    steps = len(plan)
+
+    def count(right):
+        return right[0].shape[0] if isinstance(right, tuple) else right.shape[1] // chunk
+
     flat = [r for group in rights for r in group]
-    firsts, pos = [], 0
+    owners = [li for li, group in enumerate(rights) for _ in group]
+    firsts, steps = [], 0
     for right in flat:
-        firsts.append(pos)
-        pos += (right.shape[0] if right.ndim == 3 else 1) * (right.shape[-1] // chunk)
-    owners = [li for li, group in enumerate(rights) for _ in group]
+        firsts.append(steps)
+        steps += count(right)
+    spread = [(i, r) for i, right in enumerate(flat) for r in (right if isinstance(right, tuple) else (right,))]
     below = 0 if extra is None else extra.shape[1]
     cut = (steps + 1) // 2
     n_left = len(lefts)
@@ -545,8 +551,10 @@
     def kernel(meta_ref, *refs):
         left_refs = refs[: 4 * n_left]
         pos = 4 * n_left
-        right_refs = refs[pos : pos + len(flat)]
-        pos += len(flat)
+        right_refs = [[] for _ in flat]
+        for i, _ in spread:
+            right_refs[i].append(refs[pos])
+            pos += 1
         extra_refs = refs[pos : pos + 4] if below else ()
         pos += len(extra_refs)
         come_ref = refs[pos] if come is not None else None
@@ -555,8 +563,9 @@
         c = pl.program_id(0)
 
         def store(lefts_here, right):
+            joined = tn(jnp.concatenate([left[...] for left in lefts_here], axis=1), right) if tall < 256 else None
             for k in range(4):
-                part = tn(lefts_here[k][...], right)
+                part = tn(lefts_here[k][...], right) if joined is None else joined[k * tall : (k + 1) * tall]
                 if come is None:
                     outs[0][k, 0:tall, :] = part.astype(BF)
                     if below:
@@ -583,26 +592,25 @@
                     if below:
                         outs[4][tall:, :] = low
 
-        for i, right_ref in enumerate(right_refs):
+        for i in range(len(flat)):
             last = firsts[i + 1] if i + 1 < len(flat) else steps
             li = owners[i]
 
             @pl.when((c >= firsts[i]) & (c < last))
-            def _(right_ref=right_ref, li=li):
-                store(left_refs[4 * li : 4 * li + 4], right_ref[...])
+            def _(i=i, li=li):
+                store(left_refs[4 * li : 4 * li + 4], jnp.concatenate([r[...] for r in right_refs[i]], axis=1))
 
     def left_spec(k):
         return pl.BlockSpec((rows, tall), lambda c, m: (0, m[0] ^ (2 * k + odd)))
 
     def right_spec(i, right):
         last = (firsts[i + 1] if i + 1 < len(flat) else steps) - 1
-        inner = right.shape[-1] // chunk
 
         def place(c):
             return jnp.clip(c, firsts[i], last) - firsts[i]
 
         if right.ndim == 3:
-            return pl.BlockSpec((None, rows, chunk), lambda c, m: (place(c) // inner, 0, place(c) % inner))
+            return pl.BlockSpec((None, rows, right.shape[2]), lambda c, m: (place(c), 0, 0))
         return pl.BlockSpec((rows, chunk), lambda c, m: (0, place(c)))
 
     def extra_spec(k):
@@ -610,8 +618,8 @@
 
     high = tall + below
     four = pl.BlockSpec((4, high, chunk), lambda c, m: (0, 0, c))
-    in_specs = [left_spec(k) for _ in lefts for k in range(4)] + [right_spec(i, r) for i, r in enumerate(flat)]
-    args = [left for left in lefts for _ in range(4)] + flat
+    in_specs = [left_spec(k) for _ in lefts for k in range(4)] + [right_spec(i, r) for i, r in spread]
+    args = [left for left in lefts for _ in range(4)] + [r for _, r in spread]
     if below:
         in_specs += [extra_spec(k) for k in range(4)]
         args += [extra] * 4
@@ -660,6 +668,7 @@
     thin = w_qkv.shape[0]
     tuned = ndp == 8
     half = width // (GROUP * HD) // 2
+    cut = (per + 1) // 2
 
     own = lax.dynamic_slice_in_dim(lengths, place * per, per)
     meta = jnp.concatenate([jnp.stack([me, place]).astype(jnp.int32), own])
@@ -710,7 +719,7 @@
     active, deriv = dense(up_body, "up", meta, rows, tile, [first_low], [bup], [up_w], [(ff, BF), (ff, BF)], [])
     active, down_all, cot_3 = sync(active, down_all, cot_3)
     down_w = (down_all.reshape(8, ff // 8, width), None, ff // 8, 0, width, 0)
-    cot = put_positions([part_of(cotangent, 0), cot_1, cot_2, cot_3]).reshape(rows, width)
+    cot = put_positions([(0, 0, part_of(cotangent, 0)), (1, 0, cot_1), (2, 0, cot_2), (3, 0, cot_3)], per).reshape(rows, width)
     out_parts, sum_two, second, s_gtwo, s_stwo, s_bdown = dense(
         functools.partial(down_body, n * blk, per), "down", meta, rows, tile, [active, normed_one, cot],
         [bdown, gone, sone, gtwo, stwo], [down_w], [(width, BF), (width, F32), (width, BF)], [width] * 3,
@@ -718,14 +727,13 @@
     out_parts = out_parts.reshape(per, n * blk, width)
     out_own = part_of(out_parts, 0, 1)
     out_1 = trade(part_of(out_parts, 1, 1), 1)
-    cut = (per + 1) // 2
 
     come = ()
     if tuned:
         (away,) = weight_grad("gd_away", meta, 1, [active], [[second]], 512)
         come = swap(away, "dp", 1)
         second = after(second, away)
-    hidden, s_bup = dense(hidden_body, "hidden", meta, rows, tile, [second, deriv], [], [down_w], [(ff, BF)], [ff])
+    hidden, s_bup = hidden_grad(second, down_all, deriv, 1024)
     hidden, come, out_1, out_parts = sync(hidden, come, out_1, out_parts)
     part = part_of(out_parts, 2, 1)
     out_2 = trade(part[:cut], 2)
@@ -766,10 +774,15 @@
     if tuned:
         p_two, u_near, g_down = sync(p_two, u_near, g_down)
 
-    s_proj = jnp.concatenate([jnp.sum(s_one, axis=(1, 2)), jnp.sum(s_two, axis=(1, 2))], axis=1)
-    vec = [jnp.concatenate([s_proj[0], s_proj[2]])] + [
-        jnp.sum(s, axis=0) for s in (s_bout, s_gone, s_sone, s_bup, s_bdown, s_gtwo, s_stwo)
-    ]
+    eights = (s_bout, s_gone, s_sone, s_bup, s_bdown, s_gtwo, s_stwo)
+    p_two, s_one, s_two, eights = sync(p_two, s_one, s_two, eights)
+    heads = jnp.sum(jnp.concatenate([s_one, s_two], axis=3), axis=(1, 2))
+    vec = jnp.concatenate([heads[0], heads[2], jnp.sum(jnp.concatenate(eights, axis=1), axis=0)])
+    places, pos = [], 0
+    for size in sizes:
+        places.append(vec[pos : pos + ndp * size])
+        pos += ndp * size
+    vec = places
     vec = jnp.concatenate([v.reshape(ndp, -1) for v in vec], axis=1)
 
     come = ()
@@ -777,8 +790,8 @@
         u_keep, u_away = halves_ctx(add_low(u_sums[0], *u_near), 1)
         u_come = swap(u_away, "ctx", 1)
         extra = jnp.pad(vec[:, None, :].astype(BF), ((0, 0), (0, 15), (0, 4 * width - count)))
-        products = ([x, mixed], [[p_one, p_two], [branch]])
-        (away,) = weight_grad("gb_away", meta, 1, *products, 512, extra=extra)
+        products = ([x, mixed], [[(p_one, p_two)], [branch]])
+        (away,) = weight_grad("gb_away", meta, 1, *products, 1024, extra=extra)
         sum_one = after(sum_one, away)
         away, u_come = sync(away, u_come)
         come = swap(away, "dp", 1)
@@ -793,19 +806,19 @@
     if tuned:
         u_half = add_low(u_keep, u_come)
         u_other = swap(u_half, "ctx", 2)
-        b_sums = weight_grad("gb_keep", meta, 0, *products, 512, come=come, extra=extra)
+        b_sums = weight_grad("gb_keep", meta, 0, *products, 1024, come=come, extra=extra)
         b_sums, u_other, in_1, grad_in = sync(b_sums, u_other, in_1, grad_in)
     part_2, part_3 = part_of(grad_in, 2, 1), part_of(grad_in, 3, 1)
     in_2 = trade(part_2[:cut], 2)
     if tuned:
         b_far = send_far(b_sums)
         u_whole = join_ctx(u_half, u_other, 2)
+        b_far, in_2, part_2, part_3, u_whole = sync(b_far, in_2, part_2, part_3, u_whole)
+        b_near = send_near(b_sums, b_far)
         u_other = swap(u_whole, "ctx", 1)
-        b_far, in_2, u_other, part_2, part_3 = sync(b_far, in_2, u_other, part_2, part_3)
-        b_near = send_near(b_sums, b_far)
     in_2b, in_3 = trade(part_2[cut:], 2), trade(part_3[:cut], 3)
     if tuned:
-        b_near, in_2b, in_3, part_3 = sync(b_near, in_2b, in_3, part_3)
+        b_near, in_2b, in_3, part_3, u_other = sync(b_near, in_2b, in_3, part_3, u_other)
         b_keep, b_away = halves_ctx(add_low(b_sums[0], *b_near), 1)
         b_come = swap(b_away, "ctx", 1)
     in_3b = trade(part_3[cut:], 3)
@@ -815,10 +828,7 @@
         b_half = add_low(b_keep, b_come)
         g_up = join_ctx(u_whole, u_other, 1)
         total = whole_ctx(whole_ctx(halve_ctx(b_half, 2), 2), 1).astype(F32)
-        part = width // 2
-        g_qkv = jnp.concatenate(
-            [total[:thin, (p * 3 + c) * part : (p * 3 + c + 1) * part] for c in range(3) for p in range(2)], axis=1
-        )
+        g_qkv = total[:thin, : 3 * width]
         g_out = total[:thin, 3 * width :]
         g_up = g_up.astype(F32)
         g_down = g_down.astype(F32)

time: 548 us -> 534 us (0.974)
  other arithmetic: 45 us -> 37.2 us
  Pallas kernels: 237 us -> 231 us
    pallas_call x7 -> x6, Pallas kernels: 117 us -> 99.4 us  [dense(): pl.pallas_call(kernel, grid_spec=pltpu.PrefetchScalarGridSpec(num_scalar_...]
    pallas_call x0 -> x1, Pallas kernels: none -> 15 us  [hidden_grad(): pl.pallas_call(hidden_kernel, grid=(ff // step,), in_specs=[pl.BlockSpec(...]
    reduce_sum x9 -> x2, other arithmetic: 6.64 us -> 0.14 us  [the longest x1 0.09 us: shards(): jnp.sum(jnp.concatenate(eights, axis=1), axis=0)]
  transfers between devices with their start and end apart: 48 -> 48, of which waited for: 21 -> 21; matrix products, arithmetic and copies ran while one was open for 12% -> 10% of each run, Pallas kernels for 39% -> 38%
where the time goes in v1:
time: 534 us; the launch traced here: 526 us
  Pallas kernels  231 us (43%)
  waiting for transfers between devices  149 us (28%)
  starting transfers between devices  52.6 us (10%)
  local copies, waits for them, and re-layouts  40.7 us (8%)
  other arithmetic  37.2 us (7%)
  between operations  15.6 us (3%)
    ppermute x45, waiting for transfers between devices, swap(): return lax.ppermute(x, axis, [(i, i ^ bit) for i in range(n)])  109 us
    pallas_call x6, Pallas kernels, dense(): pl.pallas_call(kernel, grid_spec=pltpu.PrefetchScalarGridSpec(num_scalar_...  99.4 us
    pallas_call x6, Pallas kernels, weight_grad(): pl.pallas_call(kernel, grid_spec=pltpu.PrefetchScalarGridSpec(num_scalar_...  63 us
    ppermute x45, starting transfers between devices, swap(): return lax.ppermute(x, axis, [(i, i ^ bit) for i in range(n)])  45.8 us
    all_to_all x1, waiting for transfers between devices, to_sequences(): return lax.all_to_all(block, 'ctx', 0, 0, tiled=True)  38 us
    pallas_call x2, Pallas kernels, attend_back(): pl.pallas_call(attend_back_kernel, grid_spec=pltpu.PrefetchScalarGridSpec...  33.3 us
    pallas_call x1, Pallas kernels, attend(): pl.pallas_call(attend_kernel, grid_spec=pltpu.PrefetchScalarGridSpec(num_...  20.5 us
    convert_element_type x13, other arithmetic, add_low(): return total.astype(BF)  15.3 us
  transfers between devices with their start and end apart: 48, of which 21 were waited for; matrix products, arithmetic and copies ran while one was open for 10% of the time, Pallas kernels for 38%

profile of v1, /device:TPU:0, one launch (start us, length us, event | category | flops | bytes accessed | tf_op | source)
XLA Modules:
  0.0 526.0 jit_solution(3197377747498041098)
XLA Ops:
  23.9 38.0 %all-to-all-done = bf16[4,2,128,1024]{3,2,1,0:T(8,128)(2,1)S(1)} async-done(((bf16[4,2,128,1024]{3,2,1,0:T(8,128)(2,1)}), bf16[4,2,128,1024]{3,2,1,0:T(8,128)(2,1)S(1)}, u32[]{:S(2)}, u32[]{:S(2)}) %all-to-all-start) | async-done | bytes 2097184 | tf_op jit(solution)/shard_map/all_to_all | solution.py:125
  70.9 7.3 %collective-permute-done.4 = bf16[144,1536]{1,0:T(8,128)(2,1)S(1)} collective-permute-done((bf16[144,1536]{1,0:T(8,128)(2,1)S(1)}, bf16[144,1536]{1,0:T(8,128)(2,1)S(1)}, u32[]{:S(2)}, u32[]{:S(2)}) %collective-permute-start.4) | collective-permute-done | bytes 442400 | tf_op jit(solution)/shard_map/ppermute | solution.py:29
  98.5 12.3 %qkv.1 = bf16[1024,3072]{1,0:T(8,128)(2,1)} custom-call(s32[4]{0:T(128)} %pad_add_fusion.meta_ref.meta, bf16[1024,1024]{1,0:T(8,128)(2,1)} %bitcast.78, f32[1,3072]{1,0:T(1,128)} %pad_maximum_fusion.5.refs_1_, bf16[4,144,3072]{2,1,0:T(8,128)(2,1)} %copy-done.1, bf16[4,144,3072]{2,1,0:T(8,128)(2,1)} %collective-permute-done.6.refs_3_.refs_4_), custom_call_target="tpu_custom_call" | custom-call | flops 12999999488 | bytes 1000000 | tf_op jit(solution)/shard_map/qkv/pallas_call | solution.py:267
  120.8 20.5 %attend.1 = (bf16[2,512,1024]{2,1,0:T(8,128)(2,1)}, f32[2,4,4,512]{3,2,1,0:T(4,128)}) custom-call(s32[4]{0:T(128)} %pad_add_fusion.meta_ref.meta, bf16[2,512,3072]{2,1,0:T(8,128)(2,1)} %bitcast.132, bf16[2,512,3072]{2,1,0:T(8,128)(2,1)} %bitcast.133, bf16[2,512,3072]{2,1,0:T(8,128)(2,1)} %bitcast.134), custom_call_target="tpu_custom_call" | custom-call | flops 24000000000 | bytes 1000000 | tf_op jit(solution)/shard_map/attend/pallas_call | solution.py:482
  145.0 9.7 %out.1 = (f32[1024,1024]{1,0:T(8,128)}, f32[1024,128]{1,0:T(8,128)}, bf16[1024,1024]{1,0:T(8,128)(2,1)}) custom-call(s32[4]{0:T(128)} %pad_add_fusion.meta_ref.meta, bf16[1024,1024]{1,0:T(8,128)(2,1)} %bitcast.88, bf16[1024,1024]{1,0:T(8,128)(2,1)} %bitcast.79, f32[1,1024]{1,0:T(1,128)} %bitcast.128, f32[1,1024]{1,0:T(1,128)} %bitcast.120, ...), custom_call_target="tpu_custom_call" | custom-call | flops 10000000000 | bytes 1000000 | tf_op jit(solution)/shard_map/out/pallas_call | solution.py:267
  158.7 22.8 %up.1 = (bf16[1024,4096]{1,0:T(8,128)(2,1)}, bf16[1024,4096]{1,0:T(8,128)(2,1)}) custom-call(s32[4]{0:T(128)} %pad_add_fusion.meta_ref.meta, bf16[1024,1024]{1,0:T(8,128)(2,1)} %get-tuple-element.159.refs_0_.refs_1_.refs_2_.refs_3_, f32[1,4096]{1,0:T(1,128)} %bitcast.119, bf16[4,128,5120]{2,1,0:T(8,128)(2,1)} %pad_maximum_fusion.refs_5_.refs_2_.refs_7_, ...), custom_call_target="tpu_custom_call" | custom-call | flops 23000000512 | bytes 1000000 | tf_op jit(solution)/shard_map/up/pallas_call | solution.py:267
  184.1 19.9 %down.1 = (bf16[1024,1024]{1,0:T(8,128)(2,1)}, f32[1024,1024]{1,0:T(8,128)}, bf16[1024,1024]{1,0:T(8,128)(2,1)}, f32[8,1024]{1,0:T(8,128)}, f32[8,1024]{1,0:T(8,128)}, /*index=5*/f32[8,1024]{1,0:T(8,128)}) custom-call(s32[4]{0:T(128)} %pad_add_fusion.meta_ref.meta, bf16[1024,4096]{1,0:T(8,128)(2,1)} %get-tuple-element.163.refs_0_.refs_1_.refs_2_.refs_3_, ...), custom_call_target="tpu_custom_call" | custom-call | flops 20999999488 | bytes 1000000 | tf_op jit(solution)/shard_map/down/pallas_call | solution.py:267
  204.0 9.4 %gd_away.1 = bf16[4,512,1024]{2,1,0:T(8,128)(2,1)} custom-call(s32[4]{0:T(128)} %pad_add_fusion.meta_ref.meta, bf16[1024,4096]{1,0:T(8,128)(2,1)} %get-tuple-element.163.refs_0_.refs_1_.refs_2_.refs_3_, bf16[1024,4096]{1,0:T(8,128)(2,1)} %get-tuple-element.163.refs_0_.refs_1_.refs_2_.refs_3_, ...), custom_call_target="tpu_custom_call" | custom-call | flops 11000000512 | bytes 1000000 | tf_op jit(solution)/shard_map/gd_away/pallas_call | solution.py:640
  216.6 15.0 %hidden.1 = (bf16[1024,4096]{1,0:T(8,128)(2,1)}, f32[8,4096]{1,0:T(8,128)}) custom-call(bf16[1024,1024]{1,0:T(8,128)(2,1)} %get-tuple-element.171.refs_4_.second, bf16[4096,1024]{1,0:T(8,128)(2,1)} %all-gather.2.cloned.1.call-done.whole, bf16[1024,4096]{1,0:T(8,128)(2,1)} %get-tuple-element.172.deriv), custom_call_target="tpu_custom_call" | custom-call | flops 17999998976 | bytes 1000000 | tf_op jit(solution)/shard_map/hidden/pallas_call | solution.py:384
  233.8 10.5 %gd_keep.1 = (bf16[512,1024]{1,0:T(8,128)(2,1)}, bf16[512,1024]{1,0:T(8,128)(2,1)}, bf16[512,1024]{1,0:T(8,128)(2,1)}, bf16[512,512]{1,0:T(8,128)(2,1)}, bf16[512,512]{1,0:T(8,128)(2,1)}) custom-call(s32[4]{0:T(128)} %pad_add_fusion.meta_ref.meta, bf16[1024,4096]{1,0:T(8,128)(2,1)} %get-tuple-element.163.refs_0_.refs_1_.refs_2_.refs_3_, ...), custom_call_target="tpu_custom_call" | custom-call | flops 11000000512 | bytes 1000000 | tf_op jit(solution)/shard_map/gd_keep/pallas_call | solution.py:640
  248.9 9.6 %gu_away.1 = bf16[4,128,4096]{2,1,0:T(8,128)(2,1)} custom-call(s32[4]{0:T(128)} %pad_add_fusion.meta_ref.meta, bf16[1024,1024]{1,0:T(8,128)(2,1)} %get-tuple-element.159.refs_0_.refs_1_.refs_2_.refs_3_, bf16[1024,1024]{1,0:T(8,128)(2,1)} %get-tuple-element.159.refs_0_.refs_1_.refs_2_.refs_3_, ...), custom_call_target="tpu_custom_call" | custom-call | flops 11000000512 | bytes 1000000 | tf_op jit(solution)/shard_map/gu_away/pallas_call | solution.py:640
  270.3 21.5 %first.1 = (f32[1024,1024]{1,0:T(8,128)}, bf16[1024,1024]{1,0:T(8,128)(2,1)}, bf16[1024,1024]{1,0:T(8,128)(2,1)}, f32[8,1024]{1,0:T(8,128)}, f32[8,1024]{1,0:T(8,128)}, /*index=5*/f32[8,1024]{1,0:T(8,128)}) custom-call(s32[4]{0:T(128)} %pad_add_fusion.meta_ref.meta, bf16[1024,4096]{1,0:T(8,128)(2,1)} %get-tuple-element.190.refs_4_.refs_0_, ...), custom_call_target="tpu_custom_call" | custom-call | flops 23000000512 | bytes 1000000 | tf_op jit(solution)/shard_map/first/pallas_call | solution.py:267
  294.9 10.5 %gu_keep.1 = (bf16[128,4096]{1,0:T(8,128)(2,1)}, bf16[128,4096]{1,0:T(8,128)(2,1)}, bf16[128,4096]{1,0:T(8,128)(2,1)}, bf16[128,2048]{1,0:T(8,128)(2,1)}, bf16[128,2048]{1,0:T(8,128)(2,1)}) custom-call(s32[4]{0:T(128)} %pad_add_fusion.meta_ref.meta, bf16[1024,1024]{1,0:T(8,128)(2,1)} %get-tuple-element.159.refs_0_.refs_1_.refs_2_.refs_3_, ...), custom_call_target="tpu_custom_call" | custom-call | flops 11000000512 | bytes 1000000 | tf_op jit(solution)/shard_map/gu_keep/pallas_call | solution.py:640
  308.4 16.6 %attend_back.2 = (bf16[3,2,512,512]{3,2,1,0:T(8,128)(2,1)}, f32[3,2,8,512]{3,2,1,0:T(8,128)}) custom-call(s32[4]{0:T(128)} %pad_add_fusion.meta_ref.meta, bf16[2,512,3072]{2,1,0:T(8,128)(2,1)} %bitcast.135, bf16[2,512,3072]{2,1,0:T(8,128)(2,1)} %bitcast.136, bf16[2,512,3072]{2,1,0:T(8,128)(2,1)} %bitcast.137, bf16[2,512,1024]{2,1,0:T(8,128)(2,1)} %bitcast.141, ...), custom_call_target="tpu_custom_call" | custom-call | flops 20999999488 | bytes 1000000 | tf_op jit(solution)/shard_map/attend_back/pallas_call | solution.py:510
  327.2 16.7 %attend_back.3 = (bf16[3,2,512,512]{3,2,1,0:T(8,128)(2,1)}, f32[3,2,8,512]{3,2,1,0:T(8,128)}) custom-call(s32[4]{0:T(128)} %pad_add_fusion.meta_ref.meta, bf16[2,512,3072]{2,1,0:T(8,128)(2,1)} %bitcast.138, bf16[2,512,3072]{2,1,0:T(8,128)(2,1)} %bitcast.139, bf16[2,512,3072]{2,1,0:T(8,128)(2,1)} %bitcast.140, bf16[2,512,1024]{2,1,0:T(8,128)(2,1)} %bitcast.142, ...), custom_call_target="tpu_custom_call" | custom-call | flops 20999999488 | bytes 1000000 | tf_op jit(solution)/shard_map/attend_back/pallas_call | solution.py:510
  355.2 11.1 %gb_away.1 = bf16[4,144,4096]{2,1,0:T(8,128)(2,1)} custom-call(s32[4]{0:T(128)} %pad_add_fusion.meta_ref.meta, bf16[1024,1024]{1,0:T(8,128)(2,1)} %bitcast.80, bf16[1024,1024]{1,0:T(8,128)(2,1)} %bitcast.81, bf16[1024,1024]{1,0:T(8,128)(2,1)} %bitcast.82, bf16[1024,1024]{1,0:T(8,128)(2,1)} %bitcast.83, bf16[1024,1024]{1,0:T(8,128)(2,1)} %bitcast.89, ...), custom_call_target="tpu_custom_call" | custom-call | flops 14000000000 | bytes 1000000 | tf_op jit(solution)/shard_map/gb_away/pallas_call | solution.py:640
  368.6 13.2 %input.1 = bf16[1024,1024]{1,0:T(8,128)(2,1)} custom-call(s32[4]{0:T(128)} %pad_add_fusion.meta_ref.meta, bf16[3,1024,512]{2,1,0:T(8,128)(2,1)} %bitcast.99, bf16[3,1024,512]{2,1,0:T(8,128)(2,1)} %bitcast.102, f32[1024,1024]{1,0:T(8,128)} %get-tuple-element.241.refs_2_, bf16[4,144,3072]{2,1,0:T(8,128)(2,1)} %copy-done.1, ...), custom_call_target="tpu_custom_call" | custom-call | flops 14000000000 | bytes 1000000 | tf_op jit(solution)/shard_map/input/pallas_call | solution.py:267
  386.1 12.0 %gb_keep.1 = (bf16[144,4096]{1,0:T(8,128)(2,1)}, bf16[144,4096]{1,0:T(8,128)(2,1)}, bf16[144,4096]{1,0:T(8,128)(2,1)}, bf16[144,2048]{1,0:T(8,128)(2,1)}, bf16[144,2048]{1,0:T(8,128)(2,1)}) custom-call(s32[4]{0:T(128)} %pad_add_fusion.meta_ref.meta, bf16[1024,1024]{1,0:T(8,128)(2,1)} %bitcast.84, bf16[1024,1024]{1,0:T(8,128)(2,1)} %bitcast.85, ...), custom_call_target="tpu_custom_call" | custom-call | flops 3000000000 | bytes 1000000 | tf_op jit(solution)/shard_map/gb_keep/pallas_call | solution.py:640
  407.8 10.3 %collective-permute-done.34 = bf16[1,128,1024]{2,1,0:T(8,128)(2,1)S(1)} collective-permute-done((bf16[1,128,1024]{2,1,0:T(8,128)(2,1)S(1)}, bf16[1,128,1024]{2,1,0:T(8,128)(2,1)S(1)}, u32[]{:S(2)}, u32[]{:S(2)}) %collective-permute-start.34) | collective-permute-done | bytes 262176 | tf_op jit(solution)/shard_map/ppermute | solution.py:29
  433.8 7.9 %collective-permute-done.37 = bf16[1,128,1024]{2,1,0:T(8,128)(2,1)S(1)} collective-permute-done((bf16[1,128,1024]{2,1,0:T(8,128)(2,1)S(1)}, bf16[1,128,1024]{2,1,0:T(8,128)(2,1)S(1)}, u32[]{:S(2)}, u32[]{:S(2)}) %collective-permute-start.37) | collective-permute-done | bytes 262176 | tf_op jit(solution)/shard_map/ppermute | solution.py:29
  456.1 17.5 %collective-permute-done.40 = bf16[1,128,1024]{2,1,0:T(8,128)(2,1)S(1)} collective-permute-done((bf16[1,128,1024]{2,1,0:T(8,128)(2,1)S(1)}, bf16[1,128,1024]{2,1,0:T(8,128)(2,1)S(1)}, u32[]{:S(2)}, u32[]{:S(2)}) %collective-permute-start.40) | collective-permute-done | bytes 262176 | tf_op jit(solution)/shard_map/ppermute | solution.py:29
  475.0 10.1 %collective-permute-done.42 = bf16[144,1024]{1,0:T(8,128)(2,1)S(1)} collective-permute-done((bf16[144,1024]{1,0:T(8,128)(2,1)S(1)}, bf16[144,1024]{1,0:T(8,128)(2,1)S(1)}, u32[]{:S(2)}, u32[]{:S(2)}) %collective-permute-start.42) | collective-permute-done | bytes 294944 | tf_op jit(solution)/shard_map/ppermute | solution.py:29
  486.8 12.2 %collective-permute-done.43 = bf16[144,1024]{1,0:T(8,128)(2,1)S(1)} collective-permute-done((bf16[144,1024]{1,0:T(8,128)(2,1)S(1)}, bf16[144,1024]{1,0:T(8,128)(2,1)S(1)}, u32[]{:S(2)}, u32[]{:S(2)}) %collective-permute-start.43) | collective-permute-done | bytes 294944 | tf_op jit(solution)/shard_map/ppermute | solution.py:29
  499.3 15.1 %collective-permute-done.44 = bf16[144,2048]{1,0:T(8,128)(2,1)S(1)} collective-permute-done((bf16[144,2048]{1,0:T(8,128)(2,1)S(1)}, bf16[144,2048]{1,0:T(8,128)(2,1)S(1)}, u32[]{:S(2)}, u32[]{:S(2)}) %collective-permute-start.44) | collective-permute-done | bytes 589856 | tf_op jit(solution)/shard_map/ppermute | solution.py:29
  (308 shorter events, 160.8 us)
Async XLA Ops:
  7.2 54.7 %all-to-all-start = ((bf16[4,2,128,1024]{3,2,1,0:T(8,128)(2,1)}), bf16[4,2,128,1024]{3,2,1,0:T(8,128)(2,1)S(1)}, u32[]{:S(2)}, u32[]{:S(2)}) async-start(bf16[4,2,128,1024]{3,2,1,0:T(8,128)(2,1)} %bitcast.114), calls=%async_computation | async-start | bytes 4194304 | tf_op jit(solution)/shard_map/all_to_all | solution.py:125
  13.7 168.9 %all-gather.2.cloned.1.call-start = ((), (), s32[]{:S(2)}) async-start(), calls=%async_computation.1 | async-start | bytes 9437184 | tf_op jit(solution)/shard_map/all_gather | solution.py:708
  15.6 50.7 %collective-permute-start.2 = (bf16[128,5120]{1,0:T(8,128)(2,1)}, bf16[128,5120]{1,0:T(8,128)(2,1)S(1)}, u32[]{:S(2)}, u32[]{:S(2)}) collective-permute-start(bf16[128,5120]{1,0:T(8,128)(2,1)} %constant_dynamic-update-slice_fusion), channel_id=1, source_target_pairs={{0,8},{4,12},{8,0},{12,4},{16,24},{20,28},{24,16},{28,20},{1,9},{5... | collective-permute-start | bytes 3932168 | tf_op jit(solution)/shard_map/ppermute | solution.py:29
  17.0 49.2 %collective-permute-start.3 = (bf16[128,5120]{1,0:T(8,128)(2,1)}, bf16[128,5120]{1,0:T(8,128)(2,1)}, u32[]{:S(2)}, u32[]{:S(2)}) collective-permute-start(bf16[128,5120]{1,0:T(8,128)(2,1)} %constant_dynamic-update-slice_fusion), channel_id=1, source_target_pairs={{0,16},{4,20},{8,24},{12,28},{16,0},{20,4},{24,8},{28,12},{1,17},{... | collective-permute-start | bytes 3932168 | tf_op jit(solution)/shard_map/ppermute | solution.py:29
  22.8 42.3 %collective-permute-start = (bf16[144,3072]{1,0:T(8,128)(2,1)}, bf16[144,3072]{1,0:T(8,128)(2,1)}, u32[]{:S(2)}, u32[]{:S(2)}) collective-permute-start(bf16[144,3072]{1,0:T(8,128)(2,1)} %get-tuple-element.295), channel_id=1, source_target_pairs={{0,8},{4,12},{8,0},{12,4},{16,24},{20,28},{24,16},{28,20},{1,9},{5... | collective-permute-start | bytes 2654216 | tf_op jit(solution)/shard_map/ppermute | solution.py:29
  23.3 42.9 %collective-permute-start.1 = (bf16[144,3072]{1,0:T(8,128)(2,1)}, bf16[144,3072]{1,0:T(8,128)(2,1)}, u32[]{:S(2)}, u32[]{:S(2)}) collective-permute-start(bf16[144,3072]{1,0:T(8,128)(2,1)} %get-tuple-element.295), channel_id=1, source_target_pairs={{0,16},{4,20},{8,24},{12,28},{16,0},{20,4},{24,8},{28,12},{1,17},{... | collective-permute-start | bytes 2654216 | tf_op jit(solution)/shard_map/ppermute | solution.py:29
  86.4 24.4 %collective-permute-start.9 = (bf16[2,128,1024]{2,1,0:T(8,128)(2,1)}, bf16[2,128,1024]{2,1,0:T(8,128)(2,1)}, u32[]{:S(2)}, u32[]{:S(2)}) collective-permute-start(bf16[2,128,1024]{2,1,0:T(8,128)(2,1)} %constant_dynamic-slice_fusion.14), channel_id=1, source_target_pairs={{0,1},{1,0},{2,3},{3,2},{4,5},{5,4},{6,7},{7,6},{8,9},{9,8},{10,11... | collective-permute-start | bytes 1572872 | tf_op jit(solution)/shard_map/ppermute | solution.py:29
  89.8 21.0 %collective-permute-start.7 = (bf16[128,2560]{1,0:T(8,128)(2,1)}, bf16[128,2560]{1,0:T(8,128)(2,1)}, u32[]{:S(2)}, u32[]{:S(2)}) collective-permute-start(bf16[128,2560]{1,0:T(8,128)(2,1)} %slice.228), channel_id=1, source_target_pairs={{0,16},{4,20},{8,24},{12,28},{16,0},{20,4},{24,8},{28,12},{1,17},{... | collective-permute-start | bytes 1966088 | tf_op jit(solution)/shard_map/ppermute | solution.py:29
  110.9 235.2 %all-reduce.10.cloned.1.call-start = ((), (), s32[]{:S(2)}) async-start(), calls=%async_computation.2 | async-start | bytes 2097152 | tf_op jit(solution)/shard_map/psum | solution.py:764
  117.3 27.7 %collective-permute-start.10 = (bf16[4,128,5120]{2,1,0:T(8,128)(2,1)}, bf16[4,128,5120]{2,1,0:T(8,128)(2,1)}, u32[]{:S(2)}, u32[]{:S(2)}) collective-permute-start(bf16[4,128,5120]{2,1,0:T(8,128)(2,1)} %pad_maximum_fusion.refs_5_.refs_2_.refs_7_), channel_id=1, source_target_pairs={{0,4},{4,0},{8,12},{12,8},{16,20},{20,16},{24,28},{28,24},{1,5},{5... | collective-permute-start | bytes 15728648 | tf_op jit(solution)/shard_map/ppermute | solution.py:29
  118.4 26.5 %collective-permute-start.11 = (bf16[2,128,1024]{2,1,0:T(8,128)(2,1)S(1)}, bf16[2,128,1024]{2,1,0:T(8,128)(2,1)S(1)}, u32[]{:S(2)}, u32[]{:S(2)}) collective-permute-start(bf16[2,128,1024]{2,1,0:T(8,128)(2,1)S(1)} %constant_dynamic-slice_fusion.13), channel_id=1, source_target_pairs={{0,2},{1,3},{2,0},{3,1},{4,6},{5,7},{6,4},{7,5},{8,10},{9,11},{10,... | collective-permute-start | bytes 1572872 | tf_op jit(solution)/shard_map/ppermute | solution.py:29
  156.4 26.3 %collective-permute-start.12 = (bf16[2,128,1024]{2,1,0:T(8,128)(2,1)S(1)}, bf16[2,128,1024]{2,1,0:T(8,128)(2,1)S(1)}, u32[]{:S(2)}, u32[]{:S(2)}) collective-permute-start(bf16[2,128,1024]{2,1,0:T(8,128)(2,1)S(1)} %get-tuple-element.283), channel_id=1, source_target_pairs={{0,3},{1,2},{2,1},{3,0},{4,7},{5,6},{6,5},{7,4},{8,11},{9,10},{10,... | collective-permute-start | bytes 1572872 | tf_op jit(solution)/shard_map/ppermute | solution.py:29
  261.3 30.7 %collective-permute-start.19 = (bf16[4,128,4096]{2,1,0:T(8,128)(2,1)}, bf16[4,128,4096]{2,1,0:T(8,128)(2,1)}, u32[]{:S(2)}, u32[]{:S(2)}) collective-permute-start(bf16[4,128,4096]{2,1,0:T(8,128)(2,1)} %gu_away.1), channel_id=1, source_target_pairs={{0,4},{4,0},{8,12},{12,8},{16,20},{20,16},{24,28},{28,24},{1,5},{5... | collective-permute-start | bytes 12582920 | tf_op jit(solution)/shard_map/ppermute | solution.py:29
  263.9 27.9 %collective-permute-start.21 = (bf16[512,1024]{1,0:T(8,128)(2,1)}, bf16[512,1024]{1,0:T(8,128)(2,1)}, u32[]{:S(2)}, u32[]{:S(2)}) collective-permute-start(bf16[512,1024]{1,0:T(8,128)(2,1)} %add_convert_fusion.7), channel_id=1, source_target_pairs={{0,16},{4,20},{8,24},{12,28},{16,0},{20,4},{24,8},{28,12},{1,17},{... | collective-permute-start | bytes 3145736 | tf_op jit(solution)/shard_map/ppermute | solution.py:29
  266.6 25.5 %collective-permute-start.20 = (bf16[512,1024]{1,0:T(8,128)(2,1)}, bf16[512,1024]{1,0:T(8,128)(2,1)S(1)}, u32[]{:S(2)}, u32[]{:S(2)}) collective-permute-start(bf16[512,1024]{1,0:T(8,128)(2,1)} %add_convert_fusion.8), channel_id=1, source_target_pairs={{0,8},{4,12},{8,0},{12,4},{16,24},{20,28},{24,16},{28,20},{1,9},{5... | collective-permute-start | bytes 3145736 | tf_op jit(solution)/shard_map/ppermute | solution.py:29
  268.1 23.7 %collective-permute-start.22 = (bf16[2,128,1024]{2,1,0:T(8,128)(2,1)}, bf16[2,128,1024]{2,1,0:T(8,128)(2,1)S(1)}, u32[]{:S(2)}, u32[]{:S(2)}) collective-permute-start(bf16[2,128,1024]{2,1,0:T(8,128)(2,1)} %constant_dynamic-slice_fusion.8), channel_id=1, source_target_pairs={{0,3},{1,2},{2,1},{3,0},{4,7},{5,6},{6,5},{7,4},{8,11},{9,10},{10,... | collective-permute-start | bytes 1572872 | tf_op jit(solution)/shard_map/ppermute | solution.py:29
  325.3 24.6 %collective-permute-start.26 = (bf16[128,4096]{1,0:T(8,128)(2,1)S(1)}, bf16[128,4096]{1,0:T(8,128)(2,1)}, u32[]{:S(2)}, u32[]{:S(2)}) collective-permute-start(bf16[128,4096]{1,0:T(8,128)(2,1)S(1)} %add_convert_fusion.5), channel_id=1, source_target_pairs={{0,16},{4,20},{8,24},{12,28},{16,0},{20,4},{24,8},{28,12},{1,17},{... | collective-permute-start | bytes 3145736 | tf_op jit(solution)/shard_map/ppermute | solution.py:29
  326.4 24.6 %collective-permute-start.25 = (bf16[128,4096]{1,0:T(8,128)(2,1)S(1)}, bf16[128,4096]{1,0:T(8,128)(2,1)}, u32[]{:S(2)}, u32[]{:S(2)}) collective-permute-start(bf16[128,4096]{1,0:T(8,128)(2,1)S(1)} %add_convert_fusion.6), channel_id=1, source_target_pairs={{0,8},{4,12},{8,0},{12,4},{16,24},{20,28},{24,16},{28,20},{1,9},{5... | collective-permute-start | bytes 3145736 | tf_op jit(solution)/shard_map/ppermute | solution.py:29
  420.0 28.5 %collective-permute-start.36 = (bf16[144,4096]{1,0:T(8,128)(2,1)}, bf16[144,4096]{1,0:T(8,128)(2,1)}, u32[]{:S(2)}, u32[]{:S(2)}) collective-permute-start(bf16[144,4096]{1,0:T(8,128)(2,1)} %add_convert_fusion.1), channel_id=1, source_target_pairs={{0,16},{4,20},{8,24},{12,28},{16,0},{20,4},{24,8},{28,12},{1,17},{... | collective-permute-start | bytes 3538952 | tf_op jit(solution)/shard_map/ppermute | solution.py:29
  422.5 27.4 %collective-permute-start.35 = (bf16[144,4096]{1,0:T(8,128)(2,1)}, bf16[144,4096]{1,0:T(8,128)(2,1)}, u32[]{:S(2)}, u32[]{:S(2)}) collective-permute-start(bf16[144,4096]{1,0:T(8,128)(2,1)} %add_convert_fusion.2), channel_id=1, source_target_pairs={{0,8},{4,12},{8,0},{12,4},{16,24},{20,28},{24,16},{28,20},{1,9},{5... | collective-permute-start | bytes 3538952 | tf_op jit(solution)/shard_map/ppermute | solution.py:29
  423.4 25.1 %collective-permute-start.39 = (bf16[128,2048]{1,0:T(8,128)(2,1)S(1)}, bf16[128,2048]{1,0:T(8,128)(2,1)}, u32[]{:S(2)}, u32[]{:S(2)}) collective-permute-start(bf16[128,2048]{1,0:T(8,128)(2,1)S(1)} %pad_maximum_fusion.3), channel_id=1, source_target_pairs={{0,1},{1,0},{2,3},{3,2},{4,5},{5,4},{6,7},{7,6},{8,9},{9,8},{10,11... | collective-permute-start | bytes 1572872 | tf_op jit(solution)/shard_map/ppermute | solution.py:29
  427.5 21.0 %collective-permute-start.38 = (bf16[1,128,1024]{2,1,0:T(8,128)(2,1)S(1)}, bf16[1,128,1024]{2,1,0:T(8,128)(2,1)S(1)}, u32[]{:S(2)}, u32[]{:S(2)}) collective-permute-start(bf16[1,128,1024]{2,1,0:T(8,128)(2,1)S(1)} %slice.250), channel_id=1, source_target_pairs={{0,3},{1,2},{2,1},{3,0},{4,7},{5,6},{6,5},{7,4},{8,11},{9,10},{10,... | collective-permute-start | bytes 786440 | tf_op jit(solution)/shard_map/ppermute | solution.py:29
  452.1 21.5 %collective-permute-start.41 = (bf16[144,2048]{1,0:T(8,128)(2,1)S(1)}, bf16[144,2048]{1,0:T(8,128)(2,1)S(1)}, u32[]{:S(2)}, u32[]{:S(2)}) collective-permute-start(bf16[144,2048]{1,0:T(8,128)(2,1)S(1)} %constant_dynamic-slice_fusion.1), channel_id=1, source_target_pairs={{0,1},{1,0},{2,3},{3,2},{4,5},{5,4},{6,7},{7,6},{8,9},{9,8},{10,11... | collective-permute-start | bytes 1769480 | tf_op jit(solution)/shard_map/ppermute | solution.py:29
  453.5 20.1 %collective-permute-start.40 = (bf16[1,128,1024]{2,1,0:T(8,128)(2,1)S(1)}, bf16[1,128,1024]{2,1,0:T(8,128)(2,1)S(1)}, u32[]{:S(2)}, u32[]{:S(2)}) collective-permute-start(bf16[1,128,1024]{2,1,0:T(8,128)(2,1)S(1)} %slice.251), channel_id=1, source_target_pairs={{0,3},{1,2},{2,1},{3,0},{4,7},{5,6},{6,5},{7,4},{8,11},{9,10},{10,... | collective-permute-start | bytes 786440 | tf_op jit(solution)/shard_map/ppermute | solution.py:29
  (69 other events, 834.3 us)
Sparse Core Ops, SparseCore 0:
  111.0 54.3 all-gather.1
  295.0 50.9 all-reduce.9

commit v2 on v1

--- a/solution.py
+++ b/solution.py
@@ -46,13 +46,13 @@
 def gather_far(near):
     if not near:
         return ()
-    half = near[0].shape[1] // 2
-    return swap(near[0][:, :half], "dp", 4), swap(near[1][:, half:], "dp", 2)
+    cut = near[0].shape[0] // 32 * 16
+    return swap(near[0][:cut], "dp", 4), swap(near[1][cut:], "dp", 2)
 
 
 def gather_stack(own, near, far):
     if near:
-        return jnp.stack([own, near[0], near[1], jnp.concatenate(far, axis=1)])
+        return jnp.stack([own, near[0], near[1], jnp.concatenate(far, axis=0)])
     mine = own[None]
     bit = 2
     while bit < lax.axis_size("dp"):
@@ -131,12 +131,10 @@
     return lax.dynamic_slice_in_dim(block, (lax.axis_index("ctx") ^ j) * per, per, axis=axis)
 
 
-def put_slots(pieces, per, dtype):
-    n = lax.axis_size("ctx")
-    out = jnp.zeros((n * per,) + pieces[0][2].shape[1:], dtype)
+def put_slots(pieces, per, out):
     for j, first, piece in pieces:
         start = (lax.axis_index("ctx") ^ j) * per + first
-        out = lax.dynamic_update_slice_in_dim(out, piece.astype(dtype), start, axis=0)
+        out = lax.dynamic_update_slice_in_dim(out, piece.astype(out.dtype), start, axis=0)
     return out
 
 
@@ -528,6 +526,30 @@
         name="attend_back",
     )(meta, shaped, shaped, shaped, grad.reshape(per, seq, width), mixed.reshape(per, seq, width), lse)
     return out.reshape(3, per * seq, count * lanes), sums
+
+
+def line_kernel(*refs):
+    one, two, *eights, out = refs
+    part = one.shape[-1]
+    pos = 0
+    for c in (0, 2):
+        for ref in (one, two):
+            out[:, pos : pos + part] = jnp.sum(jnp.sum(ref[c], axis=0), axis=0, keepdims=True).astype(out.dtype)
+            pos += part
+    for ref in eights:
+        width = ref.shape[1]
+        out[:, pos : pos + width] = jnp.sum(ref[...], axis=0, keepdims=True).astype(out.dtype)
+        pos += width
+
+
+def one_line(one, two, eights, dtype):
+    total = 4 * one.shape[-1] + sum(b.shape[1] for b in eights)
+    return pl.pallas_call(
+        line_kernel,
+        out_shape=jax.ShapeDtypeStruct((1, total), dtype),
+        compiler_params=pltpu.CompilerParams(vmem_limit_bytes=16 * MIB),
+        name="line",
+    )(one, two, *eights)[0]
 
 
 def weight_grad(name, meta, odd, lefts, rights, chunk, come=None, extra=None):
@@ -683,14 +705,17 @@
     x = jnp.swapaxes(to_sequences(shared), 0, 1).reshape(rows, width)
     qkv_near = gather_near(qkv_own)
     mid_near = gather_near(mid_own)
-    x, qkv_near, mid_near, cotangent = sync(x, qkv_near, mid_near, cotangent)
+    cot_parts = [part_of(cotangent, j) for j in range(n)]
+    blank = jnp.zeros((seqs, blk, width), BF)
+    x, qkv_near, mid_near, cot_parts, blank, meta = sync(x, qkv_near, mid_near, cot_parts, blank, meta)
     qkv_far = gather_far(qkv_near)
     qkv_mine = gather_stack(qkv_own, qkv_near, qkv_far)
     qkv_other = swap(qkv_mine, "dp", 1)
     mid_far = gather_far(mid_near)
-    cot_1 = trade(part_of(cotangent, 1), 1)
-
-    both = jnp.concatenate([qkv_mine[:, thin, :count], qkv_other[:, thin, :count]])
+    cot_1 = trade(cot_parts[1], 1)
+
+    lines = qkv_mine[:, thin, :count]
+    both = jnp.concatenate([lines, swap(lines, "dp", 1)])
     index = jnp.arange(ndp, dtype=jnp.int32) ^ me
     packed = jnp.take(both, (index >> 1) + (index & 1) * (ndp // 2), axis=0).astype(F32)
     fulls, pos = [], 0
@@ -702,11 +727,11 @@
 
     qkv_w = (qkv_mine, qkv_other, thin, 0, 3 * width, 3)
     (proj,) = dense(qkv_body, "qkv", meta, rows, tile, [x], [bqkv], [qkv_w], [(3 * width, BF)], [])
-    proj, mid_far, cot_1, w_down, cotangent = sync(proj, mid_far, cot_1, w_down, cotangent)
+    proj, mid_far, cot_1, w_down, cot_parts = sync(proj, mid_far, cot_1, w_down, cot_parts)
     mid_mine = gather_stack(mid_own, mid_near, mid_far)
     mid_other = swap(mid_mine, "dp", 1)
     down_all = lax.all_gather(w_down, "dp", axis=0, tiled=True)
-    cot_2 = trade(part_of(cotangent, 2), 2)
+    cot_2 = trade(cot_parts[2], 2)
     mixed, lse = attend(meta, proj, per, n * blk)
     mixed, mid_other, cot_2 = sync(mixed, mid_other, cot_2)
     out_w = (mid_mine, mid_other, thin, 0, width, 2)
@@ -714,12 +739,12 @@
     normed_one, inverse_one, first_low = dense(
         out_body, "out", meta, rows, tile, [mixed, x], [bout, gone, sone], [out_w], [(width, F32), (128, F32), (width, BF)], []
     )
-    first_low, cotangent = sync(first_low, cotangent)
-    cot_3 = trade(part_of(cotangent, 3), 3)
+    first_low, cot_parts = sync(first_low, cot_parts)
+    cot_3 = trade(cot_parts[3], 3)
     active, deriv = dense(up_body, "up", meta, rows, tile, [first_low], [bup], [up_w], [(ff, BF), (ff, BF)], [])
     active, down_all, cot_3 = sync(active, down_all, cot_3)
     down_w = (down_all.reshape(8, ff // 8, width), None, ff // 8, 0, width, 0)
-    cot = put_positions([(0, 0, part_of(cotangent, 0)), (1, 0, cot_1), (2, 0, cot_2), (3, 0, cot_3)], per).reshape(rows, width)
+    cot = put_positions([(0, 0, cot_parts[0]), (1, 0, cot_1), (2, 0, cot_2), (3, 0, cot_3)], per).reshape(rows, width)
     out_parts, sum_two, second, s_gtwo, s_stwo, s_bdown = dense(
         functools.partial(down_body, n * blk, per), "down", meta, rows, tile, [active, normed_one, cot],
         [bdown, gone, sone, gtwo, stwo], [down_w], [(width, BF), (width, F32), (width, BF)], [width] * 3,
@@ -757,7 +782,7 @@
         [(width, F32), (width, BF), (width, BF)], [width] * 3,
     )
     branch, g_mixed, come, d_near, out_3 = sync(branch, g_mixed, come, d_near, out_3)
-    output = put_slots([(0, 0, out_own), (1, 0, out_1), (2, 0, out_2), (2, cut, out_2b), (3, 0, out_3)], per, BF)
+    output = put_slots([(0, 0, out_own), (1, 0, out_1), (2, 0, out_2), (2, cut, out_2b), (3, 0, out_3)], per, blank)
     u_far = ()
     if tuned:
         d_share = add_low(d_sums[0], *d_near)
@@ -772,12 +797,11 @@
         u_near = send_near(u_sums, u_far)
     p_two, s_two = attend_back(meta, proj, g_mixed, mixed, lse, per, n * blk, half, half)
     if tuned:
-        p_two, u_near, g_down = sync(p_two, u_near, g_down)
+        p_two, u_near = sync(p_two, u_near)
 
     eights = (s_bout, s_gone, s_sone, s_bup, s_bdown, s_gtwo, s_stwo)
     p_two, s_one, s_two, eights = sync(p_two, s_one, s_two, eights)
-    heads = jnp.sum(jnp.concatenate([s_one, s_two], axis=3), axis=(1, 2))
-    vec = jnp.concatenate([heads[0], heads[2], jnp.sum(jnp.concatenate(eights, axis=1), axis=0)])
+    vec = one_line(s_one, s_two, eights, BF if tuned else F32)
     places, pos = [], 0
     for size in sizes:
         places.append(vec[pos : pos + ndp * size])
@@ -793,7 +817,7 @@
         products = ([x, mixed], [[(p_one, p_two)], [branch]])
         (away,) = weight_grad("gb_away", meta, 1, *products, 1024, extra=extra)
         sum_one = after(sum_one, away)
-        away, u_come = sync(away, u_come)
+        away, u_come, g_down = sync(away, u_come, g_down)
         come = swap(away, "dp", 1)
         u_keep, u_away = halves_ctx(add_low(u_keep, u_come), 2)
         u_come = swap(u_away, "ctx", 2)
@@ -827,12 +851,16 @@
         b_come, in_3b = sync(b_come, in_3b)
         b_half = add_low(b_keep, b_come)
         g_up = join_ctx(u_whole, u_other, 1)
-        total = whole_ctx(whole_ctx(halve_ctx(b_half, 2), 2), 1).astype(F32)
-        g_qkv = total[:thin, : 3 * width]
-        g_out = total[:thin, 3 * width :]
+        b_half = whole_ctx(halve_ctx(b_half, 2), 2)
+        b_other = swap(b_half, "ctx", 1)
+        low = place % 2 == 0
+        left = jnp.where(low, b_half, b_other).astype(F32)
+        right = jnp.where(low, b_other, b_half).astype(F32)
+        g_qkv = jnp.concatenate([left[:thin], right[:thin, :width]], axis=1)
+        g_out = right[:thin, width:]
         g_up = g_up.astype(F32)
         g_down = g_down.astype(F32)
-        vec = total[thin, :count]
+        vec = left[thin, :count]
     else:
         def whole(*products):
             return jnp.concatenate([tn(a, b).astype(BF) for a, b in products], axis=1)
@@ -850,7 +878,7 @@
         grads.append(vec[pos : pos + size])
         pos += size
     g_bqv, g_bout, g_gone, g_sone, g_bup, g_bdown, g_gtwo, g_stwo = grads
-    grad_input = put_slots([(0, 0, part_of(grad_in, 0, 1)), (1, 0, in_1)] + in_rest, per, F32)
+    grad_input = put_slots([(0, 0, part_of(grad_in, 0, 1)), (1, 0, in_1)] + in_rest, per, jnp.zeros((seqs, blk, width), F32))
     return (
         output, grad_input, g_qkv, g_bqv, g_out, g_bout, g_gone, g_sone, g_up, g_bup, g_down, g_bdown, g_gtwo, g_stwo,
     )

time: 534 us -> 527 us (0.987)
  waiting for transfers between devices: 149 us -> 136 us
  starting transfers between devices: 52.6 us -> 58.5 us
    ppermute x45 -> x46, waiting for transfers between devices: 109 us -> 101 us  [swap(): return lax.ppermute(x, axis, [(i, i ^ bit) for i in range(n)])]
    ppermute x45 -> x46, starting transfers between devices: 45.8 us -> 51.9 us  [swap(): return lax.ppermute(x, axis, [(i, i ^ bit) for i in range(n)])]
  transfers between devices with their start and end apart: 48 -> 49, of which waited for: 21 -> 25; matrix products, arithmetic and copies ran while one was open for 10% -> 11% of each run, Pallas kernels for 38% -> 37%
where the time goes in v2:
time: 527 us; the launch traced here: 518 us
  Pallas kernels  232 us (44%)
  waiting for transfers between devices  136 us (26%)
  starting transfers between devices  58.5 us (11%)
  local copies, waits for them, and re-layouts  40.4 us (8%)
  other arithmetic  36.8 us (7%)
  between operations  15.5 us (3%)
    ppermute x46, waiting for transfers between devices, swap(): return lax.ppermute(x, axis, [(i, i ^ bit) for i in range(n)])  101 us
    pallas_call x6, Pallas kernels, dense(): pl.pallas_call(kernel, grid_spec=pltpu.PrefetchScalarGridSpec(num_scalar_...  99.6 us
    pallas_call x6, Pallas kernels, weight_grad(): pl.pallas_call(kernel, grid_spec=pltpu.PrefetchScalarGridSpec(num_scalar_...  62.9 us
    ppermute x46, starting transfers between devices, swap(): return lax.ppermute(x, axis, [(i, i ^ bit) for i in range(n)])  51.9 us
    all_to_all x1, waiting for transfers between devices, to_sequences(): return lax.all_to_all(block, 'ctx', 0, 0, tiled=True)  34.4 us
    pallas_call x2, Pallas kernels, attend_back(): pl.pallas_call(attend_back_kernel, grid_spec=pltpu.PrefetchScalarGridSpec...  33.5 us
    pallas_call x1, Pallas kernels, attend(): pl.pallas_call(attend_kernel, grid_spec=pltpu.PrefetchScalarGridSpec(num_...  20.4 us
    convert_element_type x13, other arithmetic, add_low(): return total.astype(BF)  15.2 us
  transfers between devices with their start and end apart: 49, of which 25 were waited for; matrix products, arithmetic and copies ran while one was open for 11% of the time, Pallas kernels for 37%

profile of v2, /device:TPU:0, one launch (start us, length us, event | category | flops | bytes accessed | tf_op | source)
XLA Modules:
  0.0 518.5 jit_solution(6245266169295005475)
XLA Ops:
  27.4 34.4 %all-to-all-done = bf16[4,2,128,1024]{3,2,1,0:T(8,128)(2,1)S(1)} async-done(((bf16[4,2,128,1024]{3,2,1,0:T(8,128)(2,1)}), bf16[4,2,128,1024]{3,2,1,0:T(8,128)(2,1)S(1)}, u32[]{:S(2)}, u32[]{:S(2)}) %all-to-all-start) | async-done | bytes 2097184 | tf_op jit(solution)/shard_map/all_to_all | solution.py:125
  70.9 7.6 %collective-permute-done.4 = bf16[64,3072]{1,0:T(8,128)(2,1)S(1)} collective-permute-done((bf16[64,3072]{1,0:T(8,128)(2,1)S(1)}, bf16[64,3072]{1,0:T(8,128)(2,1)S(1)}, u32[]{:S(2)}, u32[]{:S(2)}) %collective-permute-start.4) | collective-permute-done | bytes 393248 | tf_op jit(solution)/shard_map/ppermute | solution.py:29
  94.0 12.3 %qkv.1 = bf16[1024,3072]{1,0:T(8,128)(2,1)} custom-call(s32[4]{0:T(128)} %pad_add_fusion.meta_ref.meta, bf16[1024,1024]{1,0:T(8,128)(2,1)} %bitcast.74, f32[1,3072]{1,0:T(1,128)} %pad_maximum_fusion.6.refs_1_, bf16[4,144,3072]{2,1,0:T(8,128)(2,1)} %copy-done.10, bf16[4,144,3072]{2,1,0:T(8,128)(2,1)} %collective-permute-done.7.refs_3_.refs_4_), custom_call_target="tpu_custom_call" | custom-call | flops 12999999488 | bytes 1000000 | tf_op jit(solution)/shard_map/qkv/pallas_call | solution.py:265
  116.5 20.4 %attend.1 = (bf16[2,512,1024]{2,1,0:T(8,128)(2,1)}, f32[2,4,4,512]{3,2,1,0:T(4,128)}) custom-call(s32[4]{0:T(128)} %pad_add_fusion.meta_ref.meta, bf16[2,512,3072]{2,1,0:T(8,128)(2,1)} %bitcast.129, bf16[2,512,3072]{2,1,0:T(8,128)(2,1)} %bitcast.130, bf16[2,512,3072]{2,1,0:T(8,128)(2,1)} %bitcast.131), custom_call_target="tpu_custom_call" | custom-call | flops 24000000000 | bytes 1000000 | tf_op jit(solution)/shard_map/attend/pallas_call | solution.py:480
  140.6 10.0 %out.1 = (f32[1024,1024]{1,0:T(8,128)}, f32[1024,128]{1,0:T(8,128)}, bf16[1024,1024]{1,0:T(8,128)(2,1)}) custom-call(s32[4]{0:T(128)} %pad_add_fusion.meta_ref.meta, bf16[1024,1024]{1,0:T(8,128)(2,1)} %bitcast.84, bf16[1024,1024]{1,0:T(8,128)(2,1)} %bitcast.75, f32[1,1024]{1,0:T(1,128)} %bitcast.125, f32[1,1024]{1,0:T(1,128)} %bitcast.117, ...), custom_call_target="tpu_custom_call" | custom-call | flops 10000000000 | bytes 1000000 | tf_op jit(solution)/shard_map/out/pallas_call | solution.py:265
  152.9 22.5 %up.1 = (bf16[1024,4096]{1,0:T(8,128)(2,1)}, bf16[1024,4096]{1,0:T(8,128)(2,1)}) custom-call(s32[4]{0:T(128)} %pad_add_fusion.meta_ref.meta, bf16[1024,1024]{1,0:T(8,128)(2,1)} %get-tuple-element.174.refs_0_.refs_1_.refs_2_.refs_3_, f32[1,4096]{1,0:T(1,128)} %bitcast.116, bf16[4,128,5120]{2,1,0:T(8,128)(2,1)} %pad_maximum_fusion.refs_5_.refs_2_.refs_7_, ...), custom_call_target="tpu_custom_call" | custom-call | flops 23000000512 | bytes 1000000 | tf_op jit(solution)/shard_map/up/pallas_call | solution.py:265
  179.0 20.3 %down.1 = (bf16[1024,1024]{1,0:T(8,128)(2,1)}, f32[1024,1024]{1,0:T(8,128)}, bf16[1024,1024]{1,0:T(8,128)(2,1)}, f32[8,1024]{1,0:T(8,128)}, f32[8,1024]{1,0:T(8,128)}, /*index=5*/f32[8,1024]{1,0:T(8,128)}) custom-call(s32[4]{0:T(128)} %pad_add_fusion.meta_ref.meta, bf16[1024,4096]{1,0:T(8,128)(2,1)} %get-tuple-element.178.refs_0_.refs_1_.refs_2_.refs_3_, ...), custom_call_target="tpu_custom_call" | custom-call | flops 20999999488 | bytes 1000000 | tf_op jit(solution)/shard_map/down/pallas_call | solution.py:265
  199.3 9.3 %gd_away.1 = bf16[4,512,1024]{2,1,0:T(8,128)(2,1)} custom-call(s32[4]{0:T(128)} %pad_add_fusion.meta_ref.meta, bf16[1024,4096]{1,0:T(8,128)(2,1)} %get-tuple-element.178.refs_0_.refs_1_.refs_2_.refs_3_, bf16[1024,4096]{1,0:T(8,128)(2,1)} %get-tuple-element.178.refs_0_.refs_1_.refs_2_.refs_3_, ...), custom_call_target="tpu_custom_call" | custom-call | flops 11000000512 | bytes 1000000 | tf_op jit(solution)/shard_map/gd_away/pallas_call | solution.py:662
  211.9 15.0 %hidden.1 = (bf16[1024,4096]{1,0:T(8,128)(2,1)}, f32[8,4096]{1,0:T(8,128)}) custom-call(bf16[1024,1024]{1,0:T(8,128)(2,1)} %get-tuple-element.187.refs_4_.second, bf16[4096,1024]{1,0:T(8,128)(2,1)} %all-gather.2.cloned.1.call-done.whole, bf16[1024,4096]{1,0:T(8,128)(2,1)} %get-tuple-element.188.deriv), custom_call_target="tpu_custom_call" | custom-call | flops 17999998976 | bytes 1000000 | tf_op jit(solution)/shard_map/hidden/pallas_call | solution.py:382
  229.2 10.5 %gd_keep.1 = (bf16[512,1024]{1,0:T(8,128)(2,1)}, bf16[512,1024]{1,0:T(8,128)(2,1)}, bf16[512,1024]{1,0:T(8,128)(2,1)}, bf16[512,512]{1,0:T(8,128)(2,1)}, bf16[512,512]{1,0:T(8,128)(2,1)}) custom-call(s32[4]{0:T(128)} %pad_add_fusion.meta_ref.meta, bf16[1024,4096]{1,0:T(8,128)(2,1)} %get-tuple-element.178.refs_0_.refs_1_.refs_2_.refs_3_, ...), custom_call_target="tpu_custom_call" | custom-call | flops 11000000512 | bytes 1000000 | tf_op jit(solution)/shard_map/gd_keep/pallas_call | solution.py:662
  243.3 9.6 %gu_away.1 = bf16[4,128,4096]{2,1,0:T(8,128)(2,1)} custom-call(s32[4]{0:T(128)} %pad_add_fusion.meta_ref.meta, bf16[1024,1024]{1,0:T(8,128)(2,1)} %get-tuple-element.174.refs_0_.refs_1_.refs_2_.refs_3_, bf16[1024,1024]{1,0:T(8,128)(2,1)} %get-tuple-element.174.refs_0_.refs_1_.refs_2_.refs_3_, ...), custom_call_target="tpu_custom_call" | custom-call | flops 11000000512 | bytes 1000000 | tf_op jit(solution)/shard_map/gu_away/pallas_call | solution.py:662
  265.7 21.4 %first.1 = (f32[1024,1024]{1,0:T(8,128)}, bf16[1024,1024]{1,0:T(8,128)(2,1)}, bf16[1024,1024]{1,0:T(8,128)(2,1)}, f32[8,1024]{1,0:T(8,128)}, f32[8,1024]{1,0:T(8,128)}, /*index=5*/f32[8,1024]{1,0:T(8,128)}) custom-call(s32[4]{0:T(128)} %pad_add_fusion.meta_ref.meta, bf16[1024,4096]{1,0:T(8,128)(2,1)} %get-tuple-element.206.refs_4_.refs_0_, ...), custom_call_target="tpu_custom_call" | custom-call | flops 23000000512 | bytes 1000000 | tf_op jit(solution)/shard_map/first/pallas_call | solution.py:265
  287.9 10.4 %gu_keep.1 = (bf16[128,4096]{1,0:T(8,128)(2,1)}, bf16[128,4096]{1,0:T(8,128)(2,1)}, bf16[128,4096]{1,0:T(8,128)(2,1)}, bf16[128,2048]{1,0:T(8,128)(2,1)}, bf16[128,2048]{1,0:T(8,128)(2,1)}) custom-call(s32[4]{0:T(128)} %pad_add_fusion.meta_ref.meta, bf16[1024,1024]{1,0:T(8,128)(2,1)} %get-tuple-element.174.refs_0_.refs_1_.refs_2_.refs_3_, ...), custom_call_target="tpu_custom_call" | custom-call | flops 11000000512 | bytes 1000000 | tf_op jit(solution)/shard_map/gu_keep/pallas_call | solution.py:662
  303.0 16.8 %attend_back.2 = (bf16[3,2,512,512]{3,2,1,0:T(8,128)(2,1)}, f32[3,2,8,512]{3,2,1,0:T(8,128)}) custom-call(s32[4]{0:T(128)} %pad_add_fusion.meta_ref.meta, bf16[2,512,3072]{2,1,0:T(8,128)(2,1)} %bitcast.132, bf16[2,512,3072]{2,1,0:T(8,128)(2,1)} %bitcast.133, bf16[2,512,3072]{2,1,0:T(8,128)(2,1)} %bitcast.134, bf16[2,512,1024]{2,1,0:T(8,128)(2,1)} %bitcast.138, ...), custom_call_target="tpu_custom_call" | custom-call | flops 20999999488 | bytes 1000000 | tf_op jit(solution)/shard_map/attend_back/pallas_call | solution.py:508
  323.6 16.7 %attend_back.3 = (bf16[3,2,512,512]{3,2,1,0:T(8,128)(2,1)}, f32[3,2,8,512]{3,2,1,0:T(8,128)}) custom-call(s32[4]{0:T(128)} %pad_add_fusion.meta_ref.meta, bf16[2,512,3072]{2,1,0:T(8,128)(2,1)} %bitcast.135, bf16[2,512,3072]{2,1,0:T(8,128)(2,1)} %bitcast.136, bf16[2,512,3072]{2,1,0:T(8,128)(2,1)} %bitcast.137, bf16[2,512,1024]{2,1,0:T(8,128)(2,1)} %bitcast.139, ...), custom_call_target="tpu_custom_call" | custom-call | flops 20999999488 | bytes 1000000 | tf_op jit(solution)/shard_map/attend_back/pallas_call | solution.py:508
  351.7 11.1 %gb_away.1 = bf16[4,144,4096]{2,1,0:T(8,128)(2,1)} custom-call(s32[4]{0:T(128)} %pad_add_fusion.meta_ref.meta, bf16[1024,1024]{1,0:T(8,128)(2,1)} %bitcast.76, bf16[1024,1024]{1,0:T(8,128)(2,1)} %bitcast.77, bf16[1024,1024]{1,0:T(8,128)(2,1)} %bitcast.78, bf16[1024,1024]{1,0:T(8,128)(2,1)} %bitcast.79, bf16[1024,1024]{1,0:T(8,128)(2,1)} %bitcast.85, ...), custom_call_target="tpu_custom_call" | custom-call | flops 14000000000 | bytes 1000000 | tf_op jit(solution)/shard_map/gb_away/pallas_call | solution.py:662
  366.4 13.2 %input.1 = bf16[1024,1024]{1,0:T(8,128)(2,1)} custom-call(s32[4]{0:T(128)} %pad_add_fusion.meta_ref.meta, bf16[3,1024,512]{2,1,0:T(8,128)(2,1)} %bitcast.95, bf16[3,1024,512]{2,1,0:T(8,128)(2,1)} %bitcast.98, f32[1024,1024]{1,0:T(8,128)} %get-tuple-element.255.refs_2_, bf16[4,144,3072]{2,1,0:T(8,128)(2,1)} %copy-done.10, ...), custom_call_target="tpu_custom_call" | custom-call | flops 14000000000 | bytes 1000000 | tf_op jit(solution)/shard_map/input/pallas_call | solution.py:265
  383.4 12.0 %gb_keep.1 = (bf16[144,4096]{1,0:T(8,128)(2,1)}, bf16[144,4096]{1,0:T(8,128)(2,1)}, bf16[144,4096]{1,0:T(8,128)(2,1)}, bf16[144,2048]{1,0:T(8,128)(2,1)}, bf16[144,2048]{1,0:T(8,128)(2,1)}) custom-call(s32[4]{0:T(128)} %pad_add_fusion.meta_ref.meta, bf16[1024,1024]{1,0:T(8,128)(2,1)} %bitcast.80, bf16[1024,1024]{1,0:T(8,128)(2,1)} %bitcast.81, ...), custom_call_target="tpu_custom_call" | custom-call | flops 3000000000 | bytes 1000000 | tf_op jit(solution)/shard_map/gb_keep/pallas_call | solution.py:662
  406.9 10.1 %collective-permute-done.35 = bf16[1,128,1024]{2,1,0:T(8,128)(2,1)S(1)} collective-permute-done((bf16[1,128,1024]{2,1,0:T(8,128)(2,1)S(1)}, bf16[1,128,1024]{2,1,0:T(8,128)(2,1)S(1)}, u32[]{:S(2)}, u32[]{:S(2)}) %collective-permute-start.35) | collective-permute-done | bytes 262176 | tf_op jit(solution)/shard_map/ppermute | solution.py:29
  431.7 8.0 %collective-permute-done.38 = bf16[1,128,1024]{2,1,0:T(8,128)(2,1)S(1)} collective-permute-done((bf16[1,128,1024]{2,1,0:T(8,128)(2,1)S(1)}, bf16[1,128,1024]{2,1,0:T(8,128)(2,1)S(1)}, u32[]{:S(2)}, u32[]{:S(2)}) %collective-permute-start.38) | collective-permute-done | bytes 262176 | tf_op jit(solution)/shard_map/ppermute | solution.py:29
  452.9 16.2 %collective-permute-done.41 = bf16[1,128,1024]{2,1,0:T(8,128)(2,1)S(1)} collective-permute-done((bf16[1,128,1024]{2,1,0:T(8,128)(2,1)S(1)}, bf16[1,128,1024]{2,1,0:T(8,128)(2,1)S(1)}, u32[]{:S(2)}, u32[]{:S(2)}) %collective-permute-start.41) | collective-permute-done | bytes 262176 | tf_op jit(solution)/shard_map/ppermute | solution.py:29
  473.0 9.0 %collective-permute-done.43 = bf16[144,1024]{1,0:T(8,128)(2,1)S(1)} collective-permute-done((bf16[144,1024]{1,0:T(8,128)(2,1)S(1)}, bf16[144,1024]{1,0:T(8,128)(2,1)S(1)}, u32[]{:S(2)}, u32[]{:S(2)}) %collective-permute-start.43) | collective-permute-done | bytes 294944 | tf_op jit(solution)/shard_map/ppermute | solution.py:29
  483.7 8.6 %collective-permute-done.44 = bf16[144,1024]{1,0:T(8,128)(2,1)S(1)} collective-permute-done((bf16[144,1024]{1,0:T(8,128)(2,1)S(1)}, bf16[144,1024]{1,0:T(8,128)(2,1)S(1)}, u32[]{:S(2)}, u32[]{:S(2)}) %collective-permute-start.44) | collective-permute-done | bytes 294944 | tf_op jit(solution)/shard_map/ppermute | solution.py:29
  498.5 8.5 %collective-permute-done.45 = bf16[144,2048]{1,0:T(8,128)(2,1)S(1)} collective-permute-done((bf16[144,2048]{1,0:T(8,128)(2,1)S(1)}, bf16[144,2048]{1,0:T(8,128)(2,1)S(1)}, u32[]{:S(2)}, u32[]{:S(2)}) %collective-permute-start.45) | collective-permute-done | bytes 589856 | tf_op jit(solution)/shard_map/ppermute | solution.py:29
  (310 shorter events, 169.1 us)
Async XLA Ops:
  7.2 54.7 %all-to-all-start = ((bf16[4,2,128,1024]{3,2,1,0:T(8,128)(2,1)}), bf16[4,2,128,1024]{3,2,1,0:T(8,128)(2,1)S(1)}, u32[]{:S(2)}, u32[]{:S(2)}) async-start(bf16[4,2,128,1024]{3,2,1,0:T(8,128)(2,1)} %bitcast.110), calls=%async_computation | async-start | bytes 4194304 | tf_op jit(solution)/shard_map/all_to_all | solution.py:125
  13.7 163.9 %all-gather.2.cloned.1.call-start = ((), (), s32[]{:S(2)}) async-start(), calls=%async_computation.1 | async-start | bytes 9437184 | tf_op jit(solution)/shard_map/all_gather | solution.py:733
  15.6 50.7 %collective-permute-start.2 = (bf16[128,5120]{1,0:T(8,128)(2,1)}, bf16[128,5120]{1,0:T(8,128)(2,1)S(1)}, u32[]{:S(2)}, u32[]{:S(2)}) collective-permute-start(bf16[128,5120]{1,0:T(8,128)(2,1)} %constant_dynamic-update-slice_fusion), channel_id=1, source_target_pairs={{0,8},{4,12},{8,0},{12,4},{16,24},{20,28},{24,16},{28,20},{1,9},{5... | collective-permute-start | bytes 3932168 | tf_op jit(solution)/shard_map/ppermute | solution.py:29
  17.1 49.2 %collective-permute-start.3 = (bf16[128,5120]{1,0:T(8,128)(2,1)}, bf16[128,5120]{1,0:T(8,128)(2,1)}, u32[]{:S(2)}, u32[]{:S(2)}) collective-permute-start(bf16[128,5120]{1,0:T(8,128)(2,1)} %constant_dynamic-update-slice_fusion), channel_id=1, source_target_pairs={{0,16},{4,20},{8,24},{12,28},{16,0},{20,4},{24,8},{28,12},{1,17},{... | collective-permute-start | bytes 3932168 | tf_op jit(solution)/shard_map/ppermute | solution.py:29
  22.8 42.3 %collective-permute-start = (bf16[144,3072]{1,0:T(8,128)(2,1)}, bf16[144,3072]{1,0:T(8,128)(2,1)}, u32[]{:S(2)}, u32[]{:S(2)}) collective-permute-start(bf16[144,3072]{1,0:T(8,128)(2,1)} %get-tuple-element.319), channel_id=1, source_target_pairs={{0,8},{4,12},{8,0},{12,4},{16,24},{20,28},{24,16},{28,20},{1,9},{5... | collective-permute-start | bytes 2654216 | tf_op jit(solution)/shard_map/ppermute | solution.py:29
  23.3 42.9 %collective-permute-start.1 = (bf16[144,3072]{1,0:T(8,128)(2,1)}, bf16[144,3072]{1,0:T(8,128)(2,1)}, u32[]{:S(2)}, u32[]{:S(2)}) collective-permute-start(bf16[144,3072]{1,0:T(8,128)(2,1)} %get-tuple-element.319), channel_id=1, source_target_pairs={{0,16},{4,20},{8,24},{12,28},{16,0},{20,4},{24,8},{28,12},{1,17},{... | collective-permute-start | bytes 2654216 | tf_op jit(solution)/shard_map/ppermute | solution.py:29
  83.7 22.6 %collective-permute-start.8 = (bf16[64,5120]{1,0:T(8,128)(2,1)}, bf16[64,5120]{1,0:T(8,128)(2,1)}, u32[]{:S(2)}, u32[]{:S(2)}) collective-permute-start(bf16[64,5120]{1,0:T(8,128)(2,1)} %slice.167), channel_id=1, source_target_pairs={{0,16},{4,20},{8,24},{12,28},{16,0},{20,4},{24,8},{28,12},{1,17},{... | collective-permute-start | bytes 1966088 | tf_op jit(solution)/shard_map/ppermute | solution.py:29
  106.3 256.4 %all-reduce.10.cloned.1.call-start = ((), (), s32[]{:S(2)}) async-start(), calls=%async_computation.2 | async-start | bytes 2097152 | tf_op jit(solution)/shard_map/psum | solution.py:789
  112.9 27.7 %collective-permute-start.11 = (bf16[4,128,5120]{2,1,0:T(8,128)(2,1)}, bf16[4,128,5120]{2,1,0:T(8,128)(2,1)}, u32[]{:S(2)}, u32[]{:S(2)}) collective-permute-start(bf16[4,128,5120]{2,1,0:T(8,128)(2,1)} %pad_maximum_fusion.refs_5_.refs_2_.refs_7_), channel_id=1, source_target_pairs={{0,4},{4,0},{8,12},{12,8},{16,20},{20,16},{24,28},{28,24},{1,5},{5... | collective-permute-start | bytes 15728648 | tf_op jit(solution)/shard_map/ppermute | solution.py:29
  114.1 26.5 %collective-permute-start.12 = (bf16[2,128,1024]{2,1,0:T(8,128)(2,1)S(1)}, bf16[2,128,1024]{2,1,0:T(8,128)(2,1)S(1)}, u32[]{:S(2)}, u32[]{:S(2)}) collective-permute-start(bf16[2,128,1024]{2,1,0:T(8,128)(2,1)S(1)} %copy-done.35), channel_id=1, source_target_pairs={{0,2},{1,3},{2,0},{3,1},{4,6},{5,7},{6,4},{7,5},{8,10},{9,11},{10,... | collective-permute-start | bytes 1572872 | tf_op jit(solution)/shard_map/ppermute | solution.py:29
  150.6 27.0 %collective-permute-start.13 = (bf16[2,128,1024]{2,1,0:T(8,128)(2,1)S(1)}, bf16[2,128,1024]{2,1,0:T(8,128)(2,1)S(1)}, u32[]{:S(2)}, u32[]{:S(2)}) collective-permute-start(bf16[2,128,1024]{2,1,0:T(8,128)(2,1)S(1)} %copy-done.34), channel_id=1, source_target_pairs={{0,3},{1,2},{2,1},{3,0},{4,7},{5,6},{6,5},{7,4},{8,11},{9,10},{10,... | collective-permute-start | bytes 1572872 | tf_op jit(solution)/shard_map/ppermute | solution.py:29
  255.6 31.5 %collective-permute-start.20 = (bf16[4,128,4096]{2,1,0:T(8,128)(2,1)}, bf16[4,128,4096]{2,1,0:T(8,128)(2,1)}, u32[]{:S(2)}, u32[]{:S(2)}) collective-permute-start(bf16[4,128,4096]{2,1,0:T(8,128)(2,1)} %gu_away.1), channel_id=1, source_target_pairs={{0,4},{4,0},{8,12},{12,8},{16,20},{20,16},{24,28},{28,24},{1,5},{5... | collective-permute-start | bytes 12582920 | tf_op jit(solution)/shard_map/ppermute | solution.py:29
  258.1 29.0 %collective-permute-start.21 = (bf16[512,1024]{1,0:T(8,128)(2,1)}, bf16[512,1024]{1,0:T(8,128)(2,1)}, u32[]{:S(2)}, u32[]{:S(2)}) collective-permute-start(bf16[512,1024]{1,0:T(8,128)(2,1)} %add_convert_fusion.8), channel_id=1, source_target_pairs={{0,8},{4,12},{8,0},{12,4},{16,24},{20,28},{24,16},{28,20},{1,9},{5... | collective-permute-start | bytes 3145736 | tf_op jit(solution)/shard_map/ppermute | solution.py:29
  261.1 26.0 %collective-permute-start.22 = (bf16[512,1024]{1,0:T(8,128)(2,1)}, bf16[512,1024]{1,0:T(8,128)(2,1)S(1)}, u32[]{:S(2)}, u32[]{:S(2)}) collective-permute-start(bf16[512,1024]{1,0:T(8,128)(2,1)} %add_convert_fusion.7), channel_id=1, source_target_pairs={{0,16},{4,20},{8,24},{12,28},{16,0},{20,4},{24,8},{28,12},{1,17},{... | collective-permute-start | bytes 3145736 | tf_op jit(solution)/shard_map/ppermute | solution.py:29
  263.5 23.6 %collective-permute-start.23 = (bf16[2,128,1024]{2,1,0:T(8,128)(2,1)}, bf16[2,128,1024]{2,1,0:T(8,128)(2,1)S(1)}, u32[]{:S(2)}, u32[]{:S(2)}) collective-permute-start(bf16[2,128,1024]{2,1,0:T(8,128)(2,1)} %constant_dynamic-slice_fusion.8), channel_id=1, source_target_pairs={{0,3},{1,2},{2,1},{3,0},{4,7},{5,6},{6,5},{7,4},{8,11},{9,10},{10,... | collective-permute-start | bytes 1572872 | tf_op jit(solution)/shard_map/ppermute | solution.py:29
  298.3 21.6 %collective-permute-start.24 = (bf16[128,2048]{1,0:T(8,128)(2,1)}, bf16[128,2048]{1,0:T(8,128)(2,1)S(1)}, u32[]{:S(2)}, u32[]{:S(2)}) collective-permute-start(bf16[128,2048]{1,0:T(8,128)(2,1)} %get-tuple-element.224), channel_id=1, source_target_pairs={{0,16},{4,20},{8,24},{12,28},{16,0},{20,4},{24,8},{28,12},{1,17},{... | collective-permute-start | bytes 1572872 | tf_op jit(solution)/shard_map/ppermute | solution.py:29
  298.8 21.1 %collective-permute-start.25 = (bf16[128,2048]{1,0:T(8,128)(2,1)}, bf16[128,2048]{1,0:T(8,128)(2,1)S(1)}, u32[]{:S(2)}, u32[]{:S(2)}) collective-permute-start(bf16[128,2048]{1,0:T(8,128)(2,1)} %get-tuple-element.225), channel_id=1, source_target_pairs={{0,8},{4,12},{8,0},{12,4},{16,24},{20,28},{24,16},{28,20},{1,9},{5... | collective-permute-start | bytes 1572872 | tf_op jit(solution)/shard_map/ppermute | solution.py:29
  320.9 24.3 %collective-permute-start.26 = (bf16[128,4096]{1,0:T(8,128)(2,1)S(1)}, bf16[128,4096]{1,0:T(8,128)(2,1)}, u32[]{:S(2)}, u32[]{:S(2)}) collective-permute-start(bf16[128,4096]{1,0:T(8,128)(2,1)S(1)} %add_convert_fusion.6), channel_id=1, source_target_pairs={{0,8},{4,12},{8,0},{12,4},{16,24},{20,28},{24,16},{28,20},{1,9},{5... | collective-permute-start | bytes 3145736 | tf_op jit(solution)/shard_map/ppermute | solution.py:29
  322.0 24.3 %collective-permute-start.27 = (bf16[128,4096]{1,0:T(8,128)(2,1)S(1)}, bf16[128,4096]{1,0:T(8,128)(2,1)}, u32[]{:S(2)}, u32[]{:S(2)}) collective-permute-start(bf16[128,4096]{1,0:T(8,128)(2,1)S(1)} %add_convert_fusion.5), channel_id=1, source_target_pairs={{0,16},{4,20},{8,24},{12,28},{16,0},{20,4},{24,8},{28,12},{1,17},{... | collective-permute-start | bytes 3145736 | tf_op jit(solution)/shard_map/ppermute | solution.py:29
  418.9 28.0 %collective-permute-start.36 = (bf16[144,4096]{1,0:T(8,128)(2,1)}, bf16[144,4096]{1,0:T(8,128)(2,1)}, u32[]{:S(2)}, u32[]{:S(2)}) collective-permute-start(bf16[144,4096]{1,0:T(8,128)(2,1)} %add_convert_fusion.2), channel_id=1, source_target_pairs={{0,8},{4,12},{8,0},{12,4},{16,24},{20,28},{24,16},{28,20},{1,9},{5... | collective-permute-start | bytes 3538952 | tf_op jit(solution)/shard_map/ppermute | solution.py:29
  420.7 27.6 %collective-permute-start.37 = (bf16[144,4096]{1,0:T(8,128)(2,1)}, bf16[144,4096]{1,0:T(8,128)(2,1)}, u32[]{:S(2)}, u32[]{:S(2)}) collective-permute-start(bf16[144,4096]{1,0:T(8,128)(2,1)} %add_convert_fusion.1), channel_id=1, source_target_pairs={{0,16},{4,20},{8,24},{12,28},{16,0},{20,4},{24,8},{28,12},{1,17},{... | collective-permute-start | bytes 3538952 | tf_op jit(solution)/shard_map/ppermute | solution.py:29
  421.2 24.4 %collective-permute-start.40 = (bf16[128,2048]{1,0:T(8,128)(2,1)S(1)}, bf16[128,2048]{1,0:T(8,128)(2,1)}, u32[]{:S(2)}, u32[]{:S(2)}) collective-permute-start(bf16[128,2048]{1,0:T(8,128)(2,1)S(1)} %pad_maximum_fusion.4), channel_id=1, source_target_pairs={{0,1},{1,0},{2,3},{3,2},{4,5},{5,4},{6,7},{7,6},{8,9},{9,8},{10,11... | collective-permute-start | bytes 1572872 | tf_op jit(solution)/shard_map/ppermute | solution.py:29
  423.9 20.8 %collective-permute-start.39 = (bf16[1,128,1024]{2,1,0:T(8,128)(2,1)S(1)}, bf16[1,128,1024]{2,1,0:T(8,128)(2,1)S(1)}, u32[]{:S(2)}, u32[]{:S(2)}) collective-permute-start(bf16[1,128,1024]{2,1,0:T(8,128)(2,1)S(1)} %slice.188), channel_id=1, source_target_pairs={{0,3},{1,2},{2,1},{3,0},{4,7},{5,6},{6,5},{7,4},{8,11},{9,10},{10,... | collective-permute-start | bytes 786440 | tf_op jit(solution)/shard_map/ppermute | solution.py:29
  450.5 21.1 %collective-permute-start.42 = (bf16[144,2048]{1,0:T(8,128)(2,1)S(1)}, bf16[144,2048]{1,0:T(8,128)(2,1)S(1)}, u32[]{:S(2)}, u32[]{:S(2)}) collective-permute-start(bf16[144,2048]{1,0:T(8,128)(2,1)S(1)} %constant_dynamic-slice_fusion.1), channel_id=1, source_target_pairs={{0,1},{1,0},{2,3},{3,2},{4,5},{5,4},{6,7},{7,6},{8,9},{9,8},{10,11... | collective-permute-start | bytes 1769480 | tf_op jit(solution)/shard_map/ppermute | solution.py:29
  (76 other events, 836.7 us)
Sparse Core Ops, SparseCore 0:
  106.5 53.2 all-gather.1
  303.2 50.0 all-reduce.9

commit v3 on v2

--- a/solution.py
+++ b/solution.py
@@ -534,19 +534,19 @@
     pos = 0
     for c in (0, 2):
         for ref in (one, two):
-            out[:, pos : pos + part] = jnp.sum(jnp.sum(ref[c], axis=0), axis=0, keepdims=True).astype(out.dtype)
+            out[:, pos : pos + part] = jnp.sum(jnp.sum(ref[c], axis=0), axis=0, keepdims=True)
             pos += part
     for ref in eights:
         width = ref.shape[1]
-        out[:, pos : pos + width] = jnp.sum(ref[...], axis=0, keepdims=True).astype(out.dtype)
+        out[:, pos : pos + width] = jnp.sum(ref[...], axis=0, keepdims=True)
         pos += width
 
 
-def one_line(one, two, eights, dtype):
+def one_line(one, two, eights):
     total = 4 * one.shape[-1] + sum(b.shape[1] for b in eights)
     return pl.pallas_call(
         line_kernel,
-        out_shape=jax.ShapeDtypeStruct((1, total), dtype),
+        out_shape=jax.ShapeDtypeStruct((1, total), F32),
         compiler_params=pltpu.CompilerParams(vmem_limit_bytes=16 * MIB),
         name="line",
     )(one, two, *eights)[0]
@@ -801,7 +801,7 @@
 
     eights = (s_bout, s_gone, s_sone, s_bup, s_bdown, s_gtwo, s_stwo)
     p_two, s_one, s_two, eights = sync(p_two, s_one, s_two, eights)
-    vec = one_line(s_one, s_two, eights, BF if tuned else F32)
+    vec = one_line(s_one, s_two, eights)
     places, pos = [], 0
     for size in sizes:
         places.append(vec[pos : pos + ndp * size])

time: 527 us -> 527 us (level)
  no operation moved by 1% of the time
where the time goes in v3:
time: 527 us; the launch traced here: 519 us
  Pallas kernels  231 us (44%)
  waiting for transfers between devices  138 us (26%)
  starting transfers between devices  57.6 us (11%)
  local copies, waits for them, and re-layouts  40.3 us (8%)
  other arithmetic  36.8 us (7%)
  between operations  15.5 us (3%)
    ppermute x46, waiting for transfers between devices, swap(): return lax.ppermute(x, axis, [(i, i ^ bit) for i in range(n)])  103 us
    pallas_call x6, Pallas kernels, dense(): pl.pallas_call(kernel, grid_spec=pltpu.PrefetchScalarGridSpec(num_scalar_...  99.4 us
    pallas_call x6, Pallas kernels, weight_grad(): pl.pallas_call(kernel, grid_spec=pltpu.PrefetchScalarGridSpec(num_scalar_...  62.8 us
    ppermute x46, starting transfers between devices, swap(): return lax.ppermute(x, axis, [(i, i ^ bit) for i in range(n)])  51 us
    all_to_all x1, waiting for transfers between devices, to_sequences(): return lax.all_to_all(block, 'ctx', 0, 0, tiled=True)  34.4 us
    pallas_call x2, Pallas kernels, attend_back(): pl.pallas_call(attend_back_kernel, grid_spec=pltpu.PrefetchScalarGridSpec...  33.6 us
    pallas_call x1, Pallas kernels, attend(): pl.pallas_call(attend_kernel, grid_spec=pltpu.PrefetchScalarGridSpec(num_...  20.4 us
    convert_element_type x13, other arithmetic, add_low(): return total.astype(BF)  15.3 us
  transfers between devices with their start and end apart: 49, of which 25 were waited for; matrix products, arithmetic and copies ran while one was open for 11% of the time, Pallas kernels for 37%

profile of v3, /device:TPU:0, one launch (start us, length us, event | category | flops | bytes accessed | tf_op | source)
XLA Modules:
  0.0 519.4 jit_solution(3327752282858911389)
XLA Ops:
  27.4 34.4 %all-to-all-done = bf16[4,2,128,1024]{3,2,1,0:T(8,128)(2,1)S(1)} async-done(((bf16[4,2,128,1024]{3,2,1,0:T(8,128)(2,1)}), bf16[4,2,128,1024]{3,2,1,0:T(8,128)(2,1)S(1)}, u32[]{:S(2)}, u32[]{:S(2)}) %all-to-all-start) | async-done | bytes 2097184 | tf_op jit(solution)/shard_map/all_to_all | solution.py:125
  70.9 7.6 %collective-permute-done.4 = bf16[64,3072]{1,0:T(8,128)(2,1)S(1)} collective-permute-done((bf16[64,3072]{1,0:T(8,128)(2,1)S(1)}, bf16[64,3072]{1,0:T(8,128)(2,1)S(1)}, u32[]{:S(2)}, u32[]{:S(2)}) %collective-permute-start.4) | collective-permute-done | bytes 393248 | tf_op jit(solution)/shard_map/ppermute | solution.py:29
  94.0 12.3 %qkv.1 = bf16[1024,3072]{1,0:T(8,128)(2,1)} custom-call(s32[4]{0:T(128)} %pad_add_fusion.meta_ref.meta, bf16[1024,1024]{1,0:T(8,128)(2,1)} %bitcast.87, f32[1,3072]{1,0:T(1,128)} %pad_maximum_fusion.6.refs_1_, bf16[4,144,3072]{2,1,0:T(8,128)(2,1)} %copy-done.10, bf16[4,144,3072]{2,1,0:T(8,128)(2,1)} %collective-permute-done.7.refs_3_.refs_4_), custom_call_target="tpu_custom_call" | custom-call | flops 12999999488 | bytes 1000000 | tf_op jit(solution)/shard_map/qkv/pallas_call | solution.py:265
  116.4 20.4 %attend.1 = (bf16[2,512,1024]{2,1,0:T(8,128)(2,1)}, f32[2,4,4,512]{3,2,1,0:T(4,128)}) custom-call(s32[4]{0:T(128)} %pad_add_fusion.meta_ref.meta, bf16[2,512,3072]{2,1,0:T(8,128)(2,1)} %bitcast.143, bf16[2,512,3072]{2,1,0:T(8,128)(2,1)} %bitcast.144, bf16[2,512,3072]{2,1,0:T(8,128)(2,1)} %bitcast.145), custom_call_target="tpu_custom_call" | custom-call | flops 24000000000 | bytes 1000000 | tf_op jit(solution)/shard_map/attend/pallas_call | solution.py:480
  140.5 9.9 %out.1 = (f32[1024,1024]{1,0:T(8,128)}, f32[1024,128]{1,0:T(8,128)}, bf16[1024,1024]{1,0:T(8,128)(2,1)}) custom-call(s32[4]{0:T(128)} %pad_add_fusion.meta_ref.meta, bf16[1024,1024]{1,0:T(8,128)(2,1)} %bitcast.97, bf16[1024,1024]{1,0:T(8,128)(2,1)} %bitcast.88, f32[1,1024]{1,0:T(1,128)} %bitcast.139, f32[1,1024]{1,0:T(1,128)} %bitcast.131, ...), custom_call_target="tpu_custom_call" | custom-call | flops 10000000000 | bytes 1000000 | tf_op jit(solution)/shard_map/out/pallas_call | solution.py:265
  152.9 22.4 %up.1 = (bf16[1024,4096]{1,0:T(8,128)(2,1)}, bf16[1024,4096]{1,0:T(8,128)(2,1)}) custom-call(s32[4]{0:T(128)} %pad_add_fusion.meta_ref.meta, bf16[1024,1024]{1,0:T(8,128)(2,1)} %get-tuple-element.174.refs_0_.refs_1_.refs_2_.refs_3_, f32[1,4096]{1,0:T(1,128)} %bitcast.130, bf16[4,128,5120]{2,1,0:T(8,128)(2,1)} %pad_maximum_fusion.refs_5_.refs_2_.refs_7_, ...), custom_call_target="tpu_custom_call" | custom-call | flops 23000000512 | bytes 1000000 | tf_op jit(solution)/shard_map/up/pallas_call | solution.py:265
  178.9 20.3 %down.1 = (bf16[1024,1024]{1,0:T(8,128)(2,1)}, f32[1024,1024]{1,0:T(8,128)}, bf16[1024,1024]{1,0:T(8,128)(2,1)}, f32[8,1024]{1,0:T(8,128)}, f32[8,1024]{1,0:T(8,128)}, /*index=5*/f32[8,1024]{1,0:T(8,128)}) custom-call(s32[4]{0:T(128)} %pad_add_fusion.meta_ref.meta, bf16[1024,4096]{1,0:T(8,128)(2,1)} %get-tuple-element.178.refs_0_.refs_1_.refs_2_.refs_3_, ...), custom_call_target="tpu_custom_call" | custom-call | flops 20999999488 | bytes 1000000 | tf_op jit(solution)/shard_map/down/pallas_call | solution.py:265
  199.2 9.4 %gd_away.1 = bf16[4,512,1024]{2,1,0:T(8,128)(2,1)} custom-call(s32[4]{0:T(128)} %pad_add_fusion.meta_ref.meta, bf16[1024,4096]{1,0:T(8,128)(2,1)} %get-tuple-element.178.refs_0_.refs_1_.refs_2_.refs_3_, bf16[1024,4096]{1,0:T(8,128)(2,1)} %get-tuple-element.178.refs_0_.refs_1_.refs_2_.refs_3_, ...), custom_call_target="tpu_custom_call" | custom-call | flops 11000000512 | bytes 1000000 | tf_op jit(solution)/shard_map/gd_away/pallas_call | solution.py:662
  211.8 15.0 %hidden.1 = (bf16[1024,4096]{1,0:T(8,128)(2,1)}, f32[8,4096]{1,0:T(8,128)}) custom-call(bf16[1024,1024]{1,0:T(8,128)(2,1)} %get-tuple-element.187.refs_4_.second, bf16[4096,1024]{1,0:T(8,128)(2,1)} %all-gather.2.cloned.1.call-done.whole, bf16[1024,4096]{1,0:T(8,128)(2,1)} %get-tuple-element.188.deriv), custom_call_target="tpu_custom_call" | custom-call | flops 17999998976 | bytes 1000000 | tf_op jit(solution)/shard_map/hidden/pallas_call | solution.py:382
  229.1 10.4 %gd_keep.1 = (bf16[512,1024]{1,0:T(8,128)(2,1)}, bf16[512,1024]{1,0:T(8,128)(2,1)}, bf16[512,1024]{1,0:T(8,128)(2,1)}, bf16[512,512]{1,0:T(8,128)(2,1)}, bf16[512,512]{1,0:T(8,128)(2,1)}) custom-call(s32[4]{0:T(128)} %pad_add_fusion.meta_ref.meta, bf16[1024,4096]{1,0:T(8,128)(2,1)} %get-tuple-element.178.refs_0_.refs_1_.refs_2_.refs_3_, ...), custom_call_target="tpu_custom_call" | custom-call | flops 11000000512 | bytes 1000000 | tf_op jit(solution)/shard_map/gd_keep/pallas_call | solution.py:662
  243.2 9.6 %gu_away.1 = bf16[4,128,4096]{2,1,0:T(8,128)(2,1)} custom-call(s32[4]{0:T(128)} %pad_add_fusion.meta_ref.meta, bf16[1024,1024]{1,0:T(8,128)(2,1)} %get-tuple-element.174.refs_0_.refs_1_.refs_2_.refs_3_, bf16[1024,1024]{1,0:T(8,128)(2,1)} %get-tuple-element.174.refs_0_.refs_1_.refs_2_.refs_3_, ...), custom_call_target="tpu_custom_call" | custom-call | flops 11000000512 | bytes 1000000 | tf_op jit(solution)/shard_map/gu_away/pallas_call | solution.py:662
  265.7 21.3 %first.1 = (f32[1024,1024]{1,0:T(8,128)}, bf16[1024,1024]{1,0:T(8,128)(2,1)}, bf16[1024,1024]{1,0:T(8,128)(2,1)}, f32[8,1024]{1,0:T(8,128)}, f32[8,1024]{1,0:T(8,128)}, /*index=5*/f32[8,1024]{1,0:T(8,128)}) custom-call(s32[4]{0:T(128)} %pad_add_fusion.meta_ref.meta, bf16[1024,4096]{1,0:T(8,128)(2,1)} %get-tuple-element.206.refs_4_.refs_0_, ...), custom_call_target="tpu_custom_call" | custom-call | flops 23000000512 | bytes 1000000 | tf_op jit(solution)/shard_map/first/pallas_call | solution.py:265
  287.8 10.4 %gu_keep.1 = (bf16[128,4096]{1,0:T(8,128)(2,1)}, bf16[128,4096]{1,0:T(8,128)(2,1)}, bf16[128,4096]{1,0:T(8,128)(2,1)}, bf16[128,2048]{1,0:T(8,128)(2,1)}, bf16[128,2048]{1,0:T(8,128)(2,1)}) custom-call(s32[4]{0:T(128)} %pad_add_fusion.meta_ref.meta, bf16[1024,1024]{1,0:T(8,128)(2,1)} %get-tuple-element.174.refs_0_.refs_1_.refs_2_.refs_3_, ...), custom_call_target="tpu_custom_call" | custom-call | flops 11000000512 | bytes 1000000 | tf_op jit(solution)/shard_map/gu_keep/pallas_call | solution.py:662
  303.0 16.8 %attend_back.2 = (bf16[3,2,512,512]{3,2,1,0:T(8,128)(2,1)}, f32[3,2,8,512]{3,2,1,0:T(8,128)}) custom-call(s32[4]{0:T(128)} %pad_add_fusion.meta_ref.meta, bf16[2,512,3072]{2,1,0:T(8,128)(2,1)} %bitcast.146, bf16[2,512,3072]{2,1,0:T(8,128)(2,1)} %bitcast.147, bf16[2,512,3072]{2,1,0:T(8,128)(2,1)} %bitcast.148, bf16[2,512,1024]{2,1,0:T(8,128)(2,1)} %bitcast.152, ...), custom_call_target="tpu_custom_call" | custom-call | flops 20999999488 | bytes 1000000 | tf_op jit(solution)/shard_map/attend_back/pallas_call | solution.py:508
  323.5 16.7 %attend_back.3 = (bf16[3,2,512,512]{3,2,1,0:T(8,128)(2,1)}, f32[3,2,8,512]{3,2,1,0:T(8,128)}) custom-call(s32[4]{0:T(128)} %pad_add_fusion.meta_ref.meta, bf16[2,512,3072]{2,1,0:T(8,128)(2,1)} %bitcast.149, bf16[2,512,3072]{2,1,0:T(8,128)(2,1)} %bitcast.150, bf16[2,512,3072]{2,1,0:T(8,128)(2,1)} %bitcast.151, bf16[2,512,1024]{2,1,0:T(8,128)(2,1)} %bitcast.153, ...), custom_call_target="tpu_custom_call" | custom-call | flops 20999999488 | bytes 1000000 | tf_op jit(solution)/shard_map/attend_back/pallas_call | solution.py:508
  351.4 11.0 %gb_away.1 = bf16[4,144,4096]{2,1,0:T(8,128)(2,1)} custom-call(s32[4]{0:T(128)} %pad_add_fusion.meta_ref.meta, bf16[1024,1024]{1,0:T(8,128)(2,1)} %bitcast.89, bf16[1024,1024]{1,0:T(8,128)(2,1)} %bitcast.90, bf16[1024,1024]{1,0:T(8,128)(2,1)} %bitcast.91, bf16[1024,1024]{1,0:T(8,128)(2,1)} %bitcast.92, bf16[1024,1024]{1,0:T(8,128)(2,1)} %bitcast.98, ...), custom_call_target="tpu_custom_call" | custom-call | flops 14000000000 | bytes 1000000 | tf_op jit(solution)/shard_map/gb_away/pallas_call | solution.py:662
  366.3 13.2 %input.1 = bf16[1024,1024]{1,0:T(8,128)(2,1)} custom-call(s32[4]{0:T(128)} %pad_add_fusion.meta_ref.meta, bf16[3,1024,512]{2,1,0:T(8,128)(2,1)} %bitcast.108, bf16[3,1024,512]{2,1,0:T(8,128)(2,1)} %bitcast.111, f32[1024,1024]{1,0:T(8,128)} %get-tuple-element.255.refs_2_, bf16[4,144,3072]{2,1,0:T(8,128)(2,1)} %copy-done.10, ...), custom_call_target="tpu_custom_call" | custom-call | flops 14000000000 | bytes 1000000 | tf_op jit(solution)/shard_map/input/pallas_call | solution.py:265
  383.4 12.0 %gb_keep.1 = (bf16[144,4096]{1,0:T(8,128)(2,1)}, bf16[144,4096]{1,0:T(8,128)(2,1)}, bf16[144,4096]{1,0:T(8,128)(2,1)}, bf16[144,2048]{1,0:T(8,128)(2,1)}, bf16[144,2048]{1,0:T(8,128)(2,1)}) custom-call(s32[4]{0:T(128)} %pad_add_fusion.meta_ref.meta, bf16[1024,1024]{1,0:T(8,128)(2,1)} %bitcast.93, bf16[1024,1024]{1,0:T(8,128)(2,1)} %bitcast.94, ...), custom_call_target="tpu_custom_call" | custom-call | flops 3000000000 | bytes 1000000 | tf_op jit(solution)/shard_map/gb_keep/pallas_call | solution.py:662
  406.8 10.1 %collective-permute-done.35 = bf16[1,128,1024]{2,1,0:T(8,128)(2,1)S(1)} collective-permute-done((bf16[1,128,1024]{2,1,0:T(8,128)(2,1)S(1)}, bf16[1,128,1024]{2,1,0:T(8,128)(2,1)S(1)}, u32[]{:S(2)}, u32[]{:S(2)}) %collective-permute-start.35) | collective-permute-done | bytes 262176 | tf_op jit(solution)/shard_map/ppermute | solution.py:29
  431.6 8.0 %collective-permute-done.38 = bf16[1,128,1024]{2,1,0:T(8,128)(2,1)S(1)} collective-permute-done((bf16[1,128,1024]{2,1,0:T(8,128)(2,1)S(1)}, bf16[1,128,1024]{2,1,0:T(8,128)(2,1)S(1)}, u32[]{:S(2)}, u32[]{:S(2)}) %collective-permute-start.38) | collective-permute-done | bytes 262176 | tf_op jit(solution)/shard_map/ppermute | solution.py:29
  453.0 16.3 %collective-permute-done.41 = bf16[1,128,1024]{2,1,0:T(8,128)(2,1)S(1)} collective-permute-done((bf16[1,128,1024]{2,1,0:T(8,128)(2,1)S(1)}, bf16[1,128,1024]{2,1,0:T(8,128)(2,1)S(1)}, u32[]{:S(2)}, u32[]{:S(2)}) %collective-permute-start.41) | collective-permute-done | bytes 262176 | tf_op jit(solution)/shard_map/ppermute | solution.py:29
  473.4 9.2 %collective-permute-done.43 = bf16[144,1024]{1,0:T(8,128)(2,1)S(1)} collective-permute-done((bf16[144,1024]{1,0:T(8,128)(2,1)S(1)}, bf16[144,1024]{1,0:T(8,128)(2,1)S(1)}, u32[]{:S(2)}, u32[]{:S(2)}) %collective-permute-start.43) | collective-permute-done | bytes 294944 | tf_op jit(solution)/shard_map/ppermute | solution.py:29
  484.2 8.7 %collective-permute-done.44 = bf16[144,1024]{1,0:T(8,128)(2,1)S(1)} collective-permute-done((bf16[144,1024]{1,0:T(8,128)(2,1)S(1)}, bf16[144,1024]{1,0:T(8,128)(2,1)S(1)}, u32[]{:S(2)}, u32[]{:S(2)}) %collective-permute-start.44) | collective-permute-done | bytes 294944 | tf_op jit(solution)/shard_map/ppermute | solution.py:29
  498.1 9.7 %collective-permute-done.45 = bf16[144,2048]{1,0:T(8,128)(2,1)S(1)} collective-permute-done((bf16[144,2048]{1,0:T(8,128)(2,1)S(1)}, bf16[144,2048]{1,0:T(8,128)(2,1)S(1)}, u32[]{:S(2)}, u32[]{:S(2)}) %collective-permute-start.45) | collective-permute-done | bytes 589856 | tf_op jit(solution)/shard_map/ppermute | solution.py:29
  (307 shorter events, 168.6 us)
Async XLA Ops:
  7.2 54.7 %all-to-all-start = ((bf16[4,2,128,1024]{3,2,1,0:T(8,128)(2,1)}), bf16[4,2,128,1024]{3,2,1,0:T(8,128)(2,1)S(1)}, u32[]{:S(2)}, u32[]{:S(2)}) async-start(bf16[4,2,128,1024]{3,2,1,0:T(8,128)(2,1)} %bitcast.123), calls=%async_computation | async-start | bytes 4194304 | tf_op jit(solution)/shard_map/all_to_all | solution.py:125
  13.7 163.8 %all-gather.2.cloned.1.call-start = ((), (), s32[]{:S(2)}) async-start(), calls=%async_computation.1 | async-start | bytes 9437184 | tf_op jit(solution)/shard_map/all_gather | solution.py:733
  15.6 50.7 %collective-permute-start.2 = (bf16[128,5120]{1,0:T(8,128)(2,1)}, bf16[128,5120]{1,0:T(8,128)(2,1)S(1)}, u32[]{:S(2)}, u32[]{:S(2)}) collective-permute-start(bf16[128,5120]{1,0:T(8,128)(2,1)} %constant_dynamic-update-slice_fusion), channel_id=1, source_target_pairs={{0,8},{4,12},{8,0},{12,4},{16,24},{20,28},{24,16},{28,20},{1,9},{5... | collective-permute-start | bytes 3932168 | tf_op jit(solution)/shard_map/ppermute | solution.py:29
  17.1 49.2 %collective-permute-start.3 = (bf16[128,5120]{1,0:T(8,128)(2,1)}, bf16[128,5120]{1,0:T(8,128)(2,1)}, u32[]{:S(2)}, u32[]{:S(2)}) collective-permute-start(bf16[128,5120]{1,0:T(8,128)(2,1)} %constant_dynamic-update-slice_fusion), channel_id=1, source_target_pairs={{0,16},{4,20},{8,24},{12,28},{16,0},{20,4},{24,8},{28,12},{1,17},{... | collective-permute-start | bytes 3932168 | tf_op jit(solution)/shard_map/ppermute | solution.py:29
  22.8 42.3 %collective-permute-start = (bf16[144,3072]{1,0:T(8,128)(2,1)}, bf16[144,3072]{1,0:T(8,128)(2,1)}, u32[]{:S(2)}, u32[]{:S(2)}) collective-permute-start(bf16[144,3072]{1,0:T(8,128)(2,1)} %get-tuple-element.313), channel_id=1, source_target_pairs={{0,8},{4,12},{8,0},{12,4},{16,24},{20,28},{24,16},{28,20},{1,9},{5... | collective-permute-start | bytes 2654216 | tf_op jit(solution)/shard_map/ppermute | solution.py:29
  23.3 42.9 %collective-permute-start.1 = (bf16[144,3072]{1,0:T(8,128)(2,1)}, bf16[144,3072]{1,0:T(8,128)(2,1)}, u32[]{:S(2)}, u32[]{:S(2)}) collective-permute-start(bf16[144,3072]{1,0:T(8,128)(2,1)} %get-tuple-element.313), channel_id=1, source_target_pairs={{0,16},{4,20},{8,24},{12,28},{16,0},{20,4},{24,8},{28,12},{1,17},{... | collective-permute-start | bytes 2654216 | tf_op jit(solution)/shard_map/ppermute | solution.py:29
  83.7 22.6 %collective-permute-start.8 = (bf16[64,5120]{1,0:T(8,128)(2,1)}, bf16[64,5120]{1,0:T(8,128)(2,1)}, u32[]{:S(2)}, u32[]{:S(2)}) collective-permute-start(bf16[64,5120]{1,0:T(8,128)(2,1)} %slice.175), channel_id=1, source_target_pairs={{0,16},{4,20},{8,24},{12,28},{16,0},{20,4},{24,8},{28,12},{1,17},{... | collective-permute-start | bytes 1966088 | tf_op jit(solution)/shard_map/ppermute | solution.py:29
  106.4 256.1 %all-reduce.10.cloned.1.call-start = ((), (), s32[]{:S(2)}) async-start(), calls=%async_computation.2 | async-start | bytes 2097152 | tf_op jit(solution)/shard_map/psum | solution.py:789
  112.8 27.7 %collective-permute-start.11 = (bf16[4,128,5120]{2,1,0:T(8,128)(2,1)}, bf16[4,128,5120]{2,1,0:T(8,128)(2,1)}, u32[]{:S(2)}, u32[]{:S(2)}) collective-permute-start(bf16[4,128,5120]{2,1,0:T(8,128)(2,1)} %pad_maximum_fusion.refs_5_.refs_2_.refs_7_), channel_id=1, source_target_pairs={{0,4},{4,0},{8,12},{12,8},{16,20},{20,16},{24,28},{28,24},{1,5},{5... | collective-permute-start | bytes 15728648 | tf_op jit(solution)/shard_map/ppermute | solution.py:29
  114.1 26.5 %collective-permute-start.12 = (bf16[2,128,1024]{2,1,0:T(8,128)(2,1)S(1)}, bf16[2,128,1024]{2,1,0:T(8,128)(2,1)S(1)}, u32[]{:S(2)}, u32[]{:S(2)}) collective-permute-start(bf16[2,128,1024]{2,1,0:T(8,128)(2,1)S(1)} %copy-done.35), channel_id=1, source_target_pairs={{0,2},{1,3},{2,0},{3,1},{4,6},{5,7},{6,4},{7,5},{8,10},{9,11},{10,... | collective-permute-start | bytes 1572872 | tf_op jit(solution)/shard_map/ppermute | solution.py:29
  150.5 27.0 %collective-permute-start.13 = (bf16[2,128,1024]{2,1,0:T(8,128)(2,1)S(1)}, bf16[2,128,1024]{2,1,0:T(8,128)(2,1)S(1)}, u32[]{:S(2)}, u32[]{:S(2)}) collective-permute-start(bf16[2,128,1024]{2,1,0:T(8,128)(2,1)S(1)} %copy-done.34), channel_id=1, source_target_pairs={{0,3},{1,2},{2,1},{3,0},{4,7},{5,6},{6,5},{7,4},{8,11},{9,10},{10,... | collective-permute-start | bytes 1572872 | tf_op jit(solution)/shard_map/ppermute | solution.py:29
  255.5 31.6 %collective-permute-start.20 = (bf16[4,128,4096]{2,1,0:T(8,128)(2,1)}, bf16[4,128,4096]{2,1,0:T(8,128)(2,1)}, u32[]{:S(2)}, u32[]{:S(2)}) collective-permute-start(bf16[4,128,4096]{2,1,0:T(8,128)(2,1)} %gu_away.1), channel_id=1, source_target_pairs={{0,4},{4,0},{8,12},{12,8},{16,20},{20,16},{24,28},{28,24},{1,5},{5... | collective-permute-start | bytes 12582920 | tf_op jit(solution)/shard_map/ppermute | solution.py:29
  258.0 29.0 %collective-permute-start.21 = (bf16[512,1024]{1,0:T(8,128)(2,1)}, bf16[512,1024]{1,0:T(8,128)(2,1)}, u32[]{:S(2)}, u32[]{:S(2)}) collective-permute-start(bf16[512,1024]{1,0:T(8,128)(2,1)} %add_convert_fusion.8), channel_id=1, source_target_pairs={{0,8},{4,12},{8,0},{12,4},{16,24},{20,28},{24,16},{28,20},{1,9},{5... | collective-permute-start | bytes 3145736 | tf_op jit(solution)/shard_map/ppermute | solution.py:29
  261.0 26.1 %collective-permute-start.22 = (bf16[512,1024]{1,0:T(8,128)(2,1)}, bf16[512,1024]{1,0:T(8,128)(2,1)S(1)}, u32[]{:S(2)}, u32[]{:S(2)}) collective-permute-start(bf16[512,1024]{1,0:T(8,128)(2,1)} %add_convert_fusion.7), channel_id=1, source_target_pairs={{0,16},{4,20},{8,24},{12,28},{16,0},{20,4},{24,8},{28,12},{1,17},{... | collective-permute-start | bytes 3145736 | tf_op jit(solution)/shard_map/ppermute | solution.py:29
  263.5 23.6 %collective-permute-start.23 = (bf16[2,128,1024]{2,1,0:T(8,128)(2,1)}, bf16[2,128,1024]{2,1,0:T(8,128)(2,1)S(1)}, u32[]{:S(2)}, u32[]{:S(2)}) collective-permute-start(bf16[2,128,1024]{2,1,0:T(8,128)(2,1)} %constant_dynamic-slice_fusion.8), channel_id=1, source_target_pairs={{0,3},{1,2},{2,1},{3,0},{4,7},{5,6},{6,5},{7,4},{8,11},{9,10},{10,... | collective-permute-start | bytes 1572872 | tf_op jit(solution)/shard_map/ppermute | solution.py:29
  298.2 21.6 %collective-permute-start.24 = (bf16[128,2048]{1,0:T(8,128)(2,1)}, bf16[128,2048]{1,0:T(8,128)(2,1)S(1)}, u32[]{:S(2)}, u32[]{:S(2)}) collective-permute-start(bf16[128,2048]{1,0:T(8,128)(2,1)} %get-tuple-element.224), channel_id=1, source_target_pairs={{0,16},{4,20},{8,24},{12,28},{16,0},{20,4},{24,8},{28,12},{1,17},{... | collective-permute-start | bytes 1572872 | tf_op jit(solution)/shard_map/ppermute | solution.py:29
  298.8 21.1 %collective-permute-start.25 = (bf16[128,2048]{1,0:T(8,128)(2,1)}, bf16[128,2048]{1,0:T(8,128)(2,1)S(1)}, u32[]{:S(2)}, u32[]{:S(2)}) collective-permute-start(bf16[128,2048]{1,0:T(8,128)(2,1)} %get-tuple-element.225), channel_id=1, source_target_pairs={{0,8},{4,12},{8,0},{12,4},{16,24},{20,28},{24,16},{28,20},{1,9},{5... | collective-permute-start | bytes 1572872 | tf_op jit(solution)/shard_map/ppermute | solution.py:29
  320.8 24.3 %collective-permute-start.26 = (bf16[128,4096]{1,0:T(8,128)(2,1)S(1)}, bf16[128,4096]{1,0:T(8,128)(2,1)}, u32[]{:S(2)}, u32[]{:S(2)}) collective-permute-start(bf16[128,4096]{1,0:T(8,128)(2,1)S(1)} %add_convert_fusion.6), channel_id=1, source_target_pairs={{0,8},{4,12},{8,0},{12,4},{16,24},{20,28},{24,16},{28,20},{1,9},{5... | collective-permute-start | bytes 3145736 | tf_op jit(solution)/shard_map/ppermute | solution.py:29
  321.9 24.3 %collective-permute-start.27 = (bf16[128,4096]{1,0:T(8,128)(2,1)S(1)}, bf16[128,4096]{1,0:T(8,128)(2,1)}, u32[]{:S(2)}, u32[]{:S(2)}) collective-permute-start(bf16[128,4096]{1,0:T(8,128)(2,1)S(1)} %add_convert_fusion.5), channel_id=1, source_target_pairs={{0,16},{4,20},{8,24},{12,28},{16,0},{20,4},{24,8},{28,12},{1,17},{... | collective-permute-start | bytes 3145736 | tf_op jit(solution)/shard_map/ppermute | solution.py:29
  418.9 28.1 %collective-permute-start.36 = (bf16[144,4096]{1,0:T(8,128)(2,1)}, bf16[144,4096]{1,0:T(8,128)(2,1)}, u32[]{:S(2)}, u32[]{:S(2)}) collective-permute-start(bf16[144,4096]{1,0:T(8,128)(2,1)} %add_convert_fusion.2), channel_id=1, source_target_pairs={{0,8},{4,12},{8,0},{12,4},{16,24},{20,28},{24,16},{28,20},{1,9},{5... | collective-permute-start | bytes 3538952 | tf_op jit(solution)/shard_map/ppermute | solution.py:29
  420.7 27.8 %collective-permute-start.37 = (bf16[144,4096]{1,0:T(8,128)(2,1)}, bf16[144,4096]{1,0:T(8,128)(2,1)}, u32[]{:S(2)}, u32[]{:S(2)}) collective-permute-start(bf16[144,4096]{1,0:T(8,128)(2,1)} %add_convert_fusion.1), channel_id=1, source_target_pairs={{0,16},{4,20},{8,24},{12,28},{16,0},{20,4},{24,8},{28,12},{1,17},{... | collective-permute-start | bytes 3538952 | tf_op jit(solution)/shard_map/ppermute | solution.py:29
  421.2 24.5 %collective-permute-start.40 = (bf16[128,2048]{1,0:T(8,128)(2,1)S(1)}, bf16[128,2048]{1,0:T(8,128)(2,1)}, u32[]{:S(2)}, u32[]{:S(2)}) collective-permute-start(bf16[128,2048]{1,0:T(8,128)(2,1)S(1)} %pad_maximum_fusion.4), channel_id=1, source_target_pairs={{0,1},{1,0},{2,3},{3,2},{4,5},{5,4},{6,7},{7,6},{8,9},{9,8},{10,11... | collective-permute-start | bytes 1572872 | tf_op jit(solution)/shard_map/ppermute | solution.py:29
  423.9 20.9 %collective-permute-start.39 = (bf16[1,128,1024]{2,1,0:T(8,128)(2,1)S(1)}, bf16[1,128,1024]{2,1,0:T(8,128)(2,1)S(1)}, u32[]{:S(2)}, u32[]{:S(2)}) collective-permute-start(bf16[1,128,1024]{2,1,0:T(8,128)(2,1)S(1)} %slice.196), channel_id=1, source_target_pairs={{0,3},{1,2},{2,1},{3,0},{4,7},{5,6},{6,5},{7,4},{8,11},{9,10},{10,... | collective-permute-start | bytes 786440 | tf_op jit(solution)/shard_map/ppermute | solution.py:29
  450.7 21.3 %collective-permute-start.42 = (bf16[144,2048]{1,0:T(8,128)(2,1)S(1)}, bf16[144,2048]{1,0:T(8,128)(2,1)S(1)}, u32[]{:S(2)}, u32[]{:S(2)}) collective-permute-start(bf16[144,2048]{1,0:T(8,128)(2,1)S(1)} %constant_dynamic-slice_fusion.1), channel_id=1, source_target_pairs={{0,1},{1,0},{2,3},{3,2},{4,5},{5,4},{6,7},{7,6},{8,9},{9,8},{10,11... | collective-permute-start | bytes 1769480 | tf_op jit(solution)/shard_map/ppermute | solution.py:29
  (76 other events, 838.8 us)
Sparse Core Ops, SparseCore 0:
  106.5 53.3 all-gather.1
  303.1 50.1 all-reduce.9

commit v4 on v3

--- a/solution.py
+++ b/solution.py
@@ -735,7 +735,7 @@
     mixed, lse = attend(meta, proj, per, n * blk)
     mixed, mid_other, cot_2 = sync(mixed, mid_other, cot_2)
     out_w = (mid_mine, mid_other, thin, 0, width, 2)
-    up_w = (mid_mine, mid_other, thin, width, ff, 8)
+    up_w = (mid_mine, mid_other, thin, width, ff, 4)
     normed_one, inverse_one, first_low = dense(
         out_body, "out", meta, rows, tile, [mixed, x], [bout, gone, sone], [out_w], [(width, F32), (128, F32), (width, BF)], []
     )
@@ -826,18 +826,19 @@
     (grad_in,) = dense(input_body, "input", meta, rows, tile, [p_one, p_two, sum_one], [], [qkv_w[:5] + (6,)], [(width, BF)], [])
     grad_in, come, u_come = sync(grad_in, come, u_come)
     grad_in = grad_in.reshape(per, n * blk, width)
-    in_1 = trade(part_of(grad_in, 1, 1), 1)
+    part_1 = part_of(grad_in, 1, 1)
     if tuned:
         u_half = add_low(u_keep, u_come)
         u_other = swap(u_half, "ctx", 2)
         b_sums = weight_grad("gb_keep", meta, 0, *products, 1024, come=come, extra=extra)
-        b_sums, u_other, in_1, grad_in = sync(b_sums, u_other, in_1, grad_in)
+        b_sums, u_other, part_1, grad_in = sync(b_sums, u_other, part_1, grad_in)
+    in_1 = trade(part_1, 1)
     part_2, part_3 = part_of(grad_in, 2, 1), part_of(grad_in, 3, 1)
     in_2 = trade(part_2[:cut], 2)
     if tuned:
         b_far = send_far(b_sums)
         u_whole = join_ctx(u_half, u_other, 2)
-        b_far, in_2, part_2, part_3, u_whole = sync(b_far, in_2, part_2, part_3, u_whole)
+        b_far, in_1, in_2, part_2, part_3, u_whole = sync(b_far, in_1, in_2, part_2, part_3, u_whole)
         b_near = send_near(b_sums, b_far)
         u_other = swap(u_whole, "ctx", 1)
     in_2b, in_3 = trade(part_2[cut:], 2), trade(part_3[:cut], 3)

time: 527 us -> 526 us (level)
  waiting for transfers between devices: 138 us -> 144 us
  starting transfers between devices: 57.6 us -> 52 us
    ppermute x46, waiting for transfers between devices: 103 us -> 110 us  [swap(): return lax.ppermute(x, axis, [(i, i ^ bit) for i in range(n)])]
    ppermute x46, starting transfers between devices: 51 us -> 45.3 us  [swap(): return lax.ppermute(x, axis, [(i, i ^ bit) for i in range(n)])]
  transfers between devices with their start and end apart: 49 -> 49, of which waited for: 25 -> 23; matrix products, arithmetic and copies ran while one was open for 11% -> 11% of each run, Pallas kernels for 37% -> 37%
where the time goes in v4:
time: 526 us; the launch traced here: 519 us
  Pallas kernels  231 us (44%)
  waiting for transfers between devices  144 us (27%)
  starting transfers between devices  52 us (10%)
  local copies, waits for them, and re-layouts  40.2 us (8%)
  other arithmetic  35.8 us (7%)
  between operations  15.5 us (3%)
    ppermute x46, waiting for transfers between devices, swap(): return lax.ppermute(x, axis, [(i, i ^ bit) for i in range(n)])  110 us
    pallas_call x6, Pallas kernels, dense(): pl.pallas_call(kernel, grid_spec=pltpu.PrefetchScalarGridSpec(num_scalar_...  99 us
    pallas_call x6, Pallas kernels, weight_grad(): pl.pallas_call(kernel, grid_spec=pltpu.PrefetchScalarGridSpec(num_scalar_...  63.1 us
    ppermute x46, starting transfers between devices, swap(): return lax.ppermute(x, axis, [(i, i ^ bit) for i in range(n)])  45.3 us
    all_to_all x1, waiting for transfers between devices, to_sequences(): return lax.all_to_all(block, 'ctx', 0, 0, tiled=True)  34.4 us
    pallas_call x2, Pallas kernels, attend_back(): pl.pallas_call(attend_back_kernel, grid_spec=pltpu.PrefetchScalarGridSpec...  33.6 us
    pallas_call x1, Pallas kernels, attend(): pl.pallas_call(attend_kernel, grid_spec=pltpu.PrefetchScalarGridSpec(num_...  20.4 us
    convert_element_type x13, other arithmetic, add_low(): return total.astype(BF)  15.3 us
  transfers between devices with their start and end apart: 49, of which 23 were waited for; matrix products, arithmetic and copies ran while one was open for 11% of the time, Pallas kernels for 37%

profile of v4, /device:TPU:0, one launch (start us, length us, event | category | flops | bytes accessed | tf_op | source)
XLA Modules:
  0.0 518.9 jit_solution(10691345133845323253)
XLA Ops:
  27.4 34.4 %all-to-all-done = bf16[4,2,128,1024]{3,2,1,0:T(8,128)(2,1)S(1)} async-done(((bf16[4,2,128,1024]{3,2,1,0:T(8,128)(2,1)}), bf16[4,2,128,1024]{3,2,1,0:T(8,128)(2,1)S(1)}, u32[]{:S(2)}, u32[]{:S(2)}) %all-to-all-start) | async-done | bytes 2097184 | tf_op jit(solution)/shard_map/all_to_all | solution.py:125
  70.9 7.6 %collective-permute-done.4 = bf16[64,3072]{1,0:T(8,128)(2,1)S(1)} collective-permute-done((bf16[64,3072]{1,0:T(8,128)(2,1)S(1)}, bf16[64,3072]{1,0:T(8,128)(2,1)S(1)}, u32[]{:S(2)}, u32[]{:S(2)}) %collective-permute-start.4) | collective-permute-done | bytes 393248 | tf_op jit(solution)/shard_map/ppermute | solution.py:29
  94.0 12.3 %qkv.1 = bf16[1024,3072]{1,0:T(8,128)(2,1)} custom-call(s32[4]{0:T(128)} %pad_add_fusion.meta_ref.meta, bf16[1024,1024]{1,0:T(8,128)(2,1)} %bitcast.87, f32[1,3072]{1,0:T(1,128)} %pad_maximum_fusion.6.refs_1_, bf16[4,144,3072]{2,1,0:T(8,128)(2,1)} %copy-done.10, bf16[4,144,3072]{2,1,0:T(8,128)(2,1)} %collective-permute-done.7.refs_3_.refs_4_), custom_call_target="tpu_custom_call" | custom-call | flops 12999999488 | bytes 1000000 | tf_op jit(solution)/shard_map/qkv/pallas_call | solution.py:265
  116.4 20.4 %attend.1 = (bf16[2,512,1024]{2,1,0:T(8,128)(2,1)}, f32[2,4,4,512]{3,2,1,0:T(4,128)}) custom-call(s32[4]{0:T(128)} %pad_add_fusion.meta_ref.meta, bf16[2,512,3072]{2,1,0:T(8,128)(2,1)} %bitcast.143, bf16[2,512,3072]{2,1,0:T(8,128)(2,1)} %bitcast.144, bf16[2,512,3072]{2,1,0:T(8,128)(2,1)} %bitcast.145), custom_call_target="tpu_custom_call" | custom-call | flops 24000000000 | bytes 1000000 | tf_op jit(solution)/shard_map/attend/pallas_call | solution.py:480
  140.5 10.0 %out.1 = (f32[1024,1024]{1,0:T(8,128)}, f32[1024,128]{1,0:T(8,128)}, bf16[1024,1024]{1,0:T(8,128)(2,1)}) custom-call(s32[4]{0:T(128)} %pad_add_fusion.meta_ref.meta, bf16[1024,1024]{1,0:T(8,128)(2,1)} %bitcast.97, bf16[1024,1024]{1,0:T(8,128)(2,1)} %bitcast.88, f32[1,1024]{1,0:T(1,128)} %bitcast.139, f32[1,1024]{1,0:T(1,128)} %bitcast.131, ...), custom_call_target="tpu_custom_call" | custom-call | flops 10000000000 | bytes 1000000 | tf_op jit(solution)/shard_map/out/pallas_call | solution.py:265
  152.9 22.0 %up.1 = (bf16[1024,4096]{1,0:T(8,128)(2,1)}, bf16[1024,4096]{1,0:T(8,128)(2,1)}) custom-call(s32[4]{0:T(128)} %pad_add_fusion.meta_ref.meta, bf16[1024,1024]{1,0:T(8,128)(2,1)} %get-tuple-element.175.refs_0_.refs_1_.refs_2_.refs_3_, f32[1,4096]{1,0:T(1,128)} %bitcast.130, bf16[4,128,5120]{2,1,0:T(8,128)(2,1)} %pad_maximum_fusion.refs_5_.refs_2_.refs_7_, ...), custom_call_target="tpu_custom_call" | custom-call | flops 23000000512 | bytes 1000000 | tf_op jit(solution)/shard_map/up/pallas_call | solution.py:265
  178.5 20.3 %down.1 = (bf16[1024,1024]{1,0:T(8,128)(2,1)}, f32[1024,1024]{1,0:T(8,128)}, bf16[1024,1024]{1,0:T(8,128)(2,1)}, f32[8,1024]{1,0:T(8,128)}, f32[8,1024]{1,0:T(8,128)}, /*index=5*/f32[8,1024]{1,0:T(8,128)}) custom-call(s32[4]{0:T(128)} %pad_add_fusion.meta_ref.meta, bf16[1024,4096]{1,0:T(8,128)(2,1)} %get-tuple-element.179.refs_0_.refs_1_.refs_2_.refs_3_, ...), custom_call_target="tpu_custom_call" | custom-call | flops 20999999488 | bytes 1000000 | tf_op jit(solution)/shard_map/down/pallas_call | solution.py:265
  198.8 9.4 %gd_away.1 = bf16[4,512,1024]{2,1,0:T(8,128)(2,1)} custom-call(s32[4]{0:T(128)} %pad_add_fusion.meta_ref.meta, bf16[1024,4096]{1,0:T(8,128)(2,1)} %get-tuple-element.179.refs_0_.refs_1_.refs_2_.refs_3_, bf16[1024,4096]{1,0:T(8,128)(2,1)} %get-tuple-element.179.refs_0_.refs_1_.refs_2_.refs_3_, ...), custom_call_target="tpu_custom_call" | custom-call | flops 11000000512 | bytes 1000000 | tf_op jit(solution)/shard_map/gd_away/pallas_call | solution.py:662
  211.4 15.0 %hidden.1 = (bf16[1024,4096]{1,0:T(8,128)(2,1)}, f32[8,4096]{1,0:T(8,128)}) custom-call(bf16[1024,1024]{1,0:T(8,128)(2,1)} %get-tuple-element.188.refs_4_.second, bf16[4096,1024]{1,0:T(8,128)(2,1)} %all-gather.2.cloned.1.call-done.whole, bf16[1024,4096]{1,0:T(8,128)(2,1)} %get-tuple-element.189.deriv), custom_call_target="tpu_custom_call" | custom-call | flops 17999998976 | bytes 1000000 | tf_op jit(solution)/shard_map/hidden/pallas_call | solution.py:382
  228.6 10.5 %gd_keep.1 = (bf16[512,1024]{1,0:T(8,128)(2,1)}, bf16[512,1024]{1,0:T(8,128)(2,1)}, bf16[512,1024]{1,0:T(8,128)(2,1)}, bf16[512,512]{1,0:T(8,128)(2,1)}, bf16[512,512]{1,0:T(8,128)(2,1)}) custom-call(s32[4]{0:T(128)} %pad_add_fusion.meta_ref.meta, bf16[1024,4096]{1,0:T(8,128)(2,1)} %get-tuple-element.179.refs_0_.refs_1_.refs_2_.refs_3_, ...), custom_call_target="tpu_custom_call" | custom-call | flops 11000000512 | bytes 1000000 | tf_op jit(solution)/shard_map/gd_keep/pallas_call | solution.py:662
  242.7 9.6 %gu_away.1 = bf16[4,128,4096]{2,1,0:T(8,128)(2,1)} custom-call(s32[4]{0:T(128)} %pad_add_fusion.meta_ref.meta, bf16[1024,1024]{1,0:T(8,128)(2,1)} %get-tuple-element.175.refs_0_.refs_1_.refs_2_.refs_3_, bf16[1024,1024]{1,0:T(8,128)(2,1)} %get-tuple-element.175.refs_0_.refs_1_.refs_2_.refs_3_, ...), custom_call_target="tpu_custom_call" | custom-call | flops 11000000512 | bytes 1000000 | tf_op jit(solution)/shard_map/gu_away/pallas_call | solution.py:662
  265.2 21.4 %first.1 = (f32[1024,1024]{1,0:T(8,128)}, bf16[1024,1024]{1,0:T(8,128)(2,1)}, bf16[1024,1024]{1,0:T(8,128)(2,1)}, f32[8,1024]{1,0:T(8,128)}, f32[8,1024]{1,0:T(8,128)}, /*index=5*/f32[8,1024]{1,0:T(8,128)}) custom-call(s32[4]{0:T(128)} %pad_add_fusion.meta_ref.meta, bf16[1024,4096]{1,0:T(8,128)(2,1)} %get-tuple-element.207.refs_4_.refs_0_, ...), custom_call_target="tpu_custom_call" | custom-call | flops 23000000512 | bytes 1000000 | tf_op jit(solution)/shard_map/first/pallas_call | solution.py:265
  287.4 10.4 %gu_keep.1 = (bf16[128,4096]{1,0:T(8,128)(2,1)}, bf16[128,4096]{1,0:T(8,128)(2,1)}, bf16[128,4096]{1,0:T(8,128)(2,1)}, bf16[128,2048]{1,0:T(8,128)(2,1)}, bf16[128,2048]{1,0:T(8,128)(2,1)}) custom-call(s32[4]{0:T(128)} %pad_add_fusion.meta_ref.meta, bf16[1024,1024]{1,0:T(8,128)(2,1)} %get-tuple-element.175.refs_0_.refs_1_.refs_2_.refs_3_, ...), custom_call_target="tpu_custom_call" | custom-call | flops 11000000512 | bytes 1000000 | tf_op jit(solution)/shard_map/gu_keep/pallas_call | solution.py:662
  302.6 16.8 %attend_back.2 = (bf16[3,2,512,512]{3,2,1,0:T(8,128)(2,1)}, f32[3,2,8,512]{3,2,1,0:T(8,128)}) custom-call(s32[4]{0:T(128)} %pad_add_fusion.meta_ref.meta, bf16[2,512,3072]{2,1,0:T(8,128)(2,1)} %bitcast.146, bf16[2,512,3072]{2,1,0:T(8,128)(2,1)} %bitcast.147, bf16[2,512,3072]{2,1,0:T(8,128)(2,1)} %bitcast.148, bf16[2,512,1024]{2,1,0:T(8,128)(2,1)} %bitcast.152, ...), custom_call_target="tpu_custom_call" | custom-call | flops 20999999488 | bytes 1000000 | tf_op jit(solution)/shard_map/attend_back/pallas_call | solution.py:508
  323.2 16.7 %attend_back.3 = (bf16[3,2,512,512]{3,2,1,0:T(8,128)(2,1)}, f32[3,2,8,512]{3,2,1,0:T(8,128)}) custom-call(s32[4]{0:T(128)} %pad_add_fusion.meta_ref.meta, bf16[2,512,3072]{2,1,0:T(8,128)(2,1)} %bitcast.149, bf16[2,512,3072]{2,1,0:T(8,128)(2,1)} %bitcast.150, bf16[2,512,3072]{2,1,0:T(8,128)(2,1)} %bitcast.151, bf16[2,512,1024]{2,1,0:T(8,128)(2,1)} %bitcast.153, ...), custom_call_target="tpu_custom_call" | custom-call | flops 20999999488 | bytes 1000000 | tf_op jit(solution)/shard_map/attend_back/pallas_call | solution.py:508
  351.0 11.1 %gb_away.1 = bf16[4,144,4096]{2,1,0:T(8,128)(2,1)} custom-call(s32[4]{0:T(128)} %pad_add_fusion.meta_ref.meta, bf16[1024,1024]{1,0:T(8,128)(2,1)} %bitcast.89, bf16[1024,1024]{1,0:T(8,128)(2,1)} %bitcast.90, bf16[1024,1024]{1,0:T(8,128)(2,1)} %bitcast.91, bf16[1024,1024]{1,0:T(8,128)(2,1)} %bitcast.92, bf16[1024,1024]{1,0:T(8,128)(2,1)} %bitcast.98, ...), custom_call_target="tpu_custom_call" | custom-call | flops 14000000000 | bytes 1000000 | tf_op jit(solution)/shard_map/gb_away/pallas_call | solution.py:662
  365.9 13.2 %input.1 = bf16[1024,1024]{1,0:T(8,128)(2,1)} custom-call(s32[4]{0:T(128)} %pad_add_fusion.meta_ref.meta, bf16[3,1024,512]{2,1,0:T(8,128)(2,1)} %bitcast.108, bf16[3,1024,512]{2,1,0:T(8,128)(2,1)} %bitcast.111, f32[1024,1024]{1,0:T(8,128)} %get-tuple-element.256.refs_2_, bf16[4,144,3072]{2,1,0:T(8,128)(2,1)} %copy-done.10, ...), custom_call_target="tpu_custom_call" | custom-call | flops 14000000000 | bytes 1000000 | tf_op jit(solution)/shard_map/input/pallas_call | solution.py:265
  381.0 12.1 %gb_keep.1 = (bf16[144,4096]{1,0:T(8,128)(2,1)}, bf16[144,4096]{1,0:T(8,128)(2,1)}, bf16[144,4096]{1,0:T(8,128)(2,1)}, bf16[144,2048]{1,0:T(8,128)(2,1)}, bf16[144,2048]{1,0:T(8,128)(2,1)}) custom-call(s32[4]{0:T(128)} %pad_add_fusion.meta_ref.meta, bf16[1024,1024]{1,0:T(8,128)(2,1)} %bitcast.93, bf16[1024,1024]{1,0:T(8,128)(2,1)} %bitcast.94, ...), custom_call_target="tpu_custom_call" | custom-call | flops 3000000000 | bytes 1000000 | tf_op jit(solution)/shard_map/gb_keep/pallas_call | solution.py:662
  400.3 13.6 %collective-permute-done.35 = bf16[1,128,1024]{2,1,0:T(8,128)(2,1)S(1)} collective-permute-done((bf16[1,128,1024]{2,1,0:T(8,128)(2,1)S(1)}, bf16[1,128,1024]{2,1,0:T(8,128)(2,1)S(1)}, u32[]{:S(2)}, u32[]{:S(2)}) %collective-permute-start.35) | collective-permute-done | bytes 262176 | tf_op jit(solution)/shard_map/ppermute | solution.py:29
  430.8 8.6 %collective-permute-done.38 = bf16[1,128,1024]{2,1,0:T(8,128)(2,1)S(1)} collective-permute-done((bf16[1,128,1024]{2,1,0:T(8,128)(2,1)S(1)}, bf16[1,128,1024]{2,1,0:T(8,128)(2,1)S(1)}, u32[]{:S(2)}, u32[]{:S(2)}) %collective-permute-start.38) | collective-permute-done | bytes 262176 | tf_op jit(solution)/shard_map/ppermute | solution.py:29
  451.7 16.6 %collective-permute-done.41 = bf16[1,128,1024]{2,1,0:T(8,128)(2,1)S(1)} collective-permute-done((bf16[1,128,1024]{2,1,0:T(8,128)(2,1)S(1)}, bf16[1,128,1024]{2,1,0:T(8,128)(2,1)S(1)}, u32[]{:S(2)}, u32[]{:S(2)}) %collective-permute-start.41) | collective-permute-done | bytes 262176 | tf_op jit(solution)/shard_map/ppermute | solution.py:29
  469.7 11.2 %collective-permute-done.43 = bf16[144,1024]{1,0:T(8,128)(2,1)S(1)} collective-permute-done((bf16[144,1024]{1,0:T(8,128)(2,1)S(1)}, bf16[144,1024]{1,0:T(8,128)(2,1)S(1)}, u32[]{:S(2)}, u32[]{:S(2)}) %collective-permute-start.43) | collective-permute-done | bytes 294944 | tf_op jit(solution)/shard_map/ppermute | solution.py:29
  482.6 12.2 %collective-permute-done.44 = bf16[144,1024]{1,0:T(8,128)(2,1)S(1)} collective-permute-done((bf16[144,1024]{1,0:T(8,128)(2,1)S(1)}, bf16[144,1024]{1,0:T(8,128)(2,1)S(1)}, u32[]{:S(2)}, u32[]{:S(2)}) %collective-permute-start.44) | collective-permute-done | bytes 294944 | tf_op jit(solution)/shard_map/ppermute | solution.py:29
  495.2 12.2 %collective-permute-done.45 = bf16[144,2048]{1,0:T(8,128)(2,1)S(1)} collective-permute-done((bf16[144,2048]{1,0:T(8,128)(2,1)S(1)}, bf16[144,2048]{1,0:T(8,128)(2,1)S(1)}, u32[]{:S(2)}, u32[]{:S(2)}) %collective-permute-start.45) | collective-permute-done | bytes 589856 | tf_op jit(solution)/shard_map/ppermute | solution.py:29
  (305 shorter events, 155.9 us)
Async XLA Ops:
  7.2 54.7 %all-to-all-start = ((bf16[4,2,128,1024]{3,2,1,0:T(8,128)(2,1)}), bf16[4,2,128,1024]{3,2,1,0:T(8,128)(2,1)S(1)}, u32[]{:S(2)}, u32[]{:S(2)}) async-start(bf16[4,2,128,1024]{3,2,1,0:T(8,128)(2,1)} %bitcast.123), calls=%async_computation | async-start | bytes 4194304 | tf_op jit(solution)/shard_map/all_to_all | solution.py:125
  13.7 163.4 %all-gather.2.cloned.1.call-start = ((), (), s32[]{:S(2)}) async-start(), calls=%async_computation.1 | async-start | bytes 9437184 | tf_op jit(solution)/shard_map/all_gather | solution.py:733
  15.6 50.7 %collective-permute-start.2 = (bf16[128,5120]{1,0:T(8,128)(2,1)}, bf16[128,5120]{1,0:T(8,128)(2,1)S(1)}, u32[]{:S(2)}, u32[]{:S(2)}) collective-permute-start(bf16[128,5120]{1,0:T(8,128)(2,1)} %constant_dynamic-update-slice_fusion), channel_id=1, source_target_pairs={{0,8},{4,12},{8,0},{12,4},{16,24},{20,28},{24,16},{28,20},{1,9},{5... | collective-permute-start | bytes 3932168 | tf_op jit(solution)/shard_map/ppermute | solution.py:29
  17.1 49.2 %collective-permute-start.3 = (bf16[128,5120]{1,0:T(8,128)(2,1)}, bf16[128,5120]{1,0:T(8,128)(2,1)}, u32[]{:S(2)}, u32[]{:S(2)}) collective-permute-start(bf16[128,5120]{1,0:T(8,128)(2,1)} %constant_dynamic-update-slice_fusion), channel_id=1, source_target_pairs={{0,16},{4,20},{8,24},{12,28},{16,0},{20,4},{24,8},{28,12},{1,17},{... | collective-permute-start | bytes 3932168 | tf_op jit(solution)/shard_map/ppermute | solution.py:29
  22.8 42.3 %collective-permute-start = (bf16[144,3072]{1,0:T(8,128)(2,1)}, bf16[144,3072]{1,0:T(8,128)(2,1)}, u32[]{:S(2)}, u32[]{:S(2)}) collective-permute-start(bf16[144,3072]{1,0:T(8,128)(2,1)} %get-tuple-element.315), channel_id=1, source_target_pairs={{0,8},{4,12},{8,0},{12,4},{16,24},{20,28},{24,16},{28,20},{1,9},{5... | collective-permute-start | bytes 2654216 | tf_op jit(solution)/shard_map/ppermute | solution.py:29
  23.3 42.9 %collective-permute-start.1 = (bf16[144,3072]{1,0:T(8,128)(2,1)}, bf16[144,3072]{1,0:T(8,128)(2,1)}, u32[]{:S(2)}, u32[]{:S(2)}) collective-permute-start(bf16[144,3072]{1,0:T(8,128)(2,1)} %get-tuple-element.315), channel_id=1, source_target_pairs={{0,16},{4,20},{8,24},{12,28},{16,0},{20,4},{24,8},{28,12},{1,17},{... | collective-permute-start | bytes 2654216 | tf_op jit(solution)/shard_map/ppermute | solution.py:29
  83.7 22.6 %collective-permute-start.8 = (bf16[64,5120]{1,0:T(8,128)(2,1)}, bf16[64,5120]{1,0:T(8,128)(2,1)}, u32[]{:S(2)}, u32[]{:S(2)}) collective-permute-start(bf16[64,5120]{1,0:T(8,128)(2,1)} %slice.175), channel_id=1, source_target_pairs={{0,16},{4,20},{8,24},{12,28},{16,0},{20,4},{24,8},{28,12},{1,17},{... | collective-permute-start | bytes 1966088 | tf_op jit(solution)/shard_map/ppermute | solution.py:29
  106.3 255.8 %all-reduce.10.cloned.1.call-start = ((), (), s32[]{:S(2)}) async-start(), calls=%async_computation.2 | async-start | bytes 2097152 | tf_op jit(solution)/shard_map/psum | solution.py:789
  112.8 27.7 %collective-permute-start.11 = (bf16[4,128,5120]{2,1,0:T(8,128)(2,1)}, bf16[4,128,5120]{2,1,0:T(8,128)(2,1)}, u32[]{:S(2)}, u32[]{:S(2)}) collective-permute-start(bf16[4,128,5120]{2,1,0:T(8,128)(2,1)} %pad_maximum_fusion.refs_5_.refs_2_.refs_7_), channel_id=1, source_target_pairs={{0,4},{4,0},{8,12},{12,8},{16,20},{20,16},{24,28},{28,24},{1,5},{5... | collective-permute-start | bytes 15728648 | tf_op jit(solution)/shard_map/ppermute | solution.py:29
  114.1 26.5 %collective-permute-start.12 = (bf16[2,128,1024]{2,1,0:T(8,128)(2,1)S(1)}, bf16[2,128,1024]{2,1,0:T(8,128)(2,1)S(1)}, u32[]{:S(2)}, u32[]{:S(2)}) collective-permute-start(bf16[2,128,1024]{2,1,0:T(8,128)(2,1)S(1)} %copy-done.35), channel_id=1, source_target_pairs={{0,2},{1,3},{2,0},{3,1},{4,6},{5,7},{6,4},{7,5},{8,10},{9,11},{10,... | collective-permute-start | bytes 1572872 | tf_op jit(solution)/shard_map/ppermute | solution.py:29
  150.5 26.6 %collective-permute-start.13 = (bf16[2,128,1024]{2,1,0:T(8,128)(2,1)S(1)}, bf16[2,128,1024]{2,1,0:T(8,128)(2,1)S(1)}, u32[]{:S(2)}, u32[]{:S(2)}) collective-permute-start(bf16[2,128,1024]{2,1,0:T(8,128)(2,1)S(1)} %copy-done.34), channel_id=1, source_target_pairs={{0,3},{1,2},{2,1},{3,0},{4,7},{5,6},{6,5},{7,4},{8,11},{9,10},{10,... | collective-permute-start | bytes 1572872 | tf_op jit(solution)/shard_map/ppermute | solution.py:29
  255.0 31.7 %collective-permute-start.20 = (bf16[4,128,4096]{2,1,0:T(8,128)(2,1)}, bf16[4,128,4096]{2,1,0:T(8,128)(2,1)}, u32[]{:S(2)}, u32[]{:S(2)}) collective-permute-start(bf16[4,128,4096]{2,1,0:T(8,128)(2,1)} %gu_away.1), channel_id=1, source_target_pairs={{0,4},{4,0},{8,12},{12,8},{16,20},{20,16},{24,28},{28,24},{1,5},{5... | collective-permute-start | bytes 12582920 | tf_op jit(solution)/shard_map/ppermute | solution.py:29
  257.6 29.1 %collective-permute-start.21 = (bf16[512,1024]{1,0:T(8,128)(2,1)}, bf16[512,1024]{1,0:T(8,128)(2,1)}, u32[]{:S(2)}, u32[]{:S(2)}) collective-permute-start(bf16[512,1024]{1,0:T(8,128)(2,1)} %add_convert_fusion.8), channel_id=1, source_target_pairs={{0,8},{4,12},{8,0},{12,4},{16,24},{20,28},{24,16},{28,20},{1,9},{5... | collective-permute-start | bytes 3145736 | tf_op jit(solution)/shard_map/ppermute | solution.py:29
  260.6 26.1 %collective-permute-start.22 = (bf16[512,1024]{1,0:T(8,128)(2,1)}, bf16[512,1024]{1,0:T(8,128)(2,1)S(1)}, u32[]{:S(2)}, u32[]{:S(2)}) collective-permute-start(bf16[512,1024]{1,0:T(8,128)(2,1)} %add_convert_fusion.7), channel_id=1, source_target_pairs={{0,16},{4,20},{8,24},{12,28},{16,0},{20,4},{24,8},{28,12},{1,17},{... | collective-permute-start | bytes 3145736 | tf_op jit(solution)/shard_map/ppermute | solution.py:29
  263.0 23.6 %collective-permute-start.23 = (bf16[2,128,1024]{2,1,0:T(8,128)(2,1)}, bf16[2,128,1024]{2,1,0:T(8,128)(2,1)S(1)}, u32[]{:S(2)}, u32[]{:S(2)}) collective-permute-start(bf16[2,128,1024]{2,1,0:T(8,128)(2,1)} %constant_dynamic-slice_fusion.8), channel_id=1, source_target_pairs={{0,3},{1,2},{2,1},{3,0},{4,7},{5,6},{6,5},{7,4},{8,11},{9,10},{10,... | collective-permute-start | bytes 1572872 | tf_op jit(solution)/shard_map/ppermute | solution.py:29
  297.9 21.6 %collective-permute-start.24 = (bf16[128,2048]{1,0:T(8,128)(2,1)}, bf16[128,2048]{1,0:T(8,128)(2,1)S(1)}, u32[]{:S(2)}, u32[]{:S(2)}) collective-permute-start(bf16[128,2048]{1,0:T(8,128)(2,1)} %get-tuple-element.225), channel_id=1, source_target_pairs={{0,16},{4,20},{8,24},{12,28},{16,0},{20,4},{24,8},{28,12},{1,17},{... | collective-permute-start | bytes 1572872 | tf_op jit(solution)/shard_map/ppermute | solution.py:29
  298.3 21.1 %collective-permute-start.25 = (bf16[128,2048]{1,0:T(8,128)(2,1)}, bf16[128,2048]{1,0:T(8,128)(2,1)S(1)}, u32[]{:S(2)}, u32[]{:S(2)}) collective-permute-start(bf16[128,2048]{1,0:T(8,128)(2,1)} %get-tuple-element.226), channel_id=1, source_target_pairs={{0,8},{4,12},{8,0},{12,4},{16,24},{20,28},{24,16},{28,20},{1,9},{5... | collective-permute-start | bytes 1572872 | tf_op jit(solution)/shard_map/ppermute | solution.py:29
  320.4 24.3 %collective-permute-start.26 = (bf16[128,4096]{1,0:T(8,128)(2,1)S(1)}, bf16[128,4096]{1,0:T(8,128)(2,1)}, u32[]{:S(2)}, u32[]{:S(2)}) collective-permute-start(bf16[128,4096]{1,0:T(8,128)(2,1)S(1)} %add_convert_fusion.6), channel_id=1, source_target_pairs={{0,8},{4,12},{8,0},{12,4},{16,24},{20,28},{24,16},{28,20},{1,9},{5... | collective-permute-start | bytes 3145736 | tf_op jit(solution)/shard_map/ppermute | solution.py:29
  321.6 24.3 %collective-permute-start.27 = (bf16[128,4096]{1,0:T(8,128)(2,1)S(1)}, bf16[128,4096]{1,0:T(8,128)(2,1)}, u32[]{:S(2)}, u32[]{:S(2)}) collective-permute-start(bf16[128,4096]{1,0:T(8,128)(2,1)S(1)} %add_convert_fusion.5), channel_id=1, source_target_pairs={{0,16},{4,20},{8,24},{12,28},{16,0},{20,4},{24,8},{28,12},{1,17},{... | collective-permute-start | bytes 3145736 | tf_op jit(solution)/shard_map/ppermute | solution.py:29
  394.2 21.9 %collective-permute-start.32 = (bf16[144,2048]{1,0:T(8,128)(2,1)}, bf16[144,2048]{1,0:T(8,128)(2,1)S(1)}, u32[]{:S(2)}, u32[]{:S(2)}) collective-permute-start(bf16[144,2048]{1,0:T(8,128)(2,1)} %get-tuple-element.272), channel_id=1, source_target_pairs={{0,16},{4,20},{8,24},{12,28},{16,0},{20,4},{24,8},{28,12},{1,17},{... | collective-permute-start | bytes 1769480 | tf_op jit(solution)/shard_map/ppermute | solution.py:29
  395.7 20.4 %collective-permute-start.33 = (bf16[144,2048]{1,0:T(8,128)(2,1)}, bf16[144,2048]{1,0:T(8,128)(2,1)S(1)}, u32[]{:S(2)}, u32[]{:S(2)}) collective-permute-start(bf16[144,2048]{1,0:T(8,128)(2,1)} %get-tuple-element.273), channel_id=1, source_target_pairs={{0,8},{4,12},{8,0},{12,4},{16,24},{20,28},{24,16},{28,20},{1,9},{5... | collective-permute-start | bytes 1769480 | tf_op jit(solution)/shard_map/ppermute | solution.py:29
  418.0 27.1 %collective-permute-start.36 = (bf16[144,4096]{1,0:T(8,128)(2,1)}, bf16[144,4096]{1,0:T(8,128)(2,1)}, u32[]{:S(2)}, u32[]{:S(2)}) collective-permute-start(bf16[144,4096]{1,0:T(8,128)(2,1)} %add_convert_fusion.2), channel_id=1, source_target_pairs={{0,8},{4,12},{8,0},{12,4},{16,24},{20,28},{24,16},{28,20},{1,9},{5... | collective-permute-start | bytes 3538952 | tf_op jit(solution)/shard_map/ppermute | solution.py:29
  419.8 26.8 %collective-permute-start.37 = (bf16[144,4096]{1,0:T(8,128)(2,1)}, bf16[144,4096]{1,0:T(8,128)(2,1)}, u32[]{:S(2)}, u32[]{:S(2)}) collective-permute-start(bf16[144,4096]{1,0:T(8,128)(2,1)} %add_convert_fusion.1), channel_id=1, source_target_pairs={{0,16},{4,20},{8,24},{12,28},{16,0},{20,4},{24,8},{28,12},{1,17},{... | collective-permute-start | bytes 3538952 | tf_op jit(solution)/shard_map/ppermute | solution.py:29
  420.4 23.4 %collective-permute-start.40 = (bf16[128,2048]{1,0:T(8,128)(2,1)S(1)}, bf16[128,2048]{1,0:T(8,128)(2,1)}, u32[]{:S(2)}, u32[]{:S(2)}) collective-permute-start(bf16[128,2048]{1,0:T(8,128)(2,1)S(1)} %pad_maximum_fusion.4), channel_id=1, source_target_pairs={{0,1},{1,0},{2,3},{3,2},{4,5},{5,4},{6,7},{7,6},{8,9},{9,8},{10,11... | collective-permute-start | bytes 1572872 | tf_op jit(solution)/shard_map/ppermute | solution.py:29
  (75 other events, 844.1 us)
Sparse Core Ops, SparseCore 0:
  106.5 53.2 all-gather.1
  302.7 50.0 all-reduce.9
